TPU v7x, 256 devices: a whole 4x4x8 slice. The times are simulated.
256 devices in a mesh: eig: 16 (over y_lo, x, core), space: 16 (over z, y_hi).
Axes of the slice: x: 4, y: 4 (y_hi: 2, y_lo: 2; y = y_hi * 2 + y_lo), z: 8, core: 2. Of those that a mesh axis runs over, the one named last changes fastest.
Arguments:
- eigenvectors: float32 [2, 256, 4, 3, 64, 128], P(None, 'eig', None, None, 'space'), as said below
- gauge_links: float32 [2, 3, 3, 64, 128], P(None, None, None, 'space'), may hold values from -2.5 to 2.5
- separations: int32 [4], replicated, may hold values from 0 to 3, each once
Outputs:
- meson_fields: float32 [2, 4, 2, 2, 256, 256], P(None, None, None, None, 'space', 'eig')
Inputs may be any that keep to these rules, and one draw needn't show every extreme that they name: `separations`: each value appears once. `eigenvectors`: entries of size about (196608) ** -0.25.
All inputs are finite; a program needn't handle non-finite values.
Results may differ from a plain program's by a relative error of at most 0.00016.
Values sent between devices are 32-bit elements; how exact they have to be, the bound alone decides.
No kernel may reach another device: no remote copies, remote signals or barrier semaphores. Data moves between devices by JAX's collectives and lax.ppermute only.
A program may use at most 192 MiB of HBM per device.

v0:
```python
import jax
import jax.numpy as jnp
from jax import lax
from jax.sharding import PartitionSpec as P

NZD = 4
NG = 2


highest = lax.Precision.HIGHEST


def passed_along(value, axis, by):
    devices = lax.axis_size(axis)
    return lax.ppermute(value, axis, [(i, (i + by) % devices) for i in range(devices)])


def colour_step(link_real, link_imag, vector_field, adjoint):
    real_rows = []
    imag_rows = []
    for colour_out in range(3):
        total_real = jnp.zeros_like(vector_field[0, :, :, 0])
        total_imag = jnp.zeros_like(vector_field[0, :, :, 0])
        for colour_in in range(3):
            if adjoint:
                entry_real = link_real[colour_in, colour_out]
                entry_imag = -link_imag[colour_in, colour_out]
            else:
                entry_real = link_real[colour_out, colour_in]
                entry_imag = link_imag[colour_out, colour_in]
            source_real = vector_field[0, :, :, colour_in]
            source_imag = vector_field[1, :, :, colour_in]
            total_real = total_real + entry_real * source_real - entry_imag * source_imag
            total_imag = total_imag + entry_real * source_imag + entry_imag * source_real
        real_rows.append(total_real)
        imag_rows.append(total_imag)
    return jnp.stack([jnp.stack(real_rows, axis=2), jnp.stack(imag_rows, axis=2)])


def spin_mix(eigen_block):
    swapped = jnp.concatenate([eigen_block[:, :, 2:], eigen_block[:, :, :2]], axis=2)
    chiral = jnp.concatenate([eigen_block[:, :, :2], -eigen_block[:, :, 2:]], axis=2)
    return jnp.stack([swapped, chiral])


def pair_terms(mixed_block, transported):
    products = jnp.einsum("gaisczx,kdjsczx->kgadji", mixed_block, transported, precision=highest)
    real_part = products[:, :, 0, 0] + products[:, :, 1, 1]
    imag_part = products[:, :, 0, 1] - products[:, :, 1, 0]
    return jnp.stack([real_part, imag_part], axis=2)


def reflect(pair_values):
    flipped = jnp.swapaxes(pair_values[::-1], 4, 5)
    return flipped * jnp.array([1.0, -1.0], jnp.float32)[:, None, None]


def transport(vectors, gauge_links):
    link_real = gauge_links[0]
    link_imag = gauge_links[1]
    plus_list = []
    minus_list = []
    forward = vectors
    backward = vectors
    for length in range(NZD):
        above_plane = passed_along(forward[:, :, :, :, :1], "space", -1)
        forward = colour_step(
            link_real,
            link_imag,
            jnp.concatenate([forward[:, :, :, :, 1:], above_plane], axis=4),
            False,
        )
        plus_list.append(forward)
        pulled = colour_step(link_real, link_imag, backward, True)
        below_plane = passed_along(pulled[:, :, :, :, -1:], "space", 1)
        backward = jnp.concatenate([below_plane, pulled[:, :, :, :, :-1]], axis=4)
        minus_list.append(backward)
    return (jnp.stack(plus_list), jnp.stack(minus_list))


def local(eigenvectors, gauge_links, separations):
    block_size = eigenvectors.shape[1]
    plus_stack, minus_stack = transport(eigenvectors, gauge_links)

    def both_signs(eigen_block):
        mixed_block = spin_mix(eigen_block)
        return jnp.stack(
            [pair_terms(mixed_block, plus_stack), pair_terms(mixed_block, minus_stack)]
        )

    eig_count = lax.axis_size("eig")
    self_index = lax.axis_index("eig")
    total_rows = eig_count * block_size
    column = jnp.zeros((2, NZD, NG, 2, block_size, total_rows), jnp.float32)
    reflected = jnp.zeros((2, NZD, NG, 2, total_rows, block_size), jnp.float32)
    arrived = lax.all_gather(eigenvectors, "eig", axis=1, tiled=True)
    row_count = arrived.shape[1]

    def compute(current):
        pair_values = both_signs(arrived)
        row_block = jnp.arange(row_count) // block_size
        keep_rows = (row_block <= self_index).astype(jnp.float32)
        below_rows = (row_block < self_index).astype(jnp.float32)
        column_now = pair_values * keep_rows
        reflected_now = reflect(pair_values * below_rows)
        return (column_now, reflected_now)

    def unchanged(current):
        return current

    column, reflected = lax.cond(
        jnp.int32(0) < (self_index + 1) * block_size, compute, unchanged, (column, reflected)
    )
    packed = reflected.reshape(2, NZD, NG, 2, eig_count, block_size * block_size)
    received = lax.all_to_all(packed, "eig", split_axis=4, concat_axis=4, tiled=True)
    received = received.reshape(2, NZD, NG, 2, eig_count, block_size, block_size)
    column = column + jnp.swapaxes(received, 4, 5).reshape(2, NZD, NG, 2, block_size, total_rows)
    summed = lax.psum_scatter(column, "space", scatter_dimension=5, tiled=True)
    selector = (separations[:, None] == jnp.arange(NZD)[None, :]).astype(jnp.float32)
    return jnp.einsum("qk,skgcji->sqgcij", selector, summed, precision=highest)


def solution(mesh):
    return jax.shard_map(
        local,
        mesh=mesh,
        in_specs=(
            P(None, "eig", None, None, "space", None),
            P(None, None, None, "space", None),
            P(),
        ),
        out_specs=P(None, None, None, None, "space", "eig"),
        check_vma=False,
    )
```

profile of v0, /device:TPU:24, one launch (start us, length us, event | category | flops | bytes accessed | tf_op | source)
XLA Modules:
  0.0 466.3 jit_solution(4164402272456197035)
XLA Ops:
  6.5 2.3 copy.56
  8.9 0.8 slice_bitcast_fusion.27
  9.7 1.3 multiply_subtract_fusion.11
  11.0 1.3 multiply_subtract_fusion.10
  12.3 1.3 multiply_subtract_fusion.9
  13.7 2.7 collective-permute-start.4
  16.4 1.0 collective-permute-start
  17.5 10.0 %collective-permute-done.4 = f32[2,16,4,3,1,128]{5,1,4,2,3,0:T(8,128)S(1)} collective-permute-done((f32[2,16,4,3,1,128]{5,1,4,2,3,0:T(8,128)S(1)}, f32[2,16,4,3,1,128]{5,1,4,2,3,0:T(8,128)S(1)}, u32[]{:S(2)}, u32[]{:S(2)}) %collective-permute-start.4) | collective-permute-done | bytes 196640 | tf_op jit(solution)/shard_map/ppermute | solution.py:15
  27.6 0.1 multiply_subtract_fusion.8
  27.7 0.1 multiply_subtract_fusion.7
  27.8 0.1 multiply_subtract_fusion.6
  28.0 1.9 collective-permute-start.5
  29.9 0.1 multiply_add_fusion.23
  30.1 0.2 multiply_add_fusion.22
  30.4 2.9 collective-permute-start.1
  33.4 0.1 fusion.112
  33.5 10.7 %collective-permute-done.5 = f32[2,16,4,3,1,128]{5,1,4,2,3,0:T(8,128)S(1)} collective-permute-done((f32[2,16,4,3,1,128]{5,1,4,2,3,0:T(8,128)S(1)}, f32[2,16,4,3,1,128]{5,1,4,2,3,0:T(8,128)S(1)}, u32[]{:S(2)}, u32[]{:S(2)}) %collective-permute-start.5) | collective-permute-done | bytes 196640 | tf_op jit(solution)/shard_map/ppermute | solution.py:15
  44.2 0.1 fusion.31
  44.3 0.1 multiply_subtract_fusion.5
  44.4 0.1 multiply_subtract_fusion.4
  44.5 0.1 multiply_subtract_fusion.3
  44.7 3.3 collective-permute-start.6
  48.0 0.1 multiply_add_fusion.20
  48.1 0.2 multiply_add_fusion.19
  48.5 0.4 collective-permute-start.2
  49.1 12.3 %collective-permute-done.6 = f32[2,16,4,3,1,128]{5,1,4,2,3,0:T(8,128)S(1)} collective-permute-done((f32[2,16,4,3,1,128]{5,1,4,2,3,0:T(8,128)S(1)}, f32[2,16,4,3,1,128]{5,1,4,2,3,0:T(8,128)S(1)}, u32[]{:S(2)}, u32[]{:S(2)}) %collective-permute-start.6) | collective-permute-done | bytes 196640 | tf_op jit(solution)/shard_map/ppermute | solution.py:15
  61.5 0.1 multiply_subtract_fusion.2
  61.6 0.1 multiply_subtract_fusion.1
  61.8 0.1 multiply_subtract_fusion
  62.0 2.2 collective-permute-start.7
  64.1 0.1 multiply_add_fusion.17
  64.3 0.2 multiply_add_fusion.16
  64.7 1.7 collective-permute-start.3
  66.5 10.3 %collective-permute-done.3 = f32[2,16,4,3,1,128]{5,1,4,2,3,0:T(8,128)S(1)} collective-permute-done((f32[2,16,4,3,1,128]{5,1,4,2,3,0:T(8,128)S(1)}, f32[2,16,4,3,1,128]{5,1,4,2,3,0:T(8,128)S(1)}, u32[]{:S(2)}, u32[]{:S(2)}) %collective-permute-start.3) | collective-permute-done | bytes 196640 | tf_op jit(solution)/shard_map/ppermute | solution.py:15
  76.8 0.1 multiply_subtract_fusion.14
  77.0 0.1 multiply_subtract_fusion.12
  77.1 0.2 multiply_subtract_fusion.13
  77.5 0.4 pad_maximum_fusion.4
  77.9 2.0 pad_maximum_fusion.3
  79.9 32.8 %all-gather.2.cloned.1.call-done = f32[2,256,4,3,4,128]{5,1,4,2,3,0:T(8,128)} async-done(((f32[2,16,4,3,4,128]{5,1,4,2,3,0:T(8,128)}), f32[2,256,4,3,4,128]{5,1,4,2,3,0:T(8,128)}) %all-gather.2.cloned.1.call-update) | async-done | bytes 12582928 | tf_op jit(solution)/shard_map/all_gather | solution.py:96
  112.7 94.9 %conditional.1 = (f32[2,4,2,2,256,16]{4,5,1,2,3,0:T(8,128)}, f32[2,4,2,2,16,256]{5,4,3,2,1,0:T(8,128)}) conditional(s32[]{:T(128)} %convert_element_type.18, () %tuple.13, (f32[2,256,4,3,4,128]{5,1,4,2,3,0:T(8,128)}, f32[4,2,16,4,3,4,128]{6,2,5,3,4,1,0:T(8,128)}, f32[4,2,16,4,3,4,128]{6,2,5,3,4,1,0:T(8,128)S(1)}, s32[]{:T(128)}) %tuple.17), branch_computations={%region_0.0_spmd, %region_1.2_spmd.clone} | conditional | flops 19348590592 | bytes 152047728 | solution.py:111
  112.7 12.7 %fusion.110 = (f32[2,256,2,3,4,128]{5,1,4,2,3,0:T(8,128)}, f32[2,256,2,3,4,128]{5,1,4,2,3,0:T(8,128)}, f32[2,256,2,3,4,128]{5,1,4,2,3,0:T(8,128)}) fusion(f32[2,256,4,3,4,128]{5,1,4,2,3,0:T(8,128)} %get-tuple-element.26), kind=kLoop, calls=%fused_computation.285 | loop fusion | flops 1572864 | bytes 31457280 | tf_op jit(solution)/shard_map/cond/branch_1_fun/slice | solution.py:41
  125.4 18.5 %maximum_bitcast_fusion = (f32[1,2,256,4,3,4,128]{6,2,5,3,4,1,0:T(8,128)}, f32[1,2,256,4,3,4,128]{6,2,5,3,4,1,0:T(8,128)}) fusion(f32[2,256,2,3,4,128]{5,1,4,2,3,0:T(8,128)} %get-tuple-element.65, f32[2,256,2,3,4,128]{5,1,4,2,3,0:T(8,128)} %get-tuple-element.63, f32[2,256,2,3,4,128]{5,1,4,2,3,0:T(8,128)} %get-tuple-element.64), kind=kLoop, calls=%fused_computation.6 | loop fusion | flops 6291456 | bytes 44040192 | tf_op jit(solution)/shard_map/cond/branch_1_fun/stack | solution.py:43
  143.9 30.6 %fusion.7 = f32[4,2,2,2,16,256]{5,4,0,1,3,2:T(8,128)S(1)} fusion(f32[1,2,256,4,3,4,128]{6,2,5,3,4,1,0:T(8,128)} %get-tuple-element.67, f32[1,2,256,4,3,4,128]{6,2,5,3,4,1,0:T(8,128)} %get-tuple-element.66, f32[4,2,16,4,3,4,128]{6,2,5,3,4,1,0:T(8,128)S(1)} %get-tuple-element.28), kind=kOutput, calls=%fused_computation.10 | convolution fusion | flops 9669967872 | bytes 28835840 | tf_op jit(solution)/shard_map/cond/branch_1_fun/gaisczx,kdjsczx->kgadji/dot_general | solution.py:47
  174.6 31.0 %fusion.12 = f32[4,2,2,2,16,256]{5,4,3,0,2,1:T(8,128)S(1)} fusion(f32[4,2,16,4,3,4,128]{6,2,5,3,4,1,0:T(8,128)S(1)} %copy-done.1, f32[1,2,256,4,3,4,128]{6,2,5,3,4,1,0:T(8,128)} %get-tuple-element.67, f32[1,2,256,4,3,4,128]{6,2,5,3,4,1,0:T(8,128)} %get-tuple-element.66), kind=kOutput, calls=%fused_computation.11 | convolution fusion | flops 9669967872 | bytes 28835840 | tf_op jit(solution)/shard_map/cond/branch_1_fun/gaisczx,kdjsczx->kgadji/dot_general | solution.py:47
  205.7 0.1 fusion.18
  205.8 0.9 copy.83
  206.7 0.9 multiply_bitcast_fusion
  207.6 3.5 copy.65
  211.1 3.5 reshape.3702
  214.6 0.4 copy.66
  215.0 14.9 %all_to_all.5 = f32[2,4,2,2,16,256]{5,3,2,1,0,4:T(2,128)S(1)} all-to-all(f32[2,4,2,2,16,256]{5,3,2,1,0,4:T(2,128)S(1)} %copy.66), channel_id=1, replica_groups=mesh['eig'=16,'space'=16] {'eig'}, dimensions={4} | all-to-all | bytes 1048576 | tf_op jit(solution)/shard_map/all_to_all | solution.py:115
  229.9 0.3 copy.67
  230.3 2.6 reshape.3703
  232.9 5.9 %copy.68 = f32[2,4,2,2,16,16,16]{6,5,4,3,2,1,0:T(8,128)} copy(f32[2,4,2,2,16,16,16]{6,4,5,3,2,1,0:T(8,128)} %bitcast.591) | data formatting | bytes 1048576 | tf_op jit(solution)/shard_map/transpose | solution.py:117
  238.8 3.5 reshape.3704
  242.4 1.1 add.1891
  243.5 4.5 copy.80
  248.0 7.7 %reshape.3711 = f32[256,512]{1,0:T(8,128)} reshape(f32[256,2,4,2,2,16]{5,4,3,2,1,0:T(2,128)} %bitcast.590) | data formatting | bytes 1048576
  255.6 200.6 %reduce-scatter.4.cloned.1.call-done = f32[16,512]{1,0:T(8,128)} async-done(((f32[256,512]{1,0:T(8,128)}), f32[16,512]{1,0:T(8,128)}) %reduce-scatter.4.cloned.1.call-update) | async-done | bytes 32784
  456.3 1.1 reshape.3712
  457.4 0.3 copy.70
  457.7 0.4 convolution_bitcast_fusion
  458.1 0.8 copy.71
  (61 shorter events, 1.8 us)
Async XLA Ops:
  6.5 106.2 %all-gather.2.cloned.1.call-start = ((), (), s32[]{:S(2)}) async-start(), calls=%async_computation.2 | async-start | bytes 13369344 | tf_op jit(solution)/shard_map/all_gather | solution.py:96
  8.8 7.6 %copy-start = (f32[2,16,4,3,4,128]{5,1,4,2,3,0:T(8,128)S(1)}, f32[2,16,4,3,4,128]{5,1,4,2,3,0:T(8,128)}, u32[]{:S(2)}) copy-start(f32[2,16,4,3,4,128]{5,1,4,2,3,0:T(8,128)} %copy.56) | copy-start | bytes 2359300
  8.8 447.4 %reduce-scatter.4.cloned.1.call-start = ((), (), s32[]{:S(2)}) async-start(), calls=%async_computation.3 | async-start | bytes 557056
  13.7 13.8 %collective-permute-start.4 = (f32[2,16,4,3,1,128]{5,1,4,2,3,0:T(8,128)S(1)}, f32[2,16,4,3,1,128]{5,1,4,2,3,0:T(8,128)S(1)}, u32[]{:S(2)}, u32[]{:S(2)}) collective-permute-start(f32[2,16,4,3,1,128]{5,1,4,2,3,0:T(8,128)S(1)} %pad_maximum_fusion.15), channel_id=1, source_target_pairs={{0,1},{1,2},{2,3},{3,4},{4,5},{5,6},{6,7},{7,8},{8,9},{9,10},{10,1... | collective-permute-start | bytes 589832 | tf_op jit(solution)/shard_map/ppermute | solution.py:15
  16.4 13.5 %collective-permute-start = (f32[2,16,4,3,1,128]{5,1,4,2,3,0:T(8,128)S(1)}, f32[2,16,4,3,1,128]{5,1,4,2,3,0:T(8,128)S(1)}, u32[]{:S(2)}, u32[]{:S(2)}) collective-permute-start(f32[2,16,4,3,1,128]{5,1,4,2,3,0:T(8,128)S(1)} %slice.292), channel_id=1, source_target_pairs={{0,15},{1,0},{2,1},{3,2},{4,3},{5,4},{6,5},{7,6},{8,7},{9,8},{10,9... | collective-permute-start | bytes 589832 | tf_op jit(solution)/shard_map/ppermute | solution.py:15
  28.0 16.2 %collective-permute-start.5 = (f32[2,16,4,3,1,128]{5,1,4,2,3,0:T(8,128)S(1)}, f32[2,16,4,3,1,128]{5,1,4,2,3,0:T(8,128)S(1)}, u32[]{:S(2)}, u32[]{:S(2)}) collective-permute-start(f32[2,16,4,3,1,128]{5,1,4,2,3,0:T(8,128)S(1)} %pad_maximum_fusion.14), channel_id=1, source_target_pairs={{0,1},{1,2},{2,3},{3,4},{4,5},{5,6},{6,7},{7,8},{8,9},{9,10},{10,1... | collective-permute-start | bytes 589832 | tf_op jit(solution)/shard_map/ppermute | solution.py:15
  30.4 17.6 %collective-permute-start.1 = (f32[2,16,4,3,1,128]{5,1,4,2,3,0:T(8,128)S(1)}, f32[2,16,4,3,1,128]{5,1,4,2,3,0:T(8,128)S(1)}, u32[]{:S(2)}, u32[]{:S(2)}) collective-permute-start(f32[2,16,4,3,1,128]{5,1,4,2,3,0:T(8,128)S(1)} %fusion.38), channel_id=1, source_target_pairs={{0,15},{1,0},{2,1},{3,2},{4,3},{5,4},{6,5},{7,6},{8,7},{9,8},{10,9... | collective-permute-start | bytes 589832 | tf_op jit(solution)/shard_map/ppermute | solution.py:15
  44.7 16.7 %collective-permute-start.6 = (f32[2,16,4,3,1,128]{5,1,4,2,3,0:T(8,128)S(1)}, f32[2,16,4,3,1,128]{5,1,4,2,3,0:T(8,128)S(1)}, u32[]{:S(2)}, u32[]{:S(2)}) collective-permute-start(f32[2,16,4,3,1,128]{5,1,4,2,3,0:T(8,128)S(1)} %pad_maximum_fusion.13), channel_id=1, source_target_pairs={{0,1},{1,2},{2,3},{3,4},{4,5},{5,6},{6,7},{7,8},{8,9},{9,10},{10,1... | collective-permute-start | bytes 589832 | tf_op jit(solution)/shard_map/ppermute | solution.py:15
  48.5 15.6 %collective-permute-start.2 = (f32[2,16,4,3,1,128]{5,1,4,2,3,0:T(8,128)S(1)}, f32[2,16,4,3,1,128]{5,1,4,2,3,0:T(8,128)S(1)}, u32[]{:S(2)}, u32[]{:S(2)}) collective-permute-start(f32[2,16,4,3,1,128]{5,1,4,2,3,0:T(8,128)S(1)} %fusion.37), channel_id=1, source_target_pairs={{0,15},{1,0},{2,1},{3,2},{4,3},{5,4},{6,5},{7,6},{8,7},{9,8},{10,9... | collective-permute-start | bytes 589832 | tf_op jit(solution)/shard_map/ppermute | solution.py:15
  62.0 15.4 %collective-permute-start.7 = (f32[2,16,4,3,1,128]{5,1,4,2,3,0:T(8,128)S(1)}, f32[2,16,4,3,1,128]{5,1,4,2,3,0:T(8,128)S(1)}, u32[]{:S(2)}, u32[]{:S(2)}) collective-permute-start(f32[2,16,4,3,1,128]{5,1,4,2,3,0:T(8,128)S(1)} %pad_maximum_fusion.12), channel_id=1, source_target_pairs={{0,1},{1,2},{2,3},{3,4},{4,5},{5,6},{6,7},{7,8},{8,9},{9,10},{10,1... | collective-permute-start | bytes 589832 | tf_op jit(solution)/shard_map/ppermute | solution.py:15
  64.7 12.2 %collective-permute-start.3 = (f32[2,16,4,3,1,128]{5,1,4,2,3,0:T(8,128)S(1)}, f32[2,16,4,3,1,128]{5,1,4,2,3,0:T(8,128)S(1)}, u32[]{:S(2)}, u32[]{:S(2)}) collective-permute-start(f32[2,16,4,3,1,128]{5,1,4,2,3,0:T(8,128)S(1)} %fusion.36), channel_id=1, source_target_pairs={{0,15},{1,0},{2,1},{3,2},{4,3},{5,4},{6,5},{7,6},{8,7},{9,8},{10,9... | collective-permute-start | bytes 589832 | tf_op jit(solution)/shard_map/ppermute | solution.py:15
  143.9 30.6 %copy-start.1 = (f32[4,2,16,4,3,4,128]{6,2,5,3,4,1,0:T(8,128)S(1)}, f32[4,2,16,4,3,4,128]{6,2,5,3,4,1,0:T(8,128)}, u32[]{:S(2)}) copy-start(f32[4,2,16,4,3,4,128]{6,2,5,3,4,1,0:T(8,128)} %get-tuple-element.27) | copy-start | bytes 9437188 | tf_op jit(solution)/shard_map/cond
  174.5 32.1 %copy-start.3 = (f32[2]{0:T(128)S(1)}, f32[2]{0:T(128)}, u32[]{:S(2)}) copy-start(f32[2]{0:T(128)} %constant.36.clone.2) | copy-start | bytes 28 | tf_op jit(solution)/shard_map/cond
  242.3 215.4 %copy-start.2 = (s32[4]{0:T(128)S(1)}, s32[4]{0:T(128)}, u32[]{:S(2)}) copy-start(s32[4]{0:T(128)} %param.8) | copy-start | bytes 52
Sparse Core Ops, SparseCore 0:
  9.2 103.4 all-gather.1
  255.8 200.4 reduce-scatter.3
where the time goes:
time: 475 us; the launch traced here: 466 us
  waiting for transfers between devices  277 us (58%)
  matrix products  62 us (13%)
  other arithmetic  43.9 us (9%)
  local copies, waits for them, and re-layouts  38.2 us (8%)
  starting transfers between devices  16.1 us (3%)
  blocking collectives  14.9 us (3%)
  between operations  14.3 us (3%)
    unnamed x3, waiting for transfers between devices  201 us
    dot_general x2, matrix products, pair_terms(): jnp.einsum('gaisczx,kdjsczx->kgadji', mixed_block, transported, precision...  61.6 us
    ppermute x8, waiting for transfers between devices, passed_along(): lax.ppermute(value, axis, [(i, (i + by) % devices) for i in range(devices)])  43.3 us
    all_gather x1, waiting for transfers between devices, local(): arrived = lax.all_gather(eigenvectors, 'eig', axis=1, tiled=True)  32.8 us
    another operation x1, other arithmetic, spin_mix(): return jnp.stack([swapped, chiral])  18.5 us
    ppermute x8, starting transfers between devices, passed_along(): lax.ppermute(value, axis, [(i, (i + by) % devices) for i in range(devices)])  16 us
    unnamed x8, local copies, waits for them, and re-layouts  15.5 us
    all_to_all x1, blocking collectives, local(): lax.all_to_all(packed, 'eig', split_axis=4, concat_axis=4, tiled=True)  14.9 us
  transfers between devices with their start and end apart: 10, of which 6 were waited for; matrix products, arithmetic and copies ran while one was open for 2% of the time, Pallas kernels for 0%

commit v1 on v0

v1 whole, which is shorter than its diff:
```python
import jax
import jax.numpy as jnp
from jax import lax
from jax.experimental import pallas as pl
from jax.experimental.pallas import tpu as pltpu
from jax.sharding import Mesh, PartitionSpec as P

EIG = ("ylo", "x", "core")
SPACE = ("z", "yhi")
PLANE = ("yhi", "ylo", "x")
SIZES = {"ylo": 2, "x": 4, "core": 2, "z": 8, "yhi": 2}

NZD = 4
LANES = 128
PIECE = 16
ROWS = 104


def roll(value, by):
    return pltpu.roll(value, by % LANES, value.ndim - 1)


def lanes_of(value):
    return lax.broadcasted_iota(jnp.int32, value.shape, value.ndim - 1)


def exchange_pieces(rows):
    piece = lanes_of(rows[0]) >> 4
    for bit in (1, 2, 4):
        upper = (piece & bit) != 0
        after = list(rows)
        for i in range(8):
            if i & bit == 0:
                low, high = rows[i], rows[i | bit]
                after[i] = jnp.where(upper, roll(high, 16 * bit), low)
                after[i | bit] = jnp.where(upper, high, roll(low, -16 * bit))
        rows = after
    return rows


def cut_kernel(place_ref, vectors_ref, links_ref, out_ref):
    for j in range(2):
        for colour in range(3):
            for half in range(2):
                def load(part, spin, plane):
                    first = (((part * 16 + half * 8) * 4 + spin) * 3 + colour) * 4 + plane
                    return vectors_ref[pl.ds(first, 8, stride=48), :]

                plus = [None] * 8
                minus = [None] * 8
                for plane in range(4):
                    upper_real, upper_imag = load(0, j, plane), load(1, j, plane)
                    lower_real, lower_imag = load(0, j + 2, plane), load(1, j + 2, plane)
                    plus[plane] = upper_real - lower_imag
                    plus[4 + plane] = upper_imag + lower_real
                    minus[plane] = upper_real + lower_imag
                    minus[4 + plane] = upper_imag - lower_real
                for sign, rows in ((0, plus), (1, minus)):
                    first = (sign * 3 + colour) * 16 + half * 8
                    for block, value in enumerate(exchange_pieces(rows)):
                        out_ref[j * 8 + block, first : first + 8, :] = value
    own = place_ref[0]
    row = lax.broadcasted_iota(jnp.int32, (8, LANES), 0)
    rows = []
    for part in range(2):
        for plane in range(4):
            mine = links_ref[pl.ds((part * 9 + own) * 4 + plane, 1), :]
            last = links_ref[(part * 9 + 8) * 4 + plane : (part * 9 + 8) * 4 + plane + 1, :]
            rows.append(jnp.where(row == 0, mine, last))
    for block, value in enumerate(exchange_pieces(rows)):
        out_ref[block, 96:104, :] = value
        out_ref[8 + block, 96:104, :] = value


def shifted(here, here_swapped, above, above_swapped, by):
    if by == 4:
        return above, above_swapped
    keep = ((lanes_of(here) >> 4) & 3) >= by
    return (
        roll(jnp.where(keep, here, above_swapped), -16 * by),
        roll(jnp.where(keep, here_swapped, above), -16 * by),
    )


def field_kernel(
    place_ref, own_ref, other_ref, above_ref, out_ref, a_hi, a_lo, r_hi, r_lo, f_hi, f_lo, link_ref
):
    cls = place_ref[1]
    real_half = lax.broadcasted_iota(jnp.int32, (1, LANES), 1) < 64

    for source, start in ((own_ref, cls * LANES), (other_ref, (1 - cls) * LANES)):
        start = pl.multiple_of(start, LANES)
        for sign in range(2):
            for half in range(2):
                for colour in range(3):
                    first = (sign * 3 + colour) * 16
                    value = source[half, :, first : first + 16, :].reshape(LANES, LANES)
                    swapped = roll(value, 64)
                    turned = jnp.where(real_half, -swapped, swapped)
                    column = (half * 3 + colour) * LANES
                    for held, hi_ref, lo_ref in ((value, a_hi, a_lo), (turned, r_hi, r_lo)):
                        hi = held.astype(jnp.bfloat16)
                        lo = (held - hi.astype(jnp.float32)).astype(jnp.bfloat16)
                        hi_ref[sign, pl.ds(start, LANES), column : column + LANES] = hi
                        lo_ref[sign, pl.ds(start, LANES), column : column + LANES] = lo

    def link_rows(source):
        entries = [source[i, 96:97, :] for i in range(8)] + [source[0, 97:98, :]]
        return [[entries[3 * i + j] for j in range(3)] for i in range(3)]

    links = [link_rows(own_ref.at[0]), link_rows(own_ref.at[1]), link_rows(above_ref)]
    swapped_links = [[[roll(e, 64) for e in line] for line in tile] for tile in links]
    for half in range(2):
        product = links[half]
        for by in range(1, NZD + 1):
            if by > 1:
                moved = [
                    [
                        shifted(
                            links[half][i][j],
                            swapped_links[half][i][j],
                            links[half + 1][i][j],
                            swapped_links[half + 1][i][j],
                            by - 1,
                        )
                        for j in range(3)
                    ]
                    for i in range(3)
                ]
                product = [
                    [
                        sum(
                            spread[i][m][0] * moved[m][j][0] + spread[i][m][1] * moved[m][j][1]
                            for m in range(3)
                        )
                        for j in range(3)
                    ]
                    for i in range(3)
                ]
            spread = []
            for i in range(3):
                line = []
                for j in range(3):
                    entry = product[i][j]
                    swapped = roll(entry, 64)
                    real = jnp.where(real_half, entry, swapped)
                    imag = jnp.where(real_half, -swapped, entry)
                    at = ((((by - 1) * 2 + half) * 3 + i) * 3 + j) * 2
                    link_ref[at : at + 1, :] = real
                    link_ref[at + 1 : at + 2, :] = imag
                    line.append((real, imag))
                spread.append(line)

    def transport(block, carry):
        row = pl.multiple_of(block * 16, 16)
        for sign in range(2):
            tiles = []
            swapped = []
            for source in (own_ref.at[0], own_ref.at[1], above_ref):
                line = [
                    source[block, (sign * 3 + c) * 16 : (sign * 3 + c) * 16 + 16, :]
                    for c in range(3)
                ]
                tiles.append(line)
                swapped.append([roll(value, 64) for value in line])
            for by in range(1, NZD + 1):
                for half in range(2):
                    moved = [
                        shifted(
                            tiles[half][c],
                            swapped[half][c],
                            tiles[half + 1][c],
                            swapped[half + 1][c],
                            by,
                        )
                        for c in range(3)
                    ]
                    for i in range(3):
                        total = None
                        for j in range(3):
                            at = ((((by - 1) * 2 + half) * 3 + i) * 3 + j) * 2
                            term = (
                                link_ref[at : at + 1, :] * moved[j][0]
                                + link_ref[at + 1 : at + 2, :] * moved[j][1]
                            )
                            total = term if total is None else total + term
                        hi = total.astype(jnp.bfloat16)
                        lo = (total - hi.astype(jnp.float32)).astype(jnp.bfloat16)
                        column = (half * 3 + i) * LANES
                        rows = pl.ds(pl.multiple_of((by - 1) * LANES + row, 16), 16)
                        f_hi[sign, rows, column : column + LANES] = hi
                        f_lo[sign, rows, column : column + LANES] = lo
        return carry

    lax.fori_loop(0, 8, transport, 0)

    def product_of(left, right):
        return lax.dot_general(
            left, right, (((1,), (1,)), ((), ())), preferred_element_type=jnp.float32
        )

    for sign in range(2):
        for part, (hi_ref, lo_ref) in enumerate(((a_hi, a_lo), (r_hi, r_lo))):
            total = product_of(f_hi[sign], hi_ref[1 - sign])
            total = total + product_of(f_hi[sign], lo_ref[1 - sign])
            total = total + product_of(f_lo[sign], hi_ref[1 - sign])
            for by in range(NZD):
                for block in range(8):
                    for half in range(2):
                        out_ref[half, block, by * 4 + sign * 2 + part] = total[
                            by * LANES + block * 16 : by * LANES + block * 16 + 16,
                            half * LANES : half * LANES + LANES,
                        ]


def gather_kernel(separations_ref, shares_ref, out_ref):
    fields = []
    for q in range(NZD):
        at = separations_ref[q] * 4
        sums = []
        for index in range(4):
            total = shares_ref[0, at + index]
            for source in range(1, 16):
                total = total + shares_ref[source, at + index]
            sums.append(total * 0.5)
        plus_real, plus_imag, minus_real, minus_imag = sums
        fields.append(
            [
                plus_imag - minus_imag,
                minus_real - plus_real,
                plus_real + minus_real,
                plus_imag + minus_imag,
            ]
        )
    for pair in range(2):
        for z, value in enumerate(exchange_pieces(fields[2 * pair] + fields[2 * pair + 1])):
            out_ref[z, pair] = value


def place_kernel(own_ref, mirror_ref, out_ref):
    padding = jnp.zeros((LANES - 32, LANES), jnp.float32)
    turned = jnp.concatenate([own_ref[0], own_ref[1], padding]).T
    for pair in range(2):
        for index in range(8):
            q = pair * 2 + index // 4
            g = (index // 2) % 2
            part = index % 2
            out_ref[0, q, g, part] = turned[
                index * 16 : index * 16 + 16, pair * 16 : pair * 16 + 16
            ]
            value = mirror_ref[pair, :, index * 16 : index * 16 + 16]
            out_ref[1, q, g, part] = -value if part else value


SMEM = pl.BlockSpec(memory_space=pltpu.SMEM)
VMEM = pl.BlockSpec(memory_space=pltpu.VMEM)


def call(kernel, shape, inputs, scratch=(), limit=32, flops=0):
    specs = [SMEM if value.dtype == jnp.int32 else VMEM for value in inputs]
    count = sum(value.size for value in inputs)
    return pl.pallas_call(
        kernel,
        out_shape=jax.ShapeDtypeStruct(shape, jnp.float32),
        in_specs=specs,
        out_specs=VMEM,
        scratch_shapes=list(scratch),
        compiler_params=pltpu.CompilerParams(vmem_limit_bytes=limit * 1024 * 1024),
        cost_estimate=pl.CostEstimate(flops=flops, bytes_accessed=count * 8, transcendentals=0),
    )(*inputs)


def local(eigenvectors, gauge_links, separations):
    cls = lax.axis_index("core")
    block = lax.axis_index(("ylo", "x"))
    place = jnp.stack([block, cls]).astype(jnp.int32)

    vectors = eigenvectors.reshape(1536, LANES)
    links = gauge_links.reshape(72, LANES)
    chunks = call(cut_kernel, (16, ROWS, LANES), (place, vectors, links))
    own = lax.all_to_all(chunks, PLANE, split_axis=0, concat_axis=0, tiled=True)
    own = own.reshape(2, 8, ROWS, LANES)
    other = lax.ppermute(own, "core", [(0, 1), (1, 0)])
    above = lax.ppermute(own[0], "z", [(i, (i - 1) % 8) for i in range(8)])

    held = jnp.bfloat16
    shares = call(
        field_kernel,
        (2, 8, 16, 16, LANES),
        (place, own, other, above),
        [
            pltpu.VMEM((2, 256, 768), held),
            pltpu.VMEM((2, 256, 768), held),
            pltpu.VMEM((2, 256, 768), held),
            pltpu.VMEM((2, 256, 768), held),
            pltpu.VMEM((2, 512, 768), held),
            pltpu.VMEM((2, 512, 768), held),
            pltpu.VMEM((144, LANES), jnp.float32),
        ],
        limit=48,
        flops=2 * 2 * 2 * 3 * 512 * 768 * 256,
    )
    shares = shares.reshape(16, 16, 16, LANES)
    shares = lax.all_to_all(shares, PLANE, split_axis=0, concat_axis=0, tiled=True)
    parts = call(gather_kernel, (8, 2, 16, LANES), (separations, shares))
    parts = lax.all_to_all(parts, "z", split_axis=0, concat_axis=0, tiled=True)
    block = jnp.sum(parts, axis=0)
    mirror = lax.ppermute(
        block, EIG + SPACE, [(e * 16 + s, s * 16 + e) for e in range(16) for s in range(16)]
    )
    return call(place_kernel, (2, NZD, 2, 2, 16, 16), (block, mirror))


def solution(mesh):
    fine = Mesh(mesh.devices.reshape([SIZES[name] for name in EIG + SPACE]), EIG + SPACE)
    return jax.shard_map(
        local,
        mesh=fine,
        in_specs=(
            P(None, EIG, None, None, SPACE, None),
            P(None, None, None, SPACE, None),
            P(),
        ),
        out_specs=P(None, None, None, None, SPACE, EIG),
        check_vma=False,
    )
```

time: 475 us -> 107 us (0.23); the launches traced: 466 us -> 106 us
  waiting for transfers between devices: 277 us -> 18.9 us
  matrix products: 62 us -> 0 us
  blocking collectives: 14.9 us -> 64.8 us
  other arithmetic: 43.9 us -> 0.09 us
  local copies, waits for them, and re-layouts: 38.2 us -> 1.93 us
  between operations: 14.3 us -> 0.05 us
  Pallas kernels: 0 us -> 12.6 us
  starting transfers between devices: 16.1 us -> 7.86 us
    unnamed x3 -> x0, waiting for transfers between devices: 201 us -> none
    dot_general x3 -> x0, matrix products: 62 us -> none  [the longest x2 61.6 us: pair_terms(): jnp.einsum('gaisczx,kdjsczx->kgadji', mixed_block, transported, precision...]
    all_to_all x1 -> x3, blocking collectives: 14.9 us -> 64.8 us  [the longest x1 31.2 us: local(): lax.all_to_all(shares, PLANE, split_axis=0, concat_axis=0, tiled=True)]
    all_gather x1 -> x0, waiting for transfers between devices: 32.8 us -> none  [local(): arrived = lax.all_gather(eigenvectors, 'eig', axis=1, tiled=True)]
    ppermute x8 -> x3, waiting for transfers between devices: 43.3 us -> 18.9 us  [the longest x1 9.75 us: local(): above = lax.ppermute(own[0], 'z', [(i, (i - 1) % 8) for i in range(8)])]
    another operation x32 -> x1, other arithmetic: 22.2 us -> 0.07 us  [local(): place = jnp.stack([block, cls]).astype(jnp.int32)]
    unnamed x8 -> x6, local copies, waits for them, and re-layouts: 15.5 us -> 1.91 us
    slice x5 -> x0, other arithmetic: 12.8 us -> none  [the longest x1 12.7 us: spin_mix(): eigen_block[:, :, 2:]]
  transfers between devices with their start and end apart: 10 -> 3, of which waited for: 6 -> 2; matrix products, arithmetic and copies ran while one was open for 2% -> 0% of each run, Pallas kernels for 0% -> 0%
where the time goes in v1:
time: 107 us; the launch traced here: 106 us
  blocking collectives  64.8 us (61%)
  waiting for transfers between devices  18.9 us (18%)
  Pallas kernels  12.6 us (12%)
  starting transfers between devices  7.86 us (7%)
  local copies, waits for them, and re-layouts  1.93 us (2%)
    all_to_all x1, blocking collectives, local(): lax.all_to_all(shares, PLANE, split_axis=0, concat_axis=0, tiled=True)  31.2 us
    all_to_all x1, blocking collectives, local(): own = lax.all_to_all(chunks, PLANE, split_axis=0, concat_axis=0, tiled=True)  19.7 us
    all_to_all x1, blocking collectives, local(): parts = lax.all_to_all(parts, 'z', split_axis=0, concat_axis=0, tiled=True)  14 us
    pallas_call x4, Pallas kernels, call(): pl.pallas_call(kernel, out_shape=jax.ShapeDtypeStruct(shape, jnp.float32)...  12.6 us
    ppermute x1, waiting for transfers between devices, local(): above = lax.ppermute(own[0], 'z', [(i, (i - 1) % 8) for i in range(8)])  9.75 us
    ppermute x1, waiting for transfers between devices, local(): lax.ppermute(block, EIG + SPACE, [(e * 16 + s, s * 16 + e) for e in range...  9.15 us
    ppermute x1, starting transfers between devices, local(): above = lax.ppermute(own[0], 'z', [(i, (i - 1) % 8) for i in range(8)])  5.93 us
  transfers between devices with their start and end apart: 3, of which 2 were waited for; matrix products, arithmetic and copies ran while one was open for 0% of the time, Pallas kernels for 0%

profile of v1, /device:TPU:24, one launch (start us, length us, event | category | flops | bytes accessed | tf_op | source)
XLA Modules:
  0.0 106.3 jit_solution(9049706322746963579)
XLA Ops:
  0.0 0.1 pad_add_fusion.place_ref
  0.1 0.0 copy-start
  0.1 1.1 %copy-done = f32[2,16,4,3,4,128]{5,4,3,2,1,0:T(4,128)S(1)} copy-done((f32[2,16,4,3,4,128]{5,4,3,2,1,0:T(4,128)S(1)}, f32[2,16,4,3,4,128]{5,4,3,2,1,0:T(4,128)}, u32[]{:S(2)}) %copy-start) | copy-done | bytes 786456
  1.2 0.0 copy-start.1
  1.2 0.8 copy-done.1
  2.0 3.4 %shard_map.37 = f32[16,104,128]{2,1,0:T(8,128)S(1)} custom-call(s32[2]{0:T(128)S(1)} %pad_add_fusion.place_ref, f32[1536,128]{1,0:T(8,128)S(1)} %bitcast.9, f32[72,128]{1,0:T(8,128)S(1)} %bitcast.10), custom_call_target="tpu_custom_call" | custom-call | bytes 1646608 | tf_op jit(solution)/shard_map/pallas_call | solution.py:262
  5.4 19.7 %all_to_all.15 = f32[16,104,128]{2,1,0:T(8,128)S(1)} all-to-all(f32[16,104,128]{2,1,0:T(8,128)S(1)} %shard_map.37), channel_id=1, replica_groups=mesh['ylo'=2,'x'=4,'core'=2,'z'=8,'yhi'=2] {'yhi','ylo','x'}, dimensions={0} | all-to-all | bytes 1703936 | tf_op jit(solution)/shard_map/all_to_all | solution.py:281
  25.1 0.0 collective-permute-start
  25.2 5.9 %collective-permute-start.1 = (f32[8,104,128]{2,1,0:T(8,128)S(1)}, f32[8,104,128]{2,1,0:T(8,128)S(1)}, u32[]{:S(2)}, u32[]{:S(2)}) collective-permute-start(f32[8,104,128]{2,1,0:T(8,128)S(1)} %slice.5), channel_id=1, source_target_pairs={{0,14},{2,0},{4,2},{6,4},{8,6},{10,8},{12,10},{14,12},{1,15},{3,1}... | collective-permute-start | bytes 1277960 | tf_op jit(solution)/shard_map/ppermute | solution.py:284
  31.1 9.7 %collective-permute-done.1.above_ref = f32[8,104,128]{2,1,0:T(8,128)S(1)} collective-permute-done((f32[8,104,128]{2,1,0:T(8,128)S(1)}, f32[8,104,128]{2,1,0:T(8,128)S(1)}, u32[]{:S(2)}, u32[]{:S(2)}) %collective-permute-start.1) | collective-permute-done | bytes 426016 | tf_op jit(solution)/shard_map/ppermute | solution.py:284
  40.8 0.0 collective-permute-done.other_ref
  40.8 7.4 %shard_map.38 = f32[2,8,16,16,128]{4,3,2,1,0:T(8,128)S(1)} custom-call(s32[2]{0:T(128)S(1)} %pad_add_fusion.place_ref, f32[2,8,104,128]{3,2,1,0:T(8,128)S(1)} %bitcast.8, f32[2,8,104,128]{3,2,1,0:T(8,128)S(1)} %collective-permute-done.other_ref, f32[8,104,128]{2,1,0:T(8,128)S(1)} %collective-permute-done.1.above_ref), custom_call_target="tpu_custom_call" | custom-call | flops 2415919104 | bytes 4259856 | tf_op jit(solution)/shard_map/pallas_call | solution.py:262
  48.3 0.0 copy-start.2
  48.3 31.2 %all_to_all.16.shares_ref = f32[16,16,16,128]{3,2,1,0:T(8,128)S(1)} all-to-all(f32[16,16,16,128]{3,2,1,0:T(8,128)S(1)} %bitcast.6), channel_id=1, replica_groups=mesh['ylo'=2,'x'=4,'core'=2,'z'=8,'yhi'=2] {'yhi','ylo','x'}, dimensions={0} | all-to-all | bytes 4194304 | tf_op jit(solution)/shard_map/all_to_all | solution.py:304
  79.5 0.0 copy-done.2
  79.5 0.9 shard_map.39
  80.3 14.0 %all_to_all.17 = f32[8,2,16,128]{3,2,1,0:T(8,128)S(1)} all-to-all(f32[8,2,16,128]{3,2,1,0:T(8,128)S(1)} %shard_map.39), channel_id=1, replica_groups=mesh['ylo'=2,'x'=4,'core'=2,'z'=8,'yhi'=2] {'z'}, dimensions={0} | all-to-all | bytes 262144 | tf_op jit(solution)/shard_map/all_to_all | solution.py:306
  94.3 1.9 %collective-permute-start.2 = (f32[2,16,128]{2,1,0:T(8,128)S(1)}, f32[2,16,128]{2,1,0:T(8,128)S(1)}, u32[]{:S(2)}, u32[]{:S(2)}) collective-permute-start(f32[2,16,128]{2,1,0:T(8,128)S(1)} %reduce_sum.9.own_ref), channel_id=1, source_target_pairs={{0,0},{1,16},{2,32},{3,48},{4,64},{5,80},{6,96},{7,112},{8,128},{9... | collective-permute-start | bytes 49160 | tf_op jit(solution)/shard_map/ppermute | solution.py:308
  96.3 9.1 %collective-permute-done.2.mirror_ref = f32[2,16,128]{2,1,0:T(8,128)S(1)} collective-permute-done((f32[2,16,128]{2,1,0:T(8,128)S(1)}, f32[2,16,128]{2,1,0:T(8,128)S(1)}, u32[]{:S(2)}, u32[]{:S(2)}) %collective-permute-start.2) | collective-permute-done | bytes 16416 | tf_op jit(solution)/shard_map/ppermute | solution.py:308
  105.4 0.9 shard_map.40
  (2 shorter events, 0.0 us)
Async XLA Ops:
  0.1 1.1 %copy-start = (f32[2,16,4,3,4,128]{5,4,3,2,1,0:T(4,128)S(1)}, f32[2,16,4,3,4,128]{5,4,3,2,1,0:T(4,128)}, u32[]{:S(2)}) copy-start(f32[2,16,4,3,4,128]{5,4,3,2,1,0:T(4,128)} %param.3) | copy-start | bytes 2359300
  1.2 0.8 copy-start.1
  25.1 15.7 %collective-permute-start = (f32[2,8,104,128]{3,2,1,0:T(8,128)S(1)}, f32[2,8,104,128]{3,2,1,0:T(8,128)S(1)}, u32[]{:S(2)}, u32[]{:S(2)}) collective-permute-start(f32[2,8,104,128]{3,2,1,0:T(8,128)S(1)} %bitcast.7), channel_id=1, source_target_pairs={{0,16},{16,0},{1,17},{17,1},{2,18},{18,2},{3,19},{19,3},{4,20},{20... | collective-permute-start | bytes 2555912 | tf_op jit(solution)/shard_map/ppermute | solution.py:283
  25.2 15.7 %collective-permute-start.1 = (f32[8,104,128]{2,1,0:T(8,128)S(1)}, f32[8,104,128]{2,1,0:T(8,128)S(1)}, u32[]{:S(2)}, u32[]{:S(2)}) collective-permute-start(f32[8,104,128]{2,1,0:T(8,128)S(1)} %slice.5), channel_id=1, source_target_pairs={{0,14},{2,0},{4,2},{6,4},{8,6},{10,8},{12,10},{14,12},{1,15},{3,1}... | collective-permute-start | bytes 1277960 | tf_op jit(solution)/shard_map/ppermute | solution.py:284
  48.3 31.2 %copy-start.2 = (s32[4]{0:T(128)S(1)}, s32[4]{0:T(128)}, u32[]{:S(2)}) copy-start(s32[4]{0:T(128)} %separations_ref.1) | copy-start | bytes 52
  94.3 11.1 %collective-permute-start.2 = (f32[2,16,128]{2,1,0:T(8,128)S(1)}, f32[2,16,128]{2,1,0:T(8,128)S(1)}, u32[]{:S(2)}, u32[]{:S(2)}) collective-permute-start(f32[2,16,128]{2,1,0:T(8,128)S(1)} %reduce_sum.9.own_ref), channel_id=1, source_target_pairs={{0,0},{1,16},{2,32},{3,48},{4,64},{5,80},{6,96},{7,112},{8,128},{9... | collective-permute-start | bytes 49160 | tf_op jit(solution)/shard_map/ppermute | solution.py:308

commit v2 on v1

v2 whole, which is shorter than its diff:
```python
import jax
import jax.numpy as jnp
from jax import lax
from jax.experimental import pallas as pl
from jax.experimental.pallas import tpu as pltpu
from jax.sharding import Mesh, PartitionSpec as P

EIG = ("ylo", "x", "core")
SPACE = ("z", "yhi")
PLANE = ("yhi", "ylo", "x")
SIZES = {"ylo": 2, "x": 4, "core": 2, "z": 8, "yhi": 2}

NZD = 4
LANES = 128
PIECE = 16
ROWS = 104


def roll(value, by):
    return pltpu.roll(value, by % LANES, value.ndim - 1)


def lanes_of(value):
    return lax.broadcasted_iota(jnp.int32, value.shape, value.ndim - 1)


def exchange_pieces(rows):
    piece = lanes_of(rows[0]) >> 4
    for bit in (1, 2, 4):
        upper = (piece & bit) != 0
        after = list(rows)
        for i in range(8):
            if i & bit == 0:
                low, high = rows[i], rows[i | bit]
                after[i] = jnp.where(upper, roll(high, 16 * bit), low)
                after[i | bit] = jnp.where(upper, high, roll(low, -16 * bit))
        rows = after
    return rows


def cut_kernel(vectors_hbm, links_hbm, out_ref, vectors_ref, links_ref, arrived):
    copies = [
        pltpu.make_async_copy(vectors_hbm.at[rows], vectors_ref.at[rows], arrived.at[index])
        for index, rows in enumerate(pl.ds(i * 384, 384) for i in (0, 2, 1, 3))
    ]
    copies.append(pltpu.make_async_copy(links_hbm, links_ref, arrived.at[4]))
    for copy in copies:
        copy.start()
    for half in range(2):
        copies[2 * half].wait()
        copies[2 * half + 1].wait()
        for j in range(2):
            for colour in range(3):

                def load(part, spin, plane):
                    first = (((part * 16 + half * 8) * 4 + spin) * 3 + colour) * 4 + plane
                    return vectors_ref[pl.ds(first, 8, stride=48), :]

                plus = [None] * 8
                minus = [None] * 8
                for plane in range(4):
                    upper_real, upper_imag = load(0, j, plane), load(1, j, plane)
                    lower_real, lower_imag = load(0, j + 2, plane), load(1, j + 2, plane)
                    plus[plane] = upper_real - lower_imag
                    plus[4 + plane] = upper_imag + lower_real
                    minus[plane] = upper_real + lower_imag
                    minus[4 + plane] = upper_imag - lower_real
                both = [jnp.stack(pair) for pair in zip(plus, minus)]
                for block, value in enumerate(exchange_pieces(both)):
                    for sign in range(2):
                        first = (sign * 3 + colour) * 16 + half * 8
                        out_ref[j * 8 + block, first : first + 8, :] = value[sign]
    copies[4].wait()
    own = lax.axis_index(("ylo", "x"))
    row = lax.broadcasted_iota(jnp.int32, (8, LANES), 0)
    rows = []
    for part in range(2):
        for plane in range(4):
            mine = links_ref[pl.ds((part * 9 + own) * 4 + plane, 1), :]
            last = links_ref[(part * 9 + 8) * 4 + plane : (part * 9 + 8) * 4 + plane + 1, :]
            rows.append(jnp.where(row == 0, mine, last))
    for block, value in enumerate(exchange_pieces(rows)):
        out_ref[block, 96:104, :] = value
        out_ref[8 + block, 96:104, :] = value


def shifted(here, here_swapped, above, above_swapped, by):
    if by == 4:
        return above, above_swapped
    keep = ((lanes_of(here) >> 4) & 3) >= by
    return (
        roll(jnp.where(keep, here, above_swapped), -16 * by),
        roll(jnp.where(keep, here_swapped, above), -16 * by),
    )


def split(value):
    hi = value.astype(jnp.bfloat16)
    return hi, (value - hi.astype(jnp.float32)).astype(jnp.bfloat16)


def spread_link(entry):
    real_half = lanes_of(entry) < 64
    swapped = roll(entry, 64)
    return jnp.where(real_half, entry, swapped), jnp.where(real_half, -swapped, entry)


def link_rows(source):
    entries = [source[i, 96:97, :] for i in range(8)] + [source[0, 97:98, :]]
    return [[entries[3 * i + j] for j in range(3)] for i in range(3)]


def multiply_links(here_ref, above_ref, link_ref):
    here, above = link_rows(here_ref), link_rows(above_ref)
    here_swapped = [[roll(e, 64) for e in line] for line in here]
    above_swapped = [[roll(e, 64) for e in line] for line in above]
    product = here
    for by in range(1, NZD + 1):
        if by > 1:
            moved = [
                [
                    shifted(here[i][j], here_swapped[i][j], above[i][j], above_swapped[i][j], by - 1)
                    for j in range(3)
                ]
                for i in range(3)
            ]
            product = [
                [
                    sum(
                        factors[i][m][0] * moved[m][j][0] + factors[i][m][1] * moved[m][j][1]
                        for m in range(3)
                    )
                    for j in range(3)
                ]
                for i in range(3)
            ]
        factors = [[spread_link(e) for e in line] for line in product]
        for i in range(3):
            for j in range(3):
                at = ((by - 1) * 9 + i * 3 + j) * 2
                link_ref[at : at + 1, :] = factors[i][j][0]
                link_ref[at + 1 : at + 2, :] = factors[i][j][1]


def transport(here_ref, above_ref, link_ref, hi_ref, lo_ref):
    def one_block(block, carry):
        for sign in range(2):
            here, above, here_swapped, above_swapped = [], [], [], []
            for c in range(3):
                first = (sign * 3 + c) * 16
                here.append(here_ref[block, first : first + 16, :])
                above.append(above_ref[block, first : first + 16, :])
                here_swapped.append(roll(here[c], 64))
                above_swapped.append(roll(above[c], 64))
            for by in range(1, NZD + 1):
                rows = pl.ds(pl.multiple_of((by - 1) * LANES + block * 16, 16), 16)
                moved = [
                    shifted(here[c], here_swapped[c], above[c], above_swapped[c], by)
                    for c in range(3)
                ]
                for i in range(3):
                    total = None
                    for j in range(3):
                        at = ((by - 1) * 9 + i * 3 + j) * 2
                        term = (
                            link_ref[at : at + 1, :] * moved[j][0]
                            + link_ref[at + 1 : at + 2, :] * moved[j][1]
                        )
                        total = term if total is None else total + term
                    hi, lo = split(total)
                    hi_ref[sign, rows, i * LANES : i * LANES + LANES] = hi
                    lo_ref[sign, rows, i * LANES : i * LANES + LANES] = lo
        return carry

    lax.fori_loop(0, 8, one_block, 0, unroll=8)


def prepare_rows(source, half, start, refs):
    start = pl.multiple_of(start, LANES)
    for sign in range(2):
        for colour in range(3):
            first = (sign * 3 + colour) * 16
            value = source[half, :, first : first + 16, :].reshape(LANES, LANES)
            swapped = roll(value, 64)
            turned = jnp.where(lanes_of(value) < 64, -swapped, swapped)
            at = (sign, pl.ds(start, LANES), slice(colour * LANES, colour * LANES + LANES))
            refs[0][at], refs[1][at] = split(value)
            refs[2][at], refs[3][at] = split(turned)


def products(sign, part, rows, hi_ref, lo_ref):
    def product_of(left, right):
        return lax.dot_general(
            left, right, (((1,), (1,)), ((), ())), preferred_element_type=jnp.float32
        )

    rows_hi, rows_lo = rows[2 * part][1 - sign], rows[2 * part + 1][1 - sign]
    total = product_of(hi_ref[sign], rows_hi)
    total = total + product_of(hi_ref[sign], rows_lo)
    return total + product_of(lo_ref[sign], rows_hi)


def low_kernel(
    own_ref, other_ref, sum_ref, u0, u1, u2, u3, d0, d1, d2, d3, f_hi, f_lo, link_ref
):
    cls = lax.axis_index("core")
    down, up = (d0, d1, d2, d3), (u0, u1, u2, u3)
    multiply_links(own_ref.at[0], own_ref.at[1], link_ref)
    transport(own_ref.at[0], own_ref.at[1], link_ref, f_hi, f_lo)
    for source, start in ((own_ref, cls * LANES), (other_ref, (1 - cls) * LANES)):
        prepare_rows(source, 0, start, down)
        prepare_rows(source, 1, start, up)
    for sign in range(2):
        for part in range(2):
            sum_ref[sign, part] = products(sign, part, down, f_hi, f_lo)


def high_kernel(own_ref, above_ref, sum_ref, u0, u1, u2, u3, out_ref, f_hi, f_lo, link_ref):
    multiply_links(own_ref.at[1], above_ref, link_ref)
    transport(own_ref.at[1], above_ref, link_ref, f_hi, f_lo)
    for sign in range(2):
        for part in range(2):
            total = sum_ref[sign, part] + products(sign, part, (u0, u1, u2, u3), f_hi, f_lo)
            for by in range(NZD):
                for block in range(8):
                    for half in range(2):
                        out_ref[half, block, by * 4 + sign * 2 + part] = total[
                            by * LANES + block * 16 : by * LANES + block * 16 + 16,
                            half * LANES : half * LANES + LANES,
                        ]


def gather_kernel(separations_ref, shares_ref, out_ref):
    fields = []
    for q in range(NZD):
        at = separations_ref[q] * 4
        sums = []
        for index in range(4):
            total = shares_ref[0, at + index]
            for source in range(1, 16):
                total = total + shares_ref[source, at + index]
            sums.append(total * 0.5)
        plus_real, plus_imag, minus_real, minus_imag = sums
        fields.append(
            [
                plus_imag - minus_imag,
                minus_real - plus_real,
                plus_real + minus_real,
                plus_imag + minus_imag,
            ]
        )
    for pair in range(2):
        for z, value in enumerate(exchange_pieces(fields[2 * pair] + fields[2 * pair + 1])):
            out_ref[z, pair] = value


def place_kernel(own_ref, mirror_ref, out_ref):
    padding = jnp.zeros((LANES - 32, LANES), jnp.float32)
    turned = jnp.concatenate([own_ref[0], own_ref[1], padding]).T
    for pair in range(2):
        for index in range(8):
            q = pair * 2 + index // 4
            g = (index // 2) % 2
            part = index % 2
            out_ref[0, q, g, part] = turned[
                index * 16 : index * 16 + 16, pair * 16 : pair * 16 + 16
            ]
            value = mirror_ref[pair, :, index * 16 : index * 16 + 16]
            out_ref[1, q, g, part] = -value if part else value


SMEM = pl.BlockSpec(memory_space=pltpu.SMEM)
VMEM = pl.BlockSpec(memory_space=pltpu.VMEM)


def call(kernel, outs, inputs, scratch=(), limit=32, flops=0, space=VMEM):
    shapes = [jax.ShapeDtypeStruct(shape, held) for shape, held in outs]
    specs = [SMEM if value.dtype == jnp.int32 else space for value in inputs]
    count = sum(value.size for value in inputs)
    return pl.pallas_call(
        kernel,
        out_shape=shapes,
        in_specs=specs,
        out_specs=[VMEM] * len(outs),
        scratch_shapes=list(scratch),
        compiler_params=pltpu.CompilerParams(vmem_limit_bytes=limit * 1024 * 1024),
        cost_estimate=pl.CostEstimate(flops=flops, bytes_accessed=count * 4, transcendentals=0),
    )(*inputs)


F32, B16 = jnp.float32, jnp.bfloat16
FIELD_SCRATCH = (
    pltpu.VMEM((2, 512, 384), B16),
    pltpu.VMEM((2, 512, 384), B16),
    pltpu.VMEM((72, LANES), F32),
)
LOW_SCRATCH = (pltpu.VMEM((2, 256, 384), B16),) * 4 + FIELD_SCRATCH
FIELD_FLOPS = 2 * 2 * 2 * 3 * 512 * 384 * 256


def local(eigenvectors, gauge_links, separations):
    vectors = eigenvectors.reshape(1536, LANES)
    links = gauge_links.reshape(72, LANES)
    (chunks,) = call(
        cut_kernel,
        [((16, ROWS, LANES), F32)],
        (vectors, links),
        (
            pltpu.VMEM((1536, LANES), F32),
            pltpu.VMEM((72, LANES), F32),
            pltpu.SemaphoreType.DMA((5,)),
        ),
        space=pl.BlockSpec(memory_space=pltpu.HBM),
    )
    own = lax.all_to_all(chunks, PLANE, split_axis=0, concat_axis=0, tiled=True)
    own = own.reshape(2, 8, ROWS, LANES)
    above = lax.ppermute(own[0], "z", [(i, (i - 1) % 8) for i in range(8)])
    other = lax.ppermute(own, "core", [(0, 1), (1, 0)])

    low = call(
        low_kernel,
        [((2, 2, 512, 256), F32)] + [((2, 256, 384), B16)] * 4,
        (own, other),
        LOW_SCRATCH,
        flops=FIELD_FLOPS,
    )
    (shares,) = call(
        high_kernel,
        [((2, 8, 16, 16, LANES), F32)],
        (own, above, *low),
        FIELD_SCRATCH,
        flops=FIELD_FLOPS,
    )
    shares = shares.reshape(16, 16, 16, LANES)
    shares = lax.all_to_all(shares, PLANE, split_axis=0, concat_axis=0, tiled=True)
    (parts,) = call(gather_kernel, [((8, 2, 16, LANES), F32)], (separations, shares))
    parts = lax.all_to_all(parts, "z", split_axis=0, concat_axis=0, tiled=True)
    block = jnp.sum(parts, axis=0)
    mirror = lax.ppermute(
        block, EIG + SPACE, [(e * 16 + s, s * 16 + e) for e in range(16) for s in range(16)]
    )
    (fields,) = call(place_kernel, [((2, NZD, 2, 2, 16, 16), F32)], (block, mirror))
    return fields


def solution(mesh):
    fine = Mesh(mesh.devices.reshape([SIZES[name] for name in EIG + SPACE]), EIG + SPACE)
    return jax.shard_map(
        local,
        mesh=fine,
        in_specs=(
            P(None, EIG, None, None, SPACE, None),
            P(None, None, None, SPACE, None),
            P(),
        ),
        out_specs=P(None, None, None, None, SPACE, EIG),
        check_vma=False,
    )
```

time: 107 us -> 101 us (0.944)
  Pallas kernels: 12.6 us -> 9.78 us
  waiting for transfers between devices: 18.9 us -> 16.1 us
    ppermute x1, waiting for transfers between devices: 9.75 us -> 6.91 us  [local(): above = lax.ppermute(own[0], 'z', [(i, (i - 1) % 8) for i in range(8)])]
    pallas_call x4 -> x5, Pallas kernels: 12.6 us -> 9.78 us  [call(): pl.pallas_call(kernel, out_shape=shapes, in_specs=specs, out_specs=[VMEM]...]
  transfers between devices with their start and end apart: 3 -> 3, of which waited for: 2 -> 2; matrix products, arithmetic and copies ran while one was open for 0% -> 0% of each run, Pallas kernels for 0% -> 3%
where the time goes in v2:
time: 101 us
  blocking collectives  64.8 us (64%)
  waiting for transfers between devices  16.1 us (16%)
  Pallas kernels  9.78 us (10%)
  starting transfers between devices  7.86 us (8%)
  local copies, waits for them, and re-layouts  1.93 us (2%)
    all_to_all x1, blocking collectives, local(): lax.all_to_all(shares, PLANE, split_axis=0, concat_axis=0, tiled=True)  31.2 us
    all_to_all x1, blocking collectives, local(): own = lax.all_to_all(chunks, PLANE, split_axis=0, concat_axis=0, tiled=True)  19.7 us
    all_to_all x1, blocking collectives, local(): parts = lax.all_to_all(parts, 'z', split_axis=0, concat_axis=0, tiled=True)  14 us
    pallas_call x5, Pallas kernels, call(): pl.pallas_call(kernel, out_shape=shapes, in_specs=specs, out_specs=[VMEM]...  9.78 us
    ppermute x1, waiting for transfers between devices, local(): lax.ppermute(block, EIG + SPACE, [(e * 16 + s, s * 16 + e) for e in range...  9.15 us
    ppermute x1, waiting for transfers between devices, local(): above = lax.ppermute(own[0], 'z', [(i, (i - 1) % 8) for i in range(8)])  6.91 us
    ppermute x1, starting transfers between devices, local(): above = lax.ppermute(own[0], 'z', [(i, (i - 1) % 8) for i in range(8)])  5.93 us
  transfers between devices with their start and end apart: 3, of which 2 were waited for; matrix products, arithmetic and copies ran while one was open for 0% of the time, Pallas kernels for 3%

profile of v2, /device:TPU:24, one launch (start us, length us, event | category | flops | bytes accessed | tf_op | source)
XLA Modules:
  0.0 100.5 jit_solution(18228810415704816959)
XLA Ops:
  0.0 0.0 copy-start
  0.0 1.1 %copy-done = f32[2,16,4,3,4,128]{5,4,3,2,1,0:T(4,128)S(1)} copy-done((f32[2,16,4,3,4,128]{5,4,3,2,1,0:T(4,128)S(1)}, f32[2,16,4,3,4,128]{5,4,3,2,1,0:T(4,128)}, u32[]{:S(2)}) %copy-start) | copy-done | bytes 786456
  1.1 0.0 copy-start.1
  1.1 0.8 copy-done.1
  1.9 2.7 %shard_map.37 = f32[16,104,128]{2,1,0:T(8,128)S(1)} custom-call(f32[1536,128]{1,0:T(8,128)S(1)} %bitcast.8, f32[72,128]{1,0:T(8,128)S(1)} %bitcast.9), custom_call_target="tpu_custom_call" | custom-call | bytes 823296 | tf_op jit(solution)/shard_map/pallas_call | solution.py:280
  4.6 19.7 %all_to_all.15 = f32[16,104,128]{2,1,0:T(8,128)S(1)} all-to-all(f32[16,104,128]{2,1,0:T(8,128)S(1)} %shard_map.37), channel_id=1, replica_groups=mesh['ylo'=2,'x'=4,'core'=2,'z'=8,'yhi'=2] {'yhi','ylo','x'}, dimensions={0} | all-to-all | bytes 1703936 | tf_op jit(solution)/shard_map/all_to_all | solution.py:315
  24.3 0.0 collective-permute-start.1
  24.3 5.9 %collective-permute-start = (f32[8,104,128]{2,1,0:T(8,128)S(1)}, f32[8,104,128]{2,1,0:T(8,128)S(1)}, u32[]{:S(2)}, u32[]{:S(2)}) collective-permute-start(f32[8,104,128]{2,1,0:T(8,128)S(1)} %slice.5), channel_id=1, source_target_pairs={{0,14},{2,0},{4,2},{6,4},{8,6},{10,8},{12,10},{14,12},{1,15},{3,1}... | collective-permute-start | bytes 1277960 | tf_op jit(solution)/shard_map/ppermute | solution.py:317
  30.3 0.0 collective-permute-done.1.other_ref
  30.3 2.8 %shard_map.38 = (f32[2,2,512,256]{3,2,1,0:T(8,128)S(1)}, bf16[2,256,384]{2,1,0:T(8,128)(2,1)S(1)}, bf16[2,256,384]{2,1,0:T(8,128)(2,1)S(1)}, bf16[2,256,384]{2,1,0:T(8,128)(2,1)S(1)}, bf16[2,256,384]{2,1,0:T(8,128)(2,1)S(1)}) custom-call(f32[2,8,104,128]{3,2,1,0:T(8,128)S(1)} %bitcast.6, f32[2,8,104,128]{3,2,1,0:T(8,128)S(1)} %collective-permute-done.1.other_ref), custom_call_target="tpu_custom_call" | custom-call | flops 1207959552 | bytes 1703936 | tf_op jit(solution)/shard_map/pallas_call | solution.py:280
  33.1 6.9 %collective-permute-done.above_ref = f32[8,104,128]{2,1,0:T(8,128)S(1)} collective-permute-done((f32[8,104,128]{2,1,0:T(8,128)S(1)}, f32[8,104,128]{2,1,0:T(8,128)S(1)}, u32[]{:S(2)}, u32[]{:S(2)}) %collective-permute-start) | collective-permute-done | bytes 426016 | tf_op jit(solution)/shard_map/ppermute | solution.py:317
  40.0 2.6 %shard_map.39 = f32[2,8,16,16,128]{4,3,2,1,0:T(8,128)S(1)} custom-call(f32[2,8,104,128]{3,2,1,0:T(8,128)S(1)} %bitcast.7, f32[8,104,128]{2,1,0:T(8,128)S(1)} %collective-permute-done.above_ref, f32[2,2,512,256]{3,2,1,0:T(8,128)S(1)} %get-tuple-element.10.sum_ref, bf16[2,256,384]{2,1,0:T(8,128)(2,1)S(1)} %get-tuple-element.11.u0, ...), custom_call_target="tpu_custom_call" | custom-call | flops 1207959552 | bytes 6520832 | tf_op jit(solution)/shard_map/pallas_call | solution.py:280
  42.6 0.0 copy-start.2
  42.6 31.2 %all_to_all.16.shares_ref = f32[16,16,16,128]{3,2,1,0:T(8,128)S(1)} all-to-all(f32[16,16,16,128]{3,2,1,0:T(8,128)S(1)} %bitcast.4), channel_id=1, replica_groups=mesh['ylo'=2,'x'=4,'core'=2,'z'=8,'yhi'=2] {'yhi','ylo','x'}, dimensions={0} | all-to-all | bytes 4194304 | tf_op jit(solution)/shard_map/all_to_all | solution.py:335
  73.7 0.0 copy-done.2
  73.7 0.9 shard_map.40
  74.6 14.0 %all_to_all.17 = f32[8,2,16,128]{3,2,1,0:T(8,128)S(1)} all-to-all(f32[8,2,16,128]{3,2,1,0:T(8,128)S(1)} %shard_map.40), channel_id=1, replica_groups=mesh['ylo'=2,'x'=4,'core'=2,'z'=8,'yhi'=2] {'z'}, dimensions={0} | all-to-all | bytes 262144 | tf_op jit(solution)/shard_map/all_to_all | solution.py:337
  88.6 1.9 %collective-permute-start.2 = (f32[2,16,128]{2,1,0:T(8,128)S(1)}, f32[2,16,128]{2,1,0:T(8,128)S(1)}, u32[]{:S(2)}, u32[]{:S(2)}) collective-permute-start(f32[2,16,128]{2,1,0:T(8,128)S(1)} %reduce_sum.9.own_ref), channel_id=1, source_target_pairs={{0,0},{1,16},{2,32},{3,48},{4,64},{5,80},{6,96},{7,112},{8,128},{9... | collective-permute-start | bytes 49160 | tf_op jit(solution)/shard_map/ppermute | solution.py:339
  90.5 9.1 %collective-permute-done.2.mirror_ref = f32[2,16,128]{2,1,0:T(8,128)S(1)} collective-permute-done((f32[2,16,128]{2,1,0:T(8,128)S(1)}, f32[2,16,128]{2,1,0:T(8,128)S(1)}, u32[]{:S(2)}, u32[]{:S(2)}) %collective-permute-start.2) | collective-permute-done | bytes 16416 | tf_op jit(solution)/shard_map/ppermute | solution.py:339
  99.7 0.9 shard_map.41
  (2 shorter events, 0.0 us)
Async XLA Ops:
  0.0 1.1 %copy-start = (f32[2,16,4,3,4,128]{5,4,3,2,1,0:T(4,128)S(1)}, f32[2,16,4,3,4,128]{5,4,3,2,1,0:T(4,128)}, u32[]{:S(2)}) copy-start(f32[2,16,4,3,4,128]{5,4,3,2,1,0:T(4,128)} %param.3) | copy-start | bytes 2359300
  1.1 0.8 copy-start.1
  24.3 6.0 %collective-permute-start.1 = (f32[2,8,104,128]{3,2,1,0:T(8,128)S(1)}, f32[2,8,104,128]{3,2,1,0:T(8,128)S(1)}, u32[]{:S(2)}, u32[]{:S(2)}) collective-permute-start(f32[2,8,104,128]{3,2,1,0:T(8,128)S(1)} %bitcast.5), channel_id=1, source_target_pairs={{0,16},{16,0},{1,17},{17,1},{2,18},{18,2},{3,19},{19,3},{4,20},{20... | collective-permute-start | bytes 2555912 | tf_op jit(solution)/shard_map/ppermute | solution.py:318
  24.3 15.7 %collective-permute-start = (f32[8,104,128]{2,1,0:T(8,128)S(1)}, f32[8,104,128]{2,1,0:T(8,128)S(1)}, u32[]{:S(2)}, u32[]{:S(2)}) collective-permute-start(f32[8,104,128]{2,1,0:T(8,128)S(1)} %slice.5), channel_id=1, source_target_pairs={{0,14},{2,0},{4,2},{6,4},{8,6},{10,8},{12,10},{14,12},{1,15},{3,1}... | collective-permute-start | bytes 1277960 | tf_op jit(solution)/shard_map/ppermute | solution.py:317
  42.6 31.2 %copy-start.2 = (s32[4]{0:T(128)S(1)}, s32[4]{0:T(128)}, u32[]{:S(2)}) copy-start(s32[4]{0:T(128)} %separations_ref.1) | copy-start | bytes 52
  88.6 11.1 %collective-permute-start.2 = (f32[2,16,128]{2,1,0:T(8,128)S(1)}, f32[2,16,128]{2,1,0:T(8,128)S(1)}, u32[]{:S(2)}, u32[]{:S(2)}) collective-permute-start(f32[2,16,128]{2,1,0:T(8,128)S(1)} %reduce_sum.9.own_ref), channel_id=1, source_target_pairs={{0,0},{1,16},{2,32},{3,48},{4,64},{5,80},{6,96},{7,112},{8,128},{9... | collective-permute-start | bytes 49160 | tf_op jit(solution)/shard_map/ppermute | solution.py:339

commit v3 on v2

--- a/solution.py
+++ b/solution.py
@@ -216,42 +216,49 @@
 
 
 def high_kernel(own_ref, above_ref, sum_ref, u0, u1, u2, u3, out_ref, f_hi, f_lo, link_ref):
+    first_x = lax.axis_index("core") == 0
     multiply_links(own_ref.at[1], above_ref, link_ref)
     transport(own_ref.at[1], above_ref, link_ref, f_hi, f_lo)
     for sign in range(2):
         for part in range(2):
             total = sum_ref[sign, part] + products(sign, part, (u0, u1, u2, u3), f_hi, f_lo)
-            for by in range(NZD):
-                for block in range(8):
-                    for half in range(2):
-                        out_ref[half, block, by * 4 + sign * 2 + part] = total[
+            for block in range(8):
+                for half in range(2):
+                    x, y = block % 4, half * 2 + block // 4
+                    to = jnp.where(first_x, x * 4 + y, y * 4 + x)
+                    for by in range(NZD):
+                        out_ref[to, by * 4 + sign * 2 + part] = total[
                             by * LANES + block * 16 : by * LANES + block * 16 + 16,
                             half * LANES : half * LANES + LANES,
                         ]
 
 
 def gather_kernel(separations_ref, shares_ref, out_ref):
-    fields = []
-    for q in range(NZD):
-        at = separations_ref[q] * 4
-        sums = []
-        for index in range(4):
-            total = shares_ref[0, at + index]
-            for source in range(1, 16):
-                total = total + shares_ref[source, at + index]
-            sums.append(total * 0.5)
-        plus_real, plus_imag, minus_real, minus_imag = sums
-        fields.append(
-            [
-                plus_imag - minus_imag,
-                minus_real - plus_real,
-                plus_real + minus_real,
-                plus_imag + minus_imag,
-            ]
-        )
-    for pair in range(2):
-        for z, value in enumerate(exchange_pieces(fields[2 * pair] + fields[2 * pair + 1])):
-            out_ref[z, pair] = value
+    def one(line, carry):
+        fields = []
+        for q in range(NZD):
+            at = line * 16 + separations_ref[q] * 4
+            sums = []
+            for index in range(4):
+                total = shares_ref[0, at + index]
+                for source in range(1, 4):
+                    total = total + shares_ref[source, at + index]
+                sums.append(total * 0.5)
+            plus_real, plus_imag, minus_real, minus_imag = sums
+            fields.append(
+                [
+                    plus_imag - minus_imag,
+                    minus_real - plus_real,
+                    plus_real + minus_real,
+                    plus_imag + minus_imag,
+                ]
+            )
+        for pair in range(2):
+            for z, value in enumerate(exchange_pieces(fields[2 * pair] + fields[2 * pair + 1])):
+                out_ref[line * 8 + z, pair] = value
+        return carry
+
+    lax.fori_loop(0, 4, one, 0, unroll=4)
 
 
 def place_kernel(own_ref, mirror_ref, out_ref):
@@ -298,6 +305,33 @@
 FIELD_FLOPS = 2 * 2 * 2 * 3 * 512 * 384 * 256
 
 
+def position(x, y, core, z):
+    return (((y % 2 * 4 + x) * 2 + core) * 8 + z) * 2 + y // 2
+
+
+def rings(step, with_z):
+    groups = []
+    for core in range(2):
+        for line in range(4):
+            rows = []
+            for z in range(8):
+                if core == step:
+                    rows.append([position(i, line, core, z) for i in range(4)])
+                else:
+                    rows.append([position(line, i, core, z) for i in range(4)])
+            if with_z:
+                groups.append([row[i] for i in range(4) for row in rows])
+            else:
+                groups.extend(rows)
+    return groups
+
+
+def exchange(value, groups):
+    return lax.all_to_all(
+        value, EIG + SPACE, split_axis=0, concat_axis=0, tiled=True, axis_index_groups=groups
+    )
+
+
 def local(eigenvectors, gauge_links, separations):
     vectors = eigenvectors.reshape(1536, LANES)
     links = gauge_links.reshape(72, LANES)
@@ -310,6 +344,7 @@
             pltpu.VMEM((72, LANES), F32),
             pltpu.SemaphoreType.DMA((5,)),
         ),
+        limit=56,
         space=pl.BlockSpec(memory_space=pltpu.HBM),
     )
     own = lax.all_to_all(chunks, PLANE, split_axis=0, concat_axis=0, tiled=True)
@@ -326,15 +361,14 @@
     )
     (shares,) = call(
         high_kernel,
-        [((2, 8, 16, 16, LANES), F32)],
+        [((16, 16, 16, LANES), F32)],
         (own, above, *low),
         FIELD_SCRATCH,
         flops=FIELD_FLOPS,
     )
-    shares = shares.reshape(16, 16, 16, LANES)
-    shares = lax.all_to_all(shares, PLANE, split_axis=0, concat_axis=0, tiled=True)
-    (parts,) = call(gather_kernel, [((8, 2, 16, LANES), F32)], (separations, shares))
-    parts = lax.all_to_all(parts, "z", split_axis=0, concat_axis=0, tiled=True)
+    shares = exchange(shares.reshape(4, 64, 16, LANES), rings(0, False))
+    (parts,) = call(gather_kernel, [((32, 2, 16, LANES), F32)], (separations, shares))
+    parts = exchange(parts, rings(1, True))
     block = jnp.sum(parts, axis=0)
     mirror = lax.ppermute(
         block, EIG + SPACE, [(e * 16 + s, s * 16 + e) for e in range(16) for s in range(16)]

time: 101 us -> 96.6 us (0.956)
  blocking collectives: 64.8 us -> 59.8 us
  starting transfers between devices: 7.86 us -> 11.1 us
  waiting for transfers between devices: 16.1 us -> 13 us
  local copies, waits for them, and re-layouts: 1.93 us -> 0.03 us
  Pallas kernels: 9.78 us -> 11.4 us
    all_to_all x2, blocking collectives: 45.1 us -> 39.9 us  [exchange(): lax.all_to_all(value, EIG + SPACE, split_axis=0, concat_axis=0, tiled=Tru...]
    ppermute x1, starting transfers between devices: 1.92 us -> 5.17 us  [local(): lax.ppermute(block, EIG + SPACE, [(e * 16 + s, s * 16 + e) for e in range...]
    ppermute x1, waiting for transfers between devices: 9.15 us -> 6.1 us  [local(): lax.ppermute(block, EIG + SPACE, [(e * 16 + s, s * 16 + e) for e in range...]
    unnamed x6 -> x2, local copies, waits for them, and re-layouts: 1.91 us -> 0.01 us
    pallas_call x5, Pallas kernels: 9.78 us -> 11.4 us  [call(): pl.pallas_call(kernel, out_shape=shapes, in_specs=specs, out_specs=[VMEM]...]
where the time goes in v3:
time: 96.6 us; the launch traced here: 95.4 us
  blocking collectives  59.8 us (62%)
  waiting for transfers between devices  13 us (13%)
  Pallas kernels  11.4 us (12%)
  starting transfers between devices  11.1 us (11%)
    all_to_all x2, blocking collectives, exchange(): lax.all_to_all(value, EIG + SPACE, split_axis=0, concat_axis=0, tiled=Tru...  39.9 us
    all_to_all x1, blocking collectives, local(): own = lax.all_to_all(chunks, PLANE, split_axis=0, concat_axis=0, tiled=True)  19.9 us
    pallas_call x5, Pallas kernels, call(): pl.pallas_call(kernel, out_shape=shapes, in_specs=specs, out_specs=[VMEM]...  11.4 us
    ppermute x1, waiting for transfers between devices, local(): above = lax.ppermute(own[0], 'z', [(i, (i - 1) % 8) for i in range(8)])  6.91 us
    ppermute x1, waiting for transfers between devices, local(): lax.ppermute(block, EIG + SPACE, [(e * 16 + s, s * 16 + e) for e in range...  6.1 us
    ppermute x1, starting transfers between devices, local(): above = lax.ppermute(own[0], 'z', [(i, (i - 1) % 8) for i in range(8)])  5.93 us
    ppermute x1, starting transfers between devices, local(): lax.ppermute(block, EIG + SPACE, [(e * 16 + s, s * 16 + e) for e in range...  5.17 us
  transfers between devices with their start and end apart: 3, of which 2 were waited for; matrix products, arithmetic and copies ran while one was open for 0% of the time, Pallas kernels for 3%

profile of v3, /device:TPU:24, one launch (start us, length us, event | category | flops | bytes accessed | tf_op | source)
XLA Modules:
  0.0 95.4 jit_solution(1356511293897968681)
XLA Ops:
  0.0 3.6 %shard_map.37 = f32[16,104,128]{2,1,0:T(8,128)} custom-call(f32[1536,128]{1,0:T(8,128)} %bitcast.8, f32[72,128]{1,0:T(8,128)} %bitcast.9), custom_call_target="tpu_custom_call" | custom-call | bytes 823296 | tf_op jit(solution)/shard_map/pallas_call | solution.py:287
  3.6 19.9 %all_to_all.15 = f32[16,104,128]{2,1,0:T(8,128)S(1)} all-to-all(f32[16,104,128]{2,1,0:T(8,128)} %shard_map.37), channel_id=1, replica_groups=mesh['ylo'=2,'x'=4,'core'=2,'z'=8,'yhi'=2] {'yhi','ylo','x'}, dimensions={0} | all-to-all | bytes 1703936 | tf_op jit(solution)/shard_map/all_to_all | solution.py:350
  23.5 0.0 collective-permute-start.1
  23.5 5.9 %collective-permute-start = (f32[8,104,128]{2,1,0:T(8,128)S(1)}, f32[8,104,128]{2,1,0:T(8,128)S(1)}, u32[]{:S(2)}, u32[]{:S(2)}) collective-permute-start(f32[8,104,128]{2,1,0:T(8,128)S(1)} %slice.5), channel_id=1, source_target_pairs={{0,14},{2,0},{4,2},{6,4},{8,6},{10,8},{12,10},{14,12},{1,15},{3,1}... | collective-permute-start | bytes 1277960 | tf_op jit(solution)/shard_map/ppermute | solution.py:352
  29.5 0.0 collective-permute-done.1.other_ref
  29.5 2.8 %shard_map.38 = (f32[2,2,512,256]{3,2,1,0:T(8,128)S(1)}, bf16[2,256,384]{2,1,0:T(8,128)(2,1)S(1)}, bf16[2,256,384]{2,1,0:T(8,128)(2,1)S(1)}, bf16[2,256,384]{2,1,0:T(8,128)(2,1)S(1)}, bf16[2,256,384]{2,1,0:T(8,128)(2,1)S(1)}) custom-call(f32[2,8,104,128]{3,2,1,0:T(8,128)S(1)} %bitcast.6, f32[2,8,104,128]{3,2,1,0:T(8,128)S(1)} %collective-permute-done.1.other_ref), custom_call_target="tpu_custom_call" | custom-call | flops 1207959552 | bytes 1703936 | tf_op jit(solution)/shard_map/pallas_call | solution.py:287
  32.3 6.9 %collective-permute-done.above_ref = f32[8,104,128]{2,1,0:T(8,128)S(1)} collective-permute-done((f32[8,104,128]{2,1,0:T(8,128)S(1)}, f32[8,104,128]{2,1,0:T(8,128)S(1)}, u32[]{:S(2)}, u32[]{:S(2)}) %collective-permute-start) | collective-permute-done | bytes 426016 | tf_op jit(solution)/shard_map/ppermute | solution.py:352
  39.2 2.5 %shard_map.39 = f32[16,16,16,128]{3,2,1,0:T(8,128)S(1)} custom-call(f32[2,8,104,128]{3,2,1,0:T(8,128)S(1)} %bitcast.7, f32[8,104,128]{2,1,0:T(8,128)S(1)} %collective-permute-done.above_ref, f32[2,2,512,256]{3,2,1,0:T(8,128)S(1)} %get-tuple-element.10.sum_ref, bf16[2,256,384]{2,1,0:T(8,128)(2,1)S(1)} %get-tuple-element.11.u0, ...), custom_call_target="tpu_custom_call" | custom-call | flops 1207959552 | bytes 6520832 | tf_op jit(solution)/shard_map/pallas_call | solution.py:287
  41.8 0.0 copy-start
  41.8 19.0 %all_to_all.16.shares_ref = f32[4,64,16,128]{3,2,1,0:T(8,128)S(1)} all-to-all(f32[4,64,16,128]{3,2,1,0:T(8,128)S(1)} %bitcast.4), channel_id=1, replica_groups={{0,32,64,96},{2,34,66,98},{4,36,68,100},{6,38,70,102},{8,40,72,104},{10..., dimensions={0} | all-to-all | bytes 4194304 | tf_op jit(solution)/shard_map/all_to_all | solution.py:330
  60.8 0.0 copy-done
  60.8 1.6 %shard_map.40 = f32[32,2,16,128]{3,2,1,0:T(8,128)S(1)} custom-call(s32[4]{0:T(128)S(1)} %copy-done, f32[4,64,16,128]{3,2,1,0:T(8,128)S(1)} %all_to_all.16.shares_ref), custom_call_target="tpu_custom_call" | custom-call | bytes 2097168 | tf_op jit(solution)/shard_map/pallas_call | solution.py:287
  62.3 20.9 %all_to_all.17 = f32[32,2,16,128]{3,2,1,0:T(8,128)S(1)} all-to-all(f32[32,2,16,128]{3,2,1,0:T(8,128)S(1)} %shard_map.40), channel_id=1, replica_groups={{0,2,4,6,8,10,12,14,128,130,132,134,136,138,140,142,1,3,5,7,9,11,13,15,..., dimensions={0} | all-to-all | bytes 1048576 | tf_op jit(solution)/shard_map/all_to_all | solution.py:330
  83.2 5.2 %collective-permute-start.2 = (f32[2,16,128]{2,1,0:T(8,128)S(1)}, f32[2,16,128]{2,1,0:T(8,128)S(1)}, u32[]{:S(2)}, u32[]{:S(2)}) collective-permute-start(f32[2,16,128]{2,1,0:T(8,128)S(1)} %reduce_sum.9.own_ref), channel_id=1, source_target_pairs={{0,0},{1,16},{2,32},{3,48},{4,64},{5,80},{6,96},{7,112},{8,128},{9... | collective-permute-start | bytes 49160 | tf_op jit(solution)/shard_map/ppermute | solution.py:373
  88.4 6.1 %collective-permute-done.2.mirror_ref = f32[2,16,128]{2,1,0:T(8,128)S(1)} collective-permute-done((f32[2,16,128]{2,1,0:T(8,128)S(1)}, f32[2,16,128]{2,1,0:T(8,128)S(1)}, u32[]{:S(2)}, u32[]{:S(2)}) %collective-permute-start.2) | collective-permute-done | bytes 16416 | tf_op jit(solution)/shard_map/ppermute | solution.py:373
  94.5 0.9 shard_map.41
  (2 shorter events, 0.1 us)
Async XLA Ops:
  23.5 6.0 %collective-permute-start.1 = (f32[2,8,104,128]{3,2,1,0:T(8,128)S(1)}, f32[2,8,104,128]{3,2,1,0:T(8,128)S(1)}, u32[]{:S(2)}, u32[]{:S(2)}) collective-permute-start(f32[2,8,104,128]{3,2,1,0:T(8,128)S(1)} %bitcast.5), channel_id=1, source_target_pairs={{0,16},{16,0},{1,17},{17,1},{2,18},{18,2},{3,19},{19,3},{4,20},{20... | collective-permute-start | bytes 2555912 | tf_op jit(solution)/shard_map/ppermute | solution.py:353
  23.5 15.7 %collective-permute-start = (f32[8,104,128]{2,1,0:T(8,128)S(1)}, f32[8,104,128]{2,1,0:T(8,128)S(1)}, u32[]{:S(2)}, u32[]{:S(2)}) collective-permute-start(f32[8,104,128]{2,1,0:T(8,128)S(1)} %slice.5), channel_id=1, source_target_pairs={{0,14},{2,0},{4,2},{6,4},{8,6},{10,8},{12,10},{14,12},{1,15},{3,1}... | collective-permute-start | bytes 1277960 | tf_op jit(solution)/shard_map/ppermute | solution.py:352
  41.8 19.0 %copy-start = (s32[4]{0:T(128)S(1)}, s32[4]{0:T(128)}, u32[]{:S(2)}) copy-start(s32[4]{0:T(128)} %separations_ref.1) | copy-start | bytes 52
  83.2 11.3 %collective-permute-start.2 = (f32[2,16,128]{2,1,0:T(8,128)S(1)}, f32[2,16,128]{2,1,0:T(8,128)S(1)}, u32[]{:S(2)}, u32[]{:S(2)}) collective-permute-start(f32[2,16,128]{2,1,0:T(8,128)S(1)} %reduce_sum.9.own_ref), channel_id=1, source_target_pairs={{0,0},{1,16},{2,32},{3,48},{4,64},{5,80},{6,96},{7,112},{8,128},{9... | collective-permute-start | bytes 49160 | tf_op jit(solution)/shard_map/ppermute | solution.py:373

commit v4 on v3

--- a/solution.py
+++ b/solution.py
@@ -142,9 +142,9 @@
                 link_ref[at + 1 : at + 2, :] = factors[i][j][1]
 
 
-def transport(here_ref, above_ref, link_ref, hi_ref, lo_ref):
+def transport(sign, here_ref, above_ref, link_ref, hi_ref, lo_ref):
     def one_block(block, carry):
-        for sign in range(2):
+        for _ in range(1):
             here, above, here_swapped, above_swapped = [], [], [], []
             for c in range(3):
                 first = (sign * 3 + c) * 16
@@ -168,8 +168,8 @@
                         )
                         total = term if total is None else total + term
                     hi, lo = split(total)
-                    hi_ref[sign, rows, i * LANES : i * LANES + LANES] = hi
-                    lo_ref[sign, rows, i * LANES : i * LANES + LANES] = lo
+                    hi_ref[rows, i * LANES : i * LANES + LANES] = hi
+                    lo_ref[rows, i * LANES : i * LANES + LANES] = lo
         return carry
 
     lax.fori_loop(0, 8, one_block, 0, unroll=8)
@@ -195,33 +195,34 @@
         )
 
     rows_hi, rows_lo = rows[2 * part][1 - sign], rows[2 * part + 1][1 - sign]
-    total = product_of(hi_ref[sign], rows_hi)
-    total = total + product_of(hi_ref[sign], rows_lo)
-    return total + product_of(lo_ref[sign], rows_hi)
+    both = jnp.concatenate([hi_ref[...], lo_ref[...]], axis=1)
+    return product_of(both, jnp.concatenate([rows_hi, rows_hi], axis=1)) + product_of(
+        hi_ref[...], rows_lo
+    )
 
 
 def low_kernel(
-    own_ref, other_ref, sum_ref, u0, u1, u2, u3, d0, d1, d2, d3, f_hi, f_lo, link_ref
+    own_ref, other_ref, sum_ref, u0, u1, u2, u3, d0, d1, d2, d3, h0, l0, h1, l1, link_ref
 ):
     cls = lax.axis_index("core")
     down, up = (d0, d1, d2, d3), (u0, u1, u2, u3)
     multiply_links(own_ref.at[0], own_ref.at[1], link_ref)
-    transport(own_ref.at[0], own_ref.at[1], link_ref, f_hi, f_lo)
     for source, start in ((own_ref, cls * LANES), (other_ref, (1 - cls) * LANES)):
         prepare_rows(source, 0, start, down)
         prepare_rows(source, 1, start, up)
-    for sign in range(2):
+    for sign, (hi_ref, lo_ref) in enumerate(((h0, l0), (h1, l1))):
+        transport(sign, own_ref.at[0], own_ref.at[1], link_ref, hi_ref, lo_ref)
         for part in range(2):
-            sum_ref[sign, part] = products(sign, part, down, f_hi, f_lo)
-
-
-def high_kernel(own_ref, above_ref, sum_ref, u0, u1, u2, u3, out_ref, f_hi, f_lo, link_ref):
+            sum_ref[sign, part] = products(sign, part, down, hi_ref, lo_ref)
+
+
+def high_kernel(own_ref, above_ref, sum_ref, u0, u1, u2, u3, out_ref, h0, l0, h1, l1, link_ref):
     first_x = lax.axis_index("core") == 0
     multiply_links(own_ref.at[1], above_ref, link_ref)
-    transport(own_ref.at[1], above_ref, link_ref, f_hi, f_lo)
-    for sign in range(2):
+    for sign, (hi_ref, lo_ref) in enumerate(((h0, l0), (h1, l1))):
+        transport(sign, own_ref.at[1], above_ref, link_ref, hi_ref, lo_ref)
         for part in range(2):
-            total = sum_ref[sign, part] + products(sign, part, (u0, u1, u2, u3), f_hi, f_lo)
+            total = sum_ref[sign, part] + products(sign, part, (u0, u1, u2, u3), hi_ref, lo_ref)
             for block in range(8):
                 for half in range(2):
                     x, y = block % 4, half * 2 + block // 4
@@ -254,8 +255,9 @@
                 ]
             )
         for pair in range(2):
-            for z, value in enumerate(exchange_pieces(fields[2 * pair] + fields[2 * pair + 1])):
-                out_ref[line * 8 + z, pair] = value
+            turned = jnp.concatenate(fields[2 * pair] + fields[2 * pair + 1]).T
+            for z in range(8):
+                out_ref[line * 8 + z, pair] = turned[z * 16 : z * 16 + 16]
         return carry
 
     lax.fori_loop(0, 4, one, 0, unroll=4)
@@ -263,16 +265,14 @@
 
 def place_kernel(own_ref, mirror_ref, out_ref):
     padding = jnp.zeros((LANES - 32, LANES), jnp.float32)
-    turned = jnp.concatenate([own_ref[0], own_ref[1], padding]).T
+    turned = jnp.concatenate([mirror_ref[0], mirror_ref[1], padding]).T
     for pair in range(2):
         for index in range(8):
             q = pair * 2 + index // 4
             g = (index // 2) % 2
             part = index % 2
-            out_ref[0, q, g, part] = turned[
-                index * 16 : index * 16 + 16, pair * 16 : pair * 16 + 16
-            ]
-            value = mirror_ref[pair, :, index * 16 : index * 16 + 16]
+            out_ref[0, q, g, part] = own_ref[pair, :, index * 16 : index * 16 + 16]
+            value = turned[index * 16 : index * 16 + 16, pair * 16 : pair * 16 + 16]
             out_ref[1, q, g, part] = -value if part else value
 
 
@@ -297,8 +297,10 @@
 
 F32, B16 = jnp.float32, jnp.bfloat16
 FIELD_SCRATCH = (
-    pltpu.VMEM((2, 512, 384), B16),
-    pltpu.VMEM((2, 512, 384), B16),
+    pltpu.VMEM((512, 384), B16),
+    pltpu.VMEM((512, 384), B16),
+    pltpu.VMEM((512, 384), B16),
+    pltpu.VMEM((512, 384), B16),
     pltpu.VMEM((72, LANES), F32),
 )
 LOW_SCRATCH = (pltpu.VMEM((2, 256, 384), B16),) * 4 + FIELD_SCRATCH

time: 96.6 us -> 95.6 us (0.990)
  Pallas kernels: 11.4 us -> 10.1 us
    pallas_call x5, Pallas kernels: 11.4 us -> 10.1 us  [call(): pl.pallas_call(kernel, out_shape=shapes, in_specs=specs, out_specs=[VMEM]...]
where the time goes in v4:
time: 95.6 us; the launch traced here: 94.4 us
  blocking collectives  59.8 us (63%)
  waiting for transfers between devices  13.2 us (14%)
  starting transfers between devices  11.1 us (12%)
  Pallas kernels  10.1 us (11%)
    all_to_all x2, blocking collectives, exchange(): lax.all_to_all(value, EIG + SPACE, split_axis=0, concat_axis=0, tiled=Tru...  39.9 us
    all_to_all x1, blocking collectives, local(): own = lax.all_to_all(chunks, PLANE, split_axis=0, concat_axis=0, tiled=True)  19.9 us
    pallas_call x5, Pallas kernels, call(): pl.pallas_call(kernel, out_shape=shapes, in_specs=specs, out_specs=[VMEM]...  10.1 us
    ppermute x1, waiting for transfers between devices, local(): above = lax.ppermute(own[0], 'z', [(i, (i - 1) % 8) for i in range(8)])  7.11 us
    ppermute x1, waiting for transfers between devices, local(): lax.ppermute(block, EIG + SPACE, [(e * 16 + s, s * 16 + e) for e in range...  6.1 us
    ppermute x1, starting transfers between devices, local(): above = lax.ppermute(own[0], 'z', [(i, (i - 1) % 8) for i in range(8)])  5.93 us
    ppermute x1, starting transfers between devices, local(): lax.ppermute(block, EIG + SPACE, [(e * 16 + s, s * 16 + e) for e in range...  5.17 us
  transfers between devices with their start and end apart: 3, of which 2 were waited for; matrix products, arithmetic and copies ran while one was open for 0% of the time, Pallas kernels for 3%

profile of v4, /device:TPU:24, one launch (start us, length us, event | category | flops | bytes accessed | tf_op | source)
XLA Modules:
  0.0 94.4 jit_solution(9238193107074754022)
XLA Ops:
  0.0 3.6 %shard_map.37 = f32[16,104,128]{2,1,0:T(8,128)} custom-call(f32[1536,128]{1,0:T(8,128)} %bitcast.8, f32[72,128]{1,0:T(8,128)} %bitcast.9), custom_call_target="tpu_custom_call" | custom-call | bytes 823296 | tf_op jit(solution)/shard_map/pallas_call | solution.py:287
  3.6 19.9 %all_to_all.15 = f32[16,104,128]{2,1,0:T(8,128)S(1)} all-to-all(f32[16,104,128]{2,1,0:T(8,128)} %shard_map.37), channel_id=1, replica_groups=mesh['ylo'=2,'x'=4,'core'=2,'z'=8,'yhi'=2] {'yhi','ylo','x'}, dimensions={0} | all-to-all | bytes 1703936 | tf_op jit(solution)/shard_map/all_to_all | solution.py:352
  23.5 0.0 collective-permute-start.1
  23.5 5.9 %collective-permute-start = (f32[8,104,128]{2,1,0:T(8,128)S(1)}, f32[8,104,128]{2,1,0:T(8,128)S(1)}, u32[]{:S(2)}, u32[]{:S(2)}) collective-permute-start(f32[8,104,128]{2,1,0:T(8,128)S(1)} %slice.5), channel_id=1, source_target_pairs={{0,14},{2,0},{4,2},{6,4},{8,6},{10,8},{12,10},{14,12},{1,15},{3,1}... | collective-permute-start | bytes 1277960 | tf_op jit(solution)/shard_map/ppermute | solution.py:354
  29.5 0.0 collective-permute-done.1.other_ref
  29.5 2.6 %shard_map.38 = (f32[2,2,512,256]{3,2,1,0:T(8,128)S(1)}, bf16[2,256,384]{2,1,0:T(8,128)(2,1)S(1)}, bf16[2,256,384]{2,1,0:T(8,128)(2,1)S(1)}, bf16[2,256,384]{2,1,0:T(8,128)(2,1)S(1)}, bf16[2,256,384]{2,1,0:T(8,128)(2,1)S(1)}) custom-call(f32[2,8,104,128]{3,2,1,0:T(8,128)S(1)} %bitcast.6, f32[2,8,104,128]{3,2,1,0:T(8,128)S(1)} %collective-permute-done.1.other_ref), custom_call_target="tpu_custom_call" | custom-call | flops 1207959552 | bytes 1703936 | tf_op jit(solution)/shard_map/pallas_call | solution.py:287
  32.1 7.1 %collective-permute-done.above_ref = f32[8,104,128]{2,1,0:T(8,128)S(1)} collective-permute-done((f32[8,104,128]{2,1,0:T(8,128)S(1)}, f32[8,104,128]{2,1,0:T(8,128)S(1)}, u32[]{:S(2)}, u32[]{:S(2)}) %collective-permute-start) | collective-permute-done | bytes 426016 | tf_op jit(solution)/shard_map/ppermute | solution.py:354
  39.2 2.3 %shard_map.39 = f32[16,16,16,128]{3,2,1,0:T(8,128)S(1)} custom-call(f32[2,8,104,128]{3,2,1,0:T(8,128)S(1)} %bitcast.7, f32[8,104,128]{2,1,0:T(8,128)S(1)} %collective-permute-done.above_ref, f32[2,2,512,256]{3,2,1,0:T(8,128)S(1)} %get-tuple-element.10.sum_ref, bf16[2,256,384]{2,1,0:T(8,128)(2,1)S(1)} %get-tuple-element.11.u0, ...), custom_call_target="tpu_custom_call" | custom-call | flops 1207959552 | bytes 6520832 | tf_op jit(solution)/shard_map/pallas_call | solution.py:287
  41.6 0.0 copy-start
  41.6 19.0 %all_to_all.16.shares_ref = f32[4,64,16,128]{3,2,1,0:T(8,128)S(1)} all-to-all(f32[4,64,16,128]{3,2,1,0:T(8,128)S(1)} %bitcast.4), channel_id=1, replica_groups={{0,32,64,96},{2,34,66,98},{4,36,68,100},{6,38,70,102},{8,40,72,104},{10..., dimensions={0} | all-to-all | bytes 4194304 | tf_op jit(solution)/shard_map/all_to_all | solution.py:332
  60.5 0.0 copy-done
  60.5 0.8 shard_map.40
  61.3 20.9 %all_to_all.17 = f32[32,2,16,128]{3,2,1,0:T(8,128)S(1)} all-to-all(f32[32,2,16,128]{3,2,1,0:T(8,128)S(1)} %shard_map.40), channel_id=1, replica_groups={{0,2,4,6,8,10,12,14,128,130,132,134,136,138,140,142,1,3,5,7,9,11,13,15,..., dimensions={0} | all-to-all | bytes 1048576 | tf_op jit(solution)/shard_map/all_to_all | solution.py:332
  82.2 5.2 %collective-permute-start.2 = (f32[2,16,128]{2,1,0:T(8,128)S(1)}, f32[2,16,128]{2,1,0:T(8,128)S(1)}, u32[]{:S(2)}, u32[]{:S(2)}) collective-permute-start(f32[2,16,128]{2,1,0:T(8,128)S(1)} %reduce_sum.9.own_ref), channel_id=1, source_target_pairs={{0,0},{1,16},{2,32},{3,48},{4,64},{5,80},{6,96},{7,112},{8,128},{9... | collective-permute-start | bytes 49160 | tf_op jit(solution)/shard_map/ppermute | solution.py:375
  87.4 6.1 %collective-permute-done.2.mirror_ref = f32[2,16,128]{2,1,0:T(8,128)S(1)} collective-permute-done((f32[2,16,128]{2,1,0:T(8,128)S(1)}, f32[2,16,128]{2,1,0:T(8,128)S(1)}, u32[]{:S(2)}, u32[]{:S(2)}) %collective-permute-start.2) | collective-permute-done | bytes 16416 | tf_op jit(solution)/shard_map/ppermute | solution.py:375
  93.5 0.9 shard_map.41
  (2 shorter events, 0.1 us)
Async XLA Ops:
  23.5 6.0 %collective-permute-start.1 = (f32[2,8,104,128]{3,2,1,0:T(8,128)S(1)}, f32[2,8,104,128]{3,2,1,0:T(8,128)S(1)}, u32[]{:S(2)}, u32[]{:S(2)}) collective-permute-start(f32[2,8,104,128]{3,2,1,0:T(8,128)S(1)} %bitcast.5), channel_id=1, source_target_pairs={{0,16},{16,0},{1,17},{17,1},{2,18},{18,2},{3,19},{19,3},{4,20},{20... | collective-permute-start | bytes 2555912 | tf_op jit(solution)/shard_map/ppermute | solution.py:355
  23.5 15.7 %collective-permute-start = (f32[8,104,128]{2,1,0:T(8,128)S(1)}, f32[8,104,128]{2,1,0:T(8,128)S(1)}, u32[]{:S(2)}, u32[]{:S(2)}) collective-permute-start(f32[8,104,128]{2,1,0:T(8,128)S(1)} %slice.5), channel_id=1, source_target_pairs={{0,14},{2,0},{4,2},{6,4},{8,6},{10,8},{12,10},{14,12},{1,15},{3,1}... | collective-permute-start | bytes 1277960 | tf_op jit(solution)/shard_map/ppermute | solution.py:354
  41.6 19.0 %copy-start = (s32[4]{0:T(128)S(1)}, s32[4]{0:T(128)}, u32[]{:S(2)}) copy-start(s32[4]{0:T(128)} %separations_ref.1) | copy-start | bytes 52
  82.2 11.3 %collective-permute-start.2 = (f32[2,16,128]{2,1,0:T(8,128)S(1)}, f32[2,16,128]{2,1,0:T(8,128)S(1)}, u32[]{:S(2)}, u32[]{:S(2)}) collective-permute-start(f32[2,16,128]{2,1,0:T(8,128)S(1)} %reduce_sum.9.own_ref), channel_id=1, source_target_pairs={{0,0},{1,16},{2,32},{3,48},{4,64},{5,80},{6,96},{7,112},{8,128},{9... | collective-permute-start | bytes 49160 | tf_op jit(solution)/shard_map/ppermute | solution.py:375

commit v5 on v4

--- a/solution.py
+++ b/solution.py
@@ -1,3 +1,5 @@
+import functools
+
 import jax
 import jax.numpy as jnp
 from jax import lax
@@ -14,6 +16,8 @@
 LANES = 128
 PIECE = 16
 ROWS = 104
+FIRST = (0, 56)
+LINK_ROW = 48
 
 
 def roll(value, by):
@@ -68,7 +72,7 @@
                 both = [jnp.stack(pair) for pair in zip(plus, minus)]
                 for block, value in enumerate(exchange_pieces(both)):
                     for sign in range(2):
-                        first = (sign * 3 + colour) * 16 + half * 8
+                        first = FIRST[sign] + colour * 16 + half * 8
                         out_ref[j * 8 + block, first : first + 8, :] = value[sign]
     copies[4].wait()
     own = lax.axis_index(("ylo", "x"))
@@ -80,8 +84,8 @@
             last = links_ref[(part * 9 + 8) * 4 + plane : (part * 9 + 8) * 4 + plane + 1, :]
             rows.append(jnp.where(row == 0, mine, last))
     for block, value in enumerate(exchange_pieces(rows)):
-        out_ref[block, 96:104, :] = value
-        out_ref[8 + block, 96:104, :] = value
+        out_ref[block, LINK_ROW : LINK_ROW + 8, :] = value
+        out_ref[8 + block, LINK_ROW : LINK_ROW + 8, :] = value
 
 
 def shifted(here, here_swapped, above, above_swapped, by):
@@ -106,7 +110,8 @@
 
 
 def link_rows(source):
-    entries = [source[i, 96:97, :] for i in range(8)] + [source[0, 97:98, :]]
+    entries = [source[i, LINK_ROW : LINK_ROW + 1, :] for i in range(8)]
+    entries.append(source[0, LINK_ROW + 1 : LINK_ROW + 2, :])
     return [[entries[3 * i + j] for j in range(3)] for i in range(3)]
 
 
@@ -142,34 +147,31 @@
                 link_ref[at + 1 : at + 2, :] = factors[i][j][1]
 
 
-def transport(sign, here_ref, above_ref, link_ref, hi_ref, lo_ref):
+def transport(here_ref, above_ref, link_ref, hi_ref, lo_ref):
     def one_block(block, carry):
-        for _ in range(1):
-            here, above, here_swapped, above_swapped = [], [], [], []
-            for c in range(3):
-                first = (sign * 3 + c) * 16
-                here.append(here_ref[block, first : first + 16, :])
-                above.append(above_ref[block, first : first + 16, :])
-                here_swapped.append(roll(here[c], 64))
-                above_swapped.append(roll(above[c], 64))
-            for by in range(1, NZD + 1):
-                rows = pl.ds(pl.multiple_of((by - 1) * LANES + block * 16, 16), 16)
-                moved = [
-                    shifted(here[c], here_swapped[c], above[c], above_swapped[c], by)
-                    for c in range(3)
-                ]
-                for i in range(3):
-                    total = None
-                    for j in range(3):
-                        at = ((by - 1) * 9 + i * 3 + j) * 2
-                        term = (
-                            link_ref[at : at + 1, :] * moved[j][0]
-                            + link_ref[at + 1 : at + 2, :] * moved[j][1]
-                        )
-                        total = term if total is None else total + term
-                    hi, lo = split(total)
-                    hi_ref[rows, i * LANES : i * LANES + LANES] = hi
-                    lo_ref[rows, i * LANES : i * LANES + LANES] = lo
+        here, above, here_swapped, above_swapped = [], [], [], []
+        for c in range(3):
+            here.append(here_ref[block, c * 16 : c * 16 + 16, :])
+            above.append(above_ref[block, c * 16 : c * 16 + 16, :])
+            here_swapped.append(roll(here[c], 64))
+            above_swapped.append(roll(above[c], 64))
+        for by in range(1, NZD + 1):
+            rows = pl.ds(pl.multiple_of((by - 1) * LANES + block * 16, 16), 16)
+            moved = [
+                shifted(here[c], here_swapped[c], above[c], above_swapped[c], by) for c in range(3)
+            ]
+            for i in range(3):
+                total = None
+                for j in range(3):
+                    at = ((by - 1) * 9 + i * 3 + j) * 2
+                    term = (
+                        link_ref[at : at + 1, :] * moved[j][0]
+                        + link_ref[at + 1 : at + 2, :] * moved[j][1]
+                    )
+                    total = term if total is None else total + term
+                hi, lo = split(total)
+                hi_ref[rows, i * LANES : i * LANES + LANES] = hi
+                lo_ref[rows, i * LANES : i * LANES + LANES] = lo
         return carry
 
     lax.fori_loop(0, 8, one_block, 0, unroll=8)
@@ -179,7 +181,7 @@
     start = pl.multiple_of(start, LANES)
     for sign in range(2):
         for colour in range(3):
-            first = (sign * 3 + colour) * 16
+            first = FIRST[sign] + colour * 16
             value = source[half, :, first : first + 16, :].reshape(LANES, LANES)
             swapped = roll(value, 64)
             turned = jnp.where(lanes_of(value) < 64, -swapped, swapped)
@@ -201,50 +203,69 @@
     )
 
 
-def low_kernel(
-    own_ref, other_ref, sum_ref, u0, u1, u2, u3, d0, d1, d2, d3, h0, l0, h1, l1, link_ref
-):
+def low_kernel(own_ref, other_ref, *refs):
+    sum_refs, up, down, (hi_ref, lo_ref, link_ref) = refs[:2], refs[2:6], refs[6:10], refs[10:]
     cls = lax.axis_index("core")
-    down, up = (d0, d1, d2, d3), (u0, u1, u2, u3)
     multiply_links(own_ref.at[0], own_ref.at[1], link_ref)
     for source, start in ((own_ref, cls * LANES), (other_ref, (1 - cls) * LANES)):
         prepare_rows(source, 0, start, down)
         prepare_rows(source, 1, start, up)
-    for sign, (hi_ref, lo_ref) in enumerate(((h0, l0), (h1, l1))):
-        transport(sign, own_ref.at[0], own_ref.at[1], link_ref, hi_ref, lo_ref)
+    for sign in range(2):
+        mine = pl.ds(FIRST[sign], 48)
+        transport(
+            own_ref.at[0, :, mine], own_ref.at[1, :, mine], link_ref, hi_ref.at[sign], lo_ref.at[sign]
+        )
         for part in range(2):
-            sum_ref[sign, part] = products(sign, part, down, hi_ref, lo_ref)
-
-
-def high_kernel(own_ref, above_ref, sum_ref, u0, u1, u2, u3, out_ref, h0, l0, h1, l1, link_ref):
+            sum_refs[sign][part] = products(sign, part, down, hi_ref.at[sign], lo_ref.at[sign])
+
+
+def high_kernel(sign, own_ref, above_ref, *refs):
+    if sign == 0:
+        sum_ref, *up, out_ref, link_ref, hi_ref, lo_ref = refs
+        multiply_links(own_ref.at[1], above_ref, link_ref)
+    else:
+        link_ref, sum_ref, *up, out_ref, hi_ref, lo_ref = refs
     first_x = lax.axis_index("core") == 0
-    multiply_links(own_ref.at[1], above_ref, link_ref)
-    for sign, (hi_ref, lo_ref) in enumerate(((h0, l0), (h1, l1))):
-        transport(sign, own_ref.at[1], above_ref, link_ref, hi_ref, lo_ref)
-        for part in range(2):
-            total = sum_ref[sign, part] + products(sign, part, (u0, u1, u2, u3), hi_ref, lo_ref)
-            for block in range(8):
-                for half in range(2):
-                    x, y = block % 4, half * 2 + block // 4
-                    to = jnp.where(first_x, x * 4 + y, y * 4 + x)
-                    for by in range(NZD):
-                        out_ref[to, by * 4 + sign * 2 + part] = total[
-                            by * LANES + block * 16 : by * LANES + block * 16 + 16,
-                            half * LANES : half * LANES + LANES,
-                        ]
-
-
-def gather_kernel(separations_ref, shares_ref, out_ref):
+    own_x, own_y = lax.axis_index("x"), lax.axis_index(("yhi", "ylo"))
+    transport(own_ref.at[1, :, pl.ds(FIRST[sign], 48)], above_ref, link_ref, hi_ref, lo_ref)
+    for part in range(2):
+        total = sum_ref[part] + products(sign, part, up, hi_ref, lo_ref)
+        for block in range(8):
+            for half in range(2):
+                x, y = block % 4, half * 2 + block // 4
+                to = jnp.where(
+                    first_x, lax.rem(x + 4 - own_x, 4) * 4 + y, lax.rem(y + 4 - own_y, 4) * 4 + x
+                )
+                for by in range(NZD):
+                    out_ref[to, by * 2 + part] = total[
+                        by * LANES + block * 16 : by * LANES + block * 16 + 16,
+                        half * LANES : half * LANES + LANES,
+                    ]
+
+
+def add_kernel(*refs):
+    *share_refs, out_ref = refs
+    for index in range(32):
+        total = share_refs[0][index]
+        for share_ref in share_refs[1:]:
+            total = total + share_ref[index]
+        out_ref[index] = total
+
+
+def gather_kernel(separations_ref, *refs):
+    share_refs, out_ref = (refs[:1], refs[1:5]), refs[5]
+
     def one(line, carry):
         fields = []
         for q in range(NZD):
-            at = line * 16 + separations_ref[q] * 4
+            at = line * 8 + separations_ref[q] * 2
             sums = []
-            for index in range(4):
-                total = shares_ref[0, at + index]
-                for source in range(1, 4):
-                    total = total + shares_ref[source, at + index]
-                sums.append(total * 0.5)
+            for sign in range(2):
+                for part in range(2):
+                    total = share_refs[sign][0][at + part]
+                    for share_ref in share_refs[sign][1:]:
+                        total = total + share_ref[at + part]
+                    sums.append(total * 0.5)
             plus_real, plus_imag, minus_real, minus_imag = sums
             fields.append(
                 [
@@ -296,14 +317,7 @@
 
 
 F32, B16 = jnp.float32, jnp.bfloat16
-FIELD_SCRATCH = (
-    pltpu.VMEM((512, 384), B16),
-    pltpu.VMEM((512, 384), B16),
-    pltpu.VMEM((512, 384), B16),
-    pltpu.VMEM((512, 384), B16),
-    pltpu.VMEM((72, LANES), F32),
-)
-LOW_SCRATCH = (pltpu.VMEM((2, 256, 384), B16),) * 4 + FIELD_SCRATCH
+LINK_SHAPE = ((72, LANES), F32)
 FIELD_FLOPS = 2 * 2 * 2 * 3 * 512 * 384 * 256
 
 
@@ -311,21 +325,29 @@
     return (((y % 2 * 4 + x) * 2 + core) * 8 + z) * 2 + y // 2
 
 
-def rings(step, with_z):
+def second_groups():
     groups = []
-    for core in range(2):
+    for line in range(4):
+        members = [(i, z) for i in range(4) for z in range(8)]
+        groups.append([position(line, i, 0, z) for i, z in members])
+        groups.append([position(i, line, 1, z) for i, z in members])
+    return groups
+
+
+def first_shift(value, by):
+    pairs = []
+    for z in range(8):
         for line in range(4):
-            rows = []
-            for z in range(8):
-                if core == step:
-                    rows.append([position(i, line, core, z) for i in range(4)])
-                else:
-                    rows.append([position(line, i, core, z) for i in range(4)])
-            if with_z:
-                groups.append([row[i] for i in range(4) for row in rows])
-            else:
-                groups.extend(rows)
-    return groups
+            for i in range(4):
+                to = (i + by) % 4
+                pairs.append((position(i, line, 0, z), position(to, line, 0, z)))
+                pairs.append((position(line, i, 1, z), position(line, to, 1, z)))
+    return lax.ppermute(value, EIG + SPACE, pairs)
+
+
+def along_first_ring(shares):
+    shares = shares.reshape(4, 32, 16, LANES)
+    return [shares[0]] + [first_shift(shares[by], by) for by in (2, 1, 3)]
 
 
 def exchange(value, groups):
@@ -351,26 +373,42 @@
     )
     own = lax.all_to_all(chunks, PLANE, split_axis=0, concat_axis=0, tiled=True)
     own = own.reshape(2, 8, ROWS, LANES)
-    above = lax.ppermute(own[0], "z", [(i, (i - 1) % 8) for i in range(8)])
+
+    def from_above(value):
+        return lax.ppermute(value, "z", [(i, (i - 1) % 8) for i in range(8)])
+
+    above = [from_above(own[0, :, : FIRST[1]]), from_above(own[0, :, FIRST[1] :])]
     other = lax.ppermute(own, "core", [(0, 1), (1, 0)])
-
-    low = call(
+    plus, minus, *rows = call(
         low_kernel,
-        [((2, 2, 512, 256), F32)] + [((2, 256, 384), B16)] * 4,
+        [((2, 512, 256), F32)] * 2 + [((2, 256, 384), B16)] * 4,
         (own, other),
-        LOW_SCRATCH,
+        [pltpu.VMEM((2, 256, 384), B16)] * 4
+        + [pltpu.VMEM((2, 512, 384), B16)] * 2
+        + [pltpu.VMEM(*LINK_SHAPE)],
         flops=FIELD_FLOPS,
     )
+    half_scratch = [pltpu.VMEM((512, 384), B16)] * 2
+    shares, links = call(
+        functools.partial(high_kernel, 0),
+        [((16, 8, 16, LANES), F32), LINK_SHAPE],
+        (own, above[0], plus, *rows),
+        half_scratch,
+        flops=FIELD_FLOPS // 2,
+    )
+    (summed,) = call(
+        add_kernel, [((32, 16, LANES), F32)], along_first_ring(shares), flops=4 * FIELD_FLOPS
+    )
     (shares,) = call(
-        high_kernel,
-        [((16, 16, 16, LANES), F32)],
-        (own, above, *low),
-        FIELD_SCRATCH,
-        flops=FIELD_FLOPS,
-    )
-    shares = exchange(shares.reshape(4, 64, 16, LANES), rings(0, False))
-    (parts,) = call(gather_kernel, [((32, 2, 16, LANES), F32)], (separations, shares))
-    parts = exchange(parts, rings(1, True))
+        functools.partial(high_kernel, 1),
+        [((16, 8, 16, LANES), F32)],
+        (own, above[1], links, minus, *rows),
+        half_scratch,
+        flops=FIELD_FLOPS // 2,
+    )
+    summands = [summed] + along_first_ring(shares)
+    (parts,) = call(gather_kernel, [((32, 2, 16, LANES), F32)], (separations, *summands))
+    parts = exchange(parts, second_groups())
     block = jnp.sum(parts, axis=0)
     mirror = lax.ppermute(
         block, EIG + SPACE, [(e * 16 + s, s * 16 + e) for e in range(16) for s in range(16)]

time: 95.6 us -> 88.9 us (0.930)
  blocking collectives: 59.8 us -> 40.3 us
  starting transfers between devices: 11.1 us -> 20.7 us
  waiting for transfers between devices: 13.2 us -> 14.9 us
    all_to_all x2 -> x1, blocking collectives: 39.9 us -> 20.4 us  [exchange(): lax.all_to_all(value, EIG + SPACE, split_axis=0, concat_axis=0, tiled=Tru...]
    ppermute x1 -> x8, starting transfers between devices: 5.93 us -> 15.6 us  [the longest x6 8.63 us: first_shift(): return lax.ppermute(value, EIG + SPACE, pairs)]
    ppermute x1 -> x8, waiting for transfers between devices: 7.11 us -> 8.73 us  [the longest x6 6.54 us: first_shift(): return lax.ppermute(value, EIG + SPACE, pairs)]
    pallas_call x5 -> x7, Pallas kernels: 10.1 us -> 10.8 us  [call(): pl.pallas_call(kernel, out_shape=shapes, in_specs=specs, out_specs=[VMEM]...]
  transfers between devices with their start and end apart: 3 -> 10, of which waited for: 2 -> 6; matrix products, arithmetic and copies ran while one was open for 0% -> 0% of each run, Pallas kernels for 3% -> 6%
where the time goes in v5:
time: 88.9 us; the launch traced here: 87.6 us
  blocking collectives  40.3 us (45%)
  starting transfers between devices  20.7 us (23%)
  waiting for transfers between devices  14.9 us (17%)
  Pallas kernels  10.8 us (12%)
    all_to_all x1, blocking collectives, exchange(): lax.all_to_all(value, EIG + SPACE, split_axis=0, concat_axis=0, tiled=Tru...  20.4 us
    all_to_all x1, blocking collectives, local(): own = lax.all_to_all(chunks, PLANE, split_axis=0, concat_axis=0, tiled=True)  19.9 us
    pallas_call x7, Pallas kernels, call(): pl.pallas_call(kernel, out_shape=shapes, in_specs=specs, out_specs=[VMEM]...  10.8 us
    ppermute x6, starting transfers between devices, first_shift(): return lax.ppermute(value, EIG + SPACE, pairs)  8.63 us
    ppermute x2, starting transfers between devices, from_above(): return lax.ppermute(value, 'z', [(i, (i - 1) % 8) for i in range(8)])  7.02 us
    ppermute x6, waiting for transfers between devices, first_shift(): return lax.ppermute(value, EIG + SPACE, pairs)  6.54 us
    ppermute x1, waiting for transfers between devices, local(): lax.ppermute(block, EIG + SPACE, [(e * 16 + s, s * 16 + e) for e in range...  6.13 us
    ppermute x1, starting transfers between devices, local(): lax.ppermute(block, EIG + SPACE, [(e * 16 + s, s * 16 + e) for e in range...  5.05 us
  transfers between devices with their start and end apart: 10, of which 6 were waited for; matrix products, arithmetic and copies ran while one was open for 0% of the time, Pallas kernels for 6%

profile of v5, /device:TPU:24, one launch (start us, length us, event | category | flops | bytes accessed | tf_op | source)
XLA Modules:
  0.0 87.6 jit_solution(2611025974153778156)
XLA Ops:
  0.0 3.6 %shard_map.37 = f32[16,104,128]{2,1,0:T(8,128)} custom-call(f32[1536,128]{1,0:T(8,128)} %bitcast.23, f32[72,128]{1,0:T(8,128)} %bitcast.30), custom_call_target="tpu_custom_call" | custom-call | bytes 823296 | tf_op jit(solution)/shard_map/pallas_call | solution.py:308
  3.6 19.9 %all_to_all.10 = f32[16,104,128]{2,1,0:T(8,128)S(1)} all-to-all(f32[16,104,128]{2,1,0:T(8,128)} %shard_map.37), channel_id=1, replica_groups=mesh['ylo'=2,'x'=4,'core'=2,'z'=8,'yhi'=2] {'yhi','ylo','x'}, dimensions={0} | all-to-all | bytes 1703936 | tf_op jit(solution)/shard_map/all_to_all | solution.py:374
  23.5 0.0 collective-permute-start.1
  23.5 5.9 %collective-permute-start = (f32[8,56,128]{2,1,0:T(8,128)S(1)}, f32[8,56,128]{2,1,0:T(8,128)S(1)}, u32[]{:S(2)}, u32[]{:S(2)}) collective-permute-start(f32[8,56,128]{2,1,0:T(8,128)S(1)} %slice_bitcast_fusion), channel_id=1, source_target_pairs={{0,14},{2,0},{4,2},{6,4},{8,6},{10,8},{12,10},{14,12},{1,15},{3,1}... | collective-permute-start | bytes 688136 | tf_op jit(solution)/shard_map/ppermute | solution.py:378
  29.5 1.1 %collective-permute-start.5 = (f32[8,48,128]{2,1,0:T(8,128)S(1)}, f32[8,48,128]{2,1,0:T(8,128)S(1)}, u32[]{:S(2)}, u32[]{:S(2)}) collective-permute-start(f32[8,48,128]{2,1,0:T(8,128)S(1)} %slice_bitcast_fusion.1), channel_id=1, source_target_pairs={{0,14},{2,0},{4,2},{6,4},{8,6},{10,8},{12,10},{14,12},{1,15},{3,1}... | collective-permute-start | bytes 589832 | tf_op jit(solution)/shard_map/ppermute | solution.py:378
  30.6 0.0 collective-permute-done.1.other_ref
  30.6 2.6 %shard_map.38 = (f32[2,512,256]{2,1,0:T(8,128)S(1)}, f32[2,512,256]{2,1,0:T(8,128)S(1)}, bf16[2,256,384]{2,1,0:T(8,128)(2,1)S(1)}, bf16[2,256,384]{2,1,0:T(8,128...) custom-call(f32[2,8,104,128]{3,2,1,0:T(8,128)S(1)} %bitcast.18, ...), custom_call_target="tpu_custom_call" | custom-call | flops 1207959552 | bytes 1703936 | tf_op jit(solution)/shard_map/pallas_call | solution.py:308
  33.2 2.2 %collective-permute-done.above_ref = f32[8,56,128]{2,1,0:T(8,128)S(1)} collective-permute-done((f32[8,56,128]{2,1,0:T(8,128)S(1)}, f32[8,56,128]{2,1,0:T(8,128)S(1)}, u32[]{:S(2)}, u32[]{:S(2)}) %collective-permute-start) | collective-permute-done | bytes 229408 | tf_op jit(solution)/shard_map/ppermute | solution.py:378
  35.4 1.6 %shard_map.39 = (f32[16,8,16,128]{3,2,1,0:T(8,128)S(1)}, f32[72,128]{1,0:T(8,128)S(1)}) custom-call(f32[2,8,104,128]{3,2,1,0:T(8,128)S(1)} %bitcast.19, f32[8,56,128]{2,1,0:T(8,128)S(1)} %collective-permute-done.above_ref, f32[2,512,256]{2,1,0:T(8,128)S(1)} %get-tuple-element.13.refs_0_, bf16[2,256,384]{2,1,0:T(8,128)(2,1)S(1)} %get-tuple-element.14.refs_1_.refs_2_, ...), custom_call_target="tpu_custom_call" | custom-call | flops 603979776 | bytes 5275648 | tf_op jit(solution)/shard_map/pallas_call | solution.py:308
  37.0 0.1 fusion.1
  37.1 1.2 %collective-permute-start.2 = (f32[32,16,128]{2,1,0:T(8,128)S(1)}, f32[32,16,128]{2,1,0:T(8,128)S(1)}, u32[]{:S(2)}, u32[]{:S(2)}) collective-permute-start(f32[32,16,128]{2,1,0:T(8,128)S(1)} %bitcast.26), channel_id=1, source_target_pairs={{0,64},{16,17},{32,96},{144,145},{64,0},{17,16},{96,32},{145,144},... | collective-permute-start | bytes 786440 | tf_op jit(solution)/shard_map/ppermute | solution.py:345
  38.3 0.6 collective-permute-start.3
  38.9 2.6 %collective-permute-start.4 = (f32[32,16,128]{2,1,0:T(8,128)S(1)}, f32[32,16,128]{2,1,0:T(8,128)S(1)}, u32[]{:S(2)}, u32[]{:S(2)}) collective-permute-start(f32[32,16,128]{2,1,0:T(8,128)S(1)} %bitcast.24), channel_id=1, source_target_pairs={{0,96},{16,145},{32,0},{144,16},{64,32},{17,144},{96,64},{145,17},... | collective-permute-start | bytes 786440 | tf_op jit(solution)/shard_map/ppermute | solution.py:345
  41.5 0.0 collective-permute-done.5.above_ref
  41.5 1.3 %shard_map.41 = f32[16,8,16,128]{3,2,1,0:T(8,128)S(1)} custom-call(f32[2,8,104,128]{3,2,1,0:T(8,128)S(1)} %bitcast.20, f32[8,48,128]{2,1,0:T(8,128)S(1)} %collective-permute-done.5.above_ref, f32[72,128]{1,0:T(8,128)S(1)} %get-tuple-element.19.refs_0_, f32[2,512,256]{2,1,0:T(8,128)S(1)} %get-tuple-element.20.refs_1_, ...), custom_call_target="tpu_custom_call" | custom-call | flops 603979776 | bytes 5279744 | tf_op jit(solution)/shard_map/pallas_call | solution.py:308
  42.9 0.1 fusion
  42.9 1.3 %collective-permute-start.6 = (f32[32,16,128]{2,1,0:T(8,128)S(1)}, f32[32,16,128]{2,1,0:T(8,128)S(1)}, u32[]{:S(2)}, u32[]{:S(2)}) collective-permute-start(f32[32,16,128]{2,1,0:T(8,128)S(1)} %bitcast.29), channel_id=1, source_target_pairs={{0,64},{16,17},{32,96},{144,145},{64,0},{17,16},{96,32},{145,144},... | collective-permute-start | bytes 786440 | tf_op jit(solution)/shard_map/ppermute | solution.py:345
  44.2 0.6 collective-permute-start.7
  44.8 0.3 collective-permute-done.2.refs_1_
  45.1 2.3 %collective-permute-start.8 = (f32[32,16,128]{2,1,0:T(8,128)S(1)}, f32[32,16,128]{2,1,0:T(8,128)S(1)}, u32[]{:S(2)}, u32[]{:S(2)}) collective-permute-start(f32[32,16,128]{2,1,0:T(8,128)S(1)} %bitcast.27), channel_id=1, source_target_pairs={{0,96},{16,145},{32,0},{144,16},{64,32},{17,144},{96,64},{145,17},... | collective-permute-start | bytes 786440 | tf_op jit(solution)/shard_map/ppermute | solution.py:345
  47.5 0.4 collective-permute-done.3.refs_2_
  47.8 0.0 collective-permute-done.4.refs_3_
  47.9 3.1 %collective-permute-done.6.refs_2_ = f32[32,16,128]{2,1,0:T(8,128)S(1)} collective-permute-done((f32[32,16,128]{2,1,0:T(8,128)S(1)}, f32[32,16,128]{2,1,0:T(8,128)S(1)}, u32[]{:S(2)}, u32[]{:S(2)}) %collective-permute-start.6) | collective-permute-done | bytes 262176 | tf_op jit(solution)/shard_map/ppermute | solution.py:345
  51.0 2.7 %collective-permute-done.7.refs_3_ = f32[32,16,128]{2,1,0:T(8,128)S(1)} collective-permute-done((f32[32,16,128]{2,1,0:T(8,128)S(1)}, f32[32,16,128]{2,1,0:T(8,128)S(1)}, u32[]{:S(2)}, u32[]{:S(2)}) %collective-permute-start.7) | collective-permute-done | bytes 262176 | tf_op jit(solution)/shard_map/ppermute | solution.py:345
  53.7 0.0 collective-permute-done.8.refs_4_
  53.7 0.0 copy-start
  53.7 0.7 copy-done
  54.4 0.7 shard_map.42
  55.1 20.4 %all_to_all.11 = f32[32,2,16,128]{3,2,1,0:T(8,128)S(1)} all-to-all(f32[32,2,16,128]{3,2,1,0:T(8,128)S(1)} %shard_map.42), channel_id=1, replica_groups={{0,2,4,6,8,10,12,14,128,130,132,134,136,138,140,142,1,3,5,7,9,11,13,15,..., dimensions={0} | all-to-all | bytes 1048576 | tf_op jit(solution)/shard_map/all_to_all | solution.py:354
  75.5 5.1 %collective-permute-start.9 = (f32[2,16,128]{2,1,0:T(8,128)S(1)}, f32[2,16,128]{2,1,0:T(8,128)S(1)}, u32[]{:S(2)}, u32[]{:S(2)}) collective-permute-start(f32[2,16,128]{2,1,0:T(8,128)S(1)} %reduce_sum.9.own_ref), channel_id=1, source_target_pairs={{0,0},{1,16},{2,32},{3,48},{4,64},{5,80},{6,96},{7,112},{8,128},{9... | collective-permute-start | bytes 49160 | tf_op jit(solution)/shard_map/ppermute | solution.py:413
  80.6 6.1 %collective-permute-done.9.mirror_ref = f32[2,16,128]{2,1,0:T(8,128)S(1)} collective-permute-done((f32[2,16,128]{2,1,0:T(8,128)S(1)}, f32[2,16,128]{2,1,0:T(8,128)S(1)}, u32[]{:S(2)}, u32[]{:S(2)}) %collective-permute-start.9) | collective-permute-done | bytes 16416 | tf_op jit(solution)/shard_map/ppermute | solution.py:413
  86.7 0.9 shard_map.43
  (4 shorter events, 0.1 us)
Async XLA Ops:
  23.5 7.1 %collective-permute-start.1 = (f32[2,8,104,128]{3,2,1,0:T(8,128)S(1)}, f32[2,8,104,128]{3,2,1,0:T(8,128)S(1)}, u32[]{:S(2)}, u32[]{:S(2)}) collective-permute-start(f32[2,8,104,128]{3,2,1,0:T(8,128)S(1)} %bitcast.15), channel_id=1, source_target_pairs={{0,16},{16,0},{1,17},{17,1},{2,18},{18,2},{3,19},{19,3},{4,20},{20... | collective-permute-start | bytes 2555912 | tf_op jit(solution)/shard_map/ppermute | solution.py:381
  23.5 11.9 %collective-permute-start = (f32[8,56,128]{2,1,0:T(8,128)S(1)}, f32[8,56,128]{2,1,0:T(8,128)S(1)}, u32[]{:S(2)}, u32[]{:S(2)}) collective-permute-start(f32[8,56,128]{2,1,0:T(8,128)S(1)} %slice_bitcast_fusion), channel_id=1, source_target_pairs={{0,14},{2,0},{4,2},{6,4},{8,6},{10,8},{12,10},{14,12},{1,15},{3,1}... | collective-permute-start | bytes 688136 | tf_op jit(solution)/shard_map/ppermute | solution.py:378
  29.5 12.0 %collective-permute-start.5 = (f32[8,48,128]{2,1,0:T(8,128)S(1)}, f32[8,48,128]{2,1,0:T(8,128)S(1)}, u32[]{:S(2)}, u32[]{:S(2)}) collective-permute-start(f32[8,48,128]{2,1,0:T(8,128)S(1)} %slice_bitcast_fusion.1), channel_id=1, source_target_pairs={{0,14},{2,0},{4,2},{6,4},{8,6},{10,8},{12,10},{14,12},{1,15},{3,1}... | collective-permute-start | bytes 589832 | tf_op jit(solution)/shard_map/ppermute | solution.py:378
  37.1 8.1 %collective-permute-start.2 = (f32[32,16,128]{2,1,0:T(8,128)S(1)}, f32[32,16,128]{2,1,0:T(8,128)S(1)}, u32[]{:S(2)}, u32[]{:S(2)}) collective-permute-start(f32[32,16,128]{2,1,0:T(8,128)S(1)} %bitcast.26), channel_id=1, source_target_pairs={{0,64},{16,17},{32,96},{144,145},{64,0},{17,16},{96,32},{145,144},... | collective-permute-start | bytes 786440 | tf_op jit(solution)/shard_map/ppermute | solution.py:345
  38.3 9.6 %collective-permute-start.3 = (f32[32,16,128]{2,1,0:T(8,128)S(1)}, f32[32,16,128]{2,1,0:T(8,128)S(1)}, u32[]{:S(2)}, u32[]{:S(2)}) collective-permute-start(f32[32,16,128]{2,1,0:T(8,128)S(1)} %bitcast.25), channel_id=1, source_target_pairs={{0,32},{16,144},{32,64},{144,17},{64,96},{17,145},{96,0},{145,16},... | collective-permute-start | bytes 786440 | tf_op jit(solution)/shard_map/ppermute | solution.py:345
  38.9 8.9 %collective-permute-start.4 = (f32[32,16,128]{2,1,0:T(8,128)S(1)}, f32[32,16,128]{2,1,0:T(8,128)S(1)}, u32[]{:S(2)}, u32[]{:S(2)}) collective-permute-start(f32[32,16,128]{2,1,0:T(8,128)S(1)} %bitcast.24), channel_id=1, source_target_pairs={{0,96},{16,145},{32,0},{144,16},{64,32},{17,144},{96,64},{145,17},... | collective-permute-start | bytes 786440 | tf_op jit(solution)/shard_map/ppermute | solution.py:345
  42.9 8.1 %collective-permute-start.6 = (f32[32,16,128]{2,1,0:T(8,128)S(1)}, f32[32,16,128]{2,1,0:T(8,128)S(1)}, u32[]{:S(2)}, u32[]{:S(2)}) collective-permute-start(f32[32,16,128]{2,1,0:T(8,128)S(1)} %bitcast.29), channel_id=1, source_target_pairs={{0,64},{16,17},{32,96},{144,145},{64,0},{17,16},{96,32},{145,144},... | collective-permute-start | bytes 786440 | tf_op jit(solution)/shard_map/ppermute | solution.py:345
  44.2 9.5 %collective-permute-start.7 = (f32[32,16,128]{2,1,0:T(8,128)S(1)}, f32[32,16,128]{2,1,0:T(8,128)S(1)}, u32[]{:S(2)}, u32[]{:S(2)}) collective-permute-start(f32[32,16,128]{2,1,0:T(8,128)S(1)} %bitcast.28), channel_id=1, source_target_pairs={{0,32},{16,144},{32,64},{144,17},{64,96},{17,145},{96,0},{145,16},... | collective-permute-start | bytes 786440 | tf_op jit(solution)/shard_map/ppermute | solution.py:345
  45.1 8.6 %collective-permute-start.8 = (f32[32,16,128]{2,1,0:T(8,128)S(1)}, f32[32,16,128]{2,1,0:T(8,128)S(1)}, u32[]{:S(2)}, u32[]{:S(2)}) collective-permute-start(f32[32,16,128]{2,1,0:T(8,128)S(1)} %bitcast.27), channel_id=1, source_target_pairs={{0,96},{16,145},{32,0},{144,16},{64,32},{17,144},{96,64},{145,17},... | collective-permute-start | bytes 786440 | tf_op jit(solution)/shard_map/ppermute | solution.py:345
  53.7 0.7 copy-start
  75.5 11.2 %collective-permute-start.9 = (f32[2,16,128]{2,1,0:T(8,128)S(1)}, f32[2,16,128]{2,1,0:T(8,128)S(1)}, u32[]{:S(2)}, u32[]{:S(2)}) collective-permute-start(f32[2,16,128]{2,1,0:T(8,128)S(1)} %reduce_sum.9.own_ref), channel_id=1, source_target_pairs={{0,0},{1,16},{2,32},{3,48},{4,64},{5,80},{6,96},{7,112},{8,128},{9... | collective-permute-start | bytes 49160 | tf_op jit(solution)/shard_map/ppermute | solution.py:413

commit v6 on v5

--- a/solution.py
+++ b/solution.py
@@ -252,13 +252,13 @@
         out_ref[index] = total
 
 
-def gather_kernel(separations_ref, *refs):
+def gather_kernel(order_ref, *refs):
     share_refs, out_ref = (refs[:1], refs[1:5]), refs[5]
 
     def one(line, carry):
         fields = []
         for q in range(NZD):
-            at = line * 8 + separations_ref[q] * 2
+            at = line * 8 + order_ref[q]
             sums = []
             for sign in range(2):
                 for part in range(2):
@@ -407,7 +407,7 @@
         flops=FIELD_FLOPS // 2,
     )
     summands = [summed] + along_first_ring(shares)
-    (parts,) = call(gather_kernel, [((32, 2, 16, LANES), F32)], (separations, *summands))
+    (parts,) = call(gather_kernel, [((32, 2, 16, LANES), F32)], (separations * 2, *summands))
     parts = exchange(parts, second_groups())
     block = jnp.sum(parts, axis=0)
     mirror = lax.ppermute(

time: 88.9 us -> 88.2 us (level)
  waiting for transfers between devices: 14.9 us -> 17.1 us
  starting transfers between devices: 20.7 us -> 18.5 us
  blocking collectives: 40.3 us -> 39 us
    ppermute x1, waiting for transfers between devices: 6.13 us -> 8.47 us  [local(): lax.ppermute(block, EIG + SPACE, [(e * 16 + s, s * 16 + e) for e in range...]
    ppermute x1, starting transfers between devices: 5.05 us -> 2.74 us  [local(): lax.ppermute(block, EIG + SPACE, [(e * 16 + s, s * 16 + e) for e in range...]
    all_to_all x1, blocking collectives: 20.4 us -> 19.1 us  [exchange(): lax.all_to_all(value, EIG + SPACE, split_axis=0, concat_axis=0, tiled=Tru...]
  transfers between devices with their start and end apart: 10 -> 10, of which waited for: 6 -> 6; matrix products, arithmetic and copies ran while one was open for 0% -> 0% of each run, Pallas kernels for 6% -> 7%
where the time goes in v6:
time: 88.2 us; the launch traced here: 86.6 us
  blocking collectives  39 us (44%)
  starting transfers between devices  18.5 us (21%)
  waiting for transfers between devices  17.1 us (19%)
  Pallas kernels  11 us (12%)
    all_to_all x1, blocking collectives, local(): own = lax.all_to_all(chunks, PLANE, split_axis=0, concat_axis=0, tiled=True)  19.9 us
    all_to_all x1, blocking collectives, exchange(): lax.all_to_all(value, EIG + SPACE, split_axis=0, concat_axis=0, tiled=Tru...  19.1 us
    pallas_call x7, Pallas kernels, call(): pl.pallas_call(kernel, out_shape=shapes, in_specs=specs, out_specs=[VMEM]...  11 us
    ppermute x6, starting transfers between devices, first_shift(): return lax.ppermute(value, EIG + SPACE, pairs)  8.7 us
    ppermute x1, waiting for transfers between devices, local(): lax.ppermute(block, EIG + SPACE, [(e * 16 + s, s * 16 + e) for e in range...  8.47 us
    ppermute x2, starting transfers between devices, from_above(): return lax.ppermute(value, 'z', [(i, (i - 1) % 8) for i in range(8)])  7.02 us
    ppermute x6, waiting for transfers between devices, first_shift(): return lax.ppermute(value, EIG + SPACE, pairs)  6.46 us
    ppermute x1, starting transfers between devices, local(): lax.ppermute(block, EIG + SPACE, [(e * 16 + s, s * 16 + e) for e in range...  2.74 us
  transfers between devices with their start and end apart: 10, of which 6 were waited for; matrix products, arithmetic and copies ran while one was open for 0% of the time, Pallas kernels for 7%

profile of v6, /device:TPU:24, one launch (start us, length us, event | category | flops | bytes accessed | tf_op | source)
XLA Modules:
  0.0 86.6 jit_solution(10917043983727519366)
XLA Ops:
  0.0 3.6 %shard_map.37 = f32[16,104,128]{2,1,0:T(8,128)} custom-call(f32[1536,128]{1,0:T(8,128)} %bitcast.23, f32[72,128]{1,0:T(8,128)} %bitcast.30), custom_call_target="tpu_custom_call" | custom-call | bytes 823296 | tf_op jit(solution)/shard_map/pallas_call | solution.py:308
  3.6 19.9 %all_to_all.10 = f32[16,104,128]{2,1,0:T(8,128)S(1)} all-to-all(f32[16,104,128]{2,1,0:T(8,128)} %shard_map.37), channel_id=1, replica_groups=mesh['ylo'=2,'x'=4,'core'=2,'z'=8,'yhi'=2] {'yhi','ylo','x'}, dimensions={0} | all-to-all | bytes 1703936 | tf_op jit(solution)/shard_map/all_to_all | solution.py:374
  23.5 0.0 copy-start
  23.5 0.0 collective-permute-start.1
  23.5 0.7 copy-done
  24.2 5.9 %collective-permute-start = (f32[8,56,128]{2,1,0:T(8,128)S(1)}, f32[8,56,128]{2,1,0:T(8,128)S(1)}, u32[]{:S(2)}, u32[]{:S(2)}) collective-permute-start(f32[8,56,128]{2,1,0:T(8,128)S(1)} %slice_bitcast_fusion), channel_id=1, source_target_pairs={{0,14},{2,0},{4,2},{6,4},{8,6},{10,8},{12,10},{14,12},{1,15},{3,1}... | collective-permute-start | bytes 688136 | tf_op jit(solution)/shard_map/ppermute | solution.py:378
  30.1 1.1 %collective-permute-start.5 = (f32[8,48,128]{2,1,0:T(8,128)S(1)}, f32[8,48,128]{2,1,0:T(8,128)S(1)}, u32[]{:S(2)}, u32[]{:S(2)}) collective-permute-start(f32[8,48,128]{2,1,0:T(8,128)S(1)} %slice_bitcast_fusion.1), channel_id=1, source_target_pairs={{0,14},{2,0},{4,2},{6,4},{8,6},{10,8},{12,10},{14,12},{1,15},{3,1}... | collective-permute-start | bytes 589832 | tf_op jit(solution)/shard_map/ppermute | solution.py:378
  31.2 0.0 collective-permute-done.1.other_ref
  31.2 2.7 %shard_map.38 = (f32[2,512,256]{2,1,0:T(8,128)S(1)}, f32[2,512,256]{2,1,0:T(8,128)S(1)}, bf16[2,256,384]{2,1,0:T(8,128)(2,1)S(1)}, bf16[2,256,384]{2,1,0:T(8,128...) custom-call(f32[2,8,104,128]{3,2,1,0:T(8,128)S(1)} %bitcast.18, ...), custom_call_target="tpu_custom_call" | custom-call | flops 1207959552 | bytes 1703936 | tf_op jit(solution)/shard_map/pallas_call | solution.py:308
  34.0 2.2 %collective-permute-done.above_ref = f32[8,56,128]{2,1,0:T(8,128)S(1)} collective-permute-done((f32[8,56,128]{2,1,0:T(8,128)S(1)}, f32[8,56,128]{2,1,0:T(8,128)S(1)}, u32[]{:S(2)}, u32[]{:S(2)}) %collective-permute-start) | collective-permute-done | bytes 229408 | tf_op jit(solution)/shard_map/ppermute | solution.py:378
  36.1 1.6 %shard_map.39 = (f32[16,8,16,128]{3,2,1,0:T(8,128)S(1)}, f32[72,128]{1,0:T(8,128)S(1)}) custom-call(f32[2,8,104,128]{3,2,1,0:T(8,128)S(1)} %bitcast.19, f32[8,56,128]{2,1,0:T(8,128)S(1)} %collective-permute-done.above_ref, f32[2,512,256]{2,1,0:T(8,128)S(1)} %get-tuple-element.13.refs_0_, bf16[2,256,384]{2,1,0:T(8,128)(2,1)S(1)} %get-tuple-element.14.refs_1_.refs_2_, ...), custom_call_target="tpu_custom_call" | custom-call | flops 603979776 | bytes 5275648 | tf_op jit(solution)/shard_map/pallas_call | solution.py:308
  37.8 0.1 fusion.1
  37.9 1.2 %collective-permute-start.2 = (f32[32,16,128]{2,1,0:T(8,128)S(1)}, f32[32,16,128]{2,1,0:T(8,128)S(1)}, u32[]{:S(2)}, u32[]{:S(2)}) collective-permute-start(f32[32,16,128]{2,1,0:T(8,128)S(1)} %bitcast.26), channel_id=1, source_target_pairs={{0,64},{16,17},{32,96},{144,145},{64,0},{17,16},{96,32},{145,144},... | collective-permute-start | bytes 786440 | tf_op jit(solution)/shard_map/ppermute | solution.py:345
  39.1 0.6 collective-permute-start.3
  39.7 2.6 %collective-permute-start.4 = (f32[32,16,128]{2,1,0:T(8,128)S(1)}, f32[32,16,128]{2,1,0:T(8,128)S(1)}, u32[]{:S(2)}, u32[]{:S(2)}) collective-permute-start(f32[32,16,128]{2,1,0:T(8,128)S(1)} %bitcast.24), channel_id=1, source_target_pairs={{0,96},{16,145},{32,0},{144,16},{64,32},{17,144},{96,64},{145,17},... | collective-permute-start | bytes 786440 | tf_op jit(solution)/shard_map/ppermute | solution.py:345
  42.3 0.0 collective-permute-done.5.above_ref
  42.3 1.4 %shard_map.41 = f32[16,8,16,128]{3,2,1,0:T(8,128)S(1)} custom-call(f32[2,8,104,128]{3,2,1,0:T(8,128)S(1)} %bitcast.20, f32[8,48,128]{2,1,0:T(8,128)S(1)} %collective-permute-done.5.above_ref, f32[72,128]{1,0:T(8,128)S(1)} %get-tuple-element.19.refs_0_, f32[2,512,256]{2,1,0:T(8,128)S(1)} %get-tuple-element.20.refs_1_, ...), custom_call_target="tpu_custom_call" | custom-call | flops 603979776 | bytes 5279744 | tf_op jit(solution)/shard_map/pallas_call | solution.py:308
  43.7 0.1 fusion
  43.8 1.3 %collective-permute-start.6 = (f32[32,16,128]{2,1,0:T(8,128)S(1)}, f32[32,16,128]{2,1,0:T(8,128)S(1)}, u32[]{:S(2)}, u32[]{:S(2)}) collective-permute-start(f32[32,16,128]{2,1,0:T(8,128)S(1)} %bitcast.29), channel_id=1, source_target_pairs={{0,64},{16,17},{32,96},{144,145},{64,0},{17,16},{96,32},{145,144},... | collective-permute-start | bytes 786440 | tf_op jit(solution)/shard_map/ppermute | solution.py:345
  45.1 0.6 collective-permute-start.7
  45.7 0.3 collective-permute-done.2.refs_1_
  45.9 2.4 %collective-permute-start.8 = (f32[32,16,128]{2,1,0:T(8,128)S(1)}, f32[32,16,128]{2,1,0:T(8,128)S(1)}, u32[]{:S(2)}, u32[]{:S(2)}) collective-permute-start(f32[32,16,128]{2,1,0:T(8,128)S(1)} %bitcast.27), channel_id=1, source_target_pairs={{0,96},{16,145},{32,0},{144,16},{64,32},{17,144},{96,64},{145,17},... | collective-permute-start | bytes 786440 | tf_op jit(solution)/shard_map/ppermute | solution.py:345
  48.3 0.3 collective-permute-done.3.refs_2_
  48.6 0.0 collective-permute-done.4.refs_3_
  48.7 3.2 %collective-permute-done.6.refs_2_ = f32[32,16,128]{2,1,0:T(8,128)S(1)} collective-permute-done((f32[32,16,128]{2,1,0:T(8,128)S(1)}, f32[32,16,128]{2,1,0:T(8,128)S(1)}, u32[]{:S(2)}, u32[]{:S(2)}) %collective-permute-start.6) | collective-permute-done | bytes 262176 | tf_op jit(solution)/shard_map/ppermute | solution.py:345
  51.9 2.7 %collective-permute-done.7.refs_3_ = f32[32,16,128]{2,1,0:T(8,128)S(1)} collective-permute-done((f32[32,16,128]{2,1,0:T(8,128)S(1)}, f32[32,16,128]{2,1,0:T(8,128)S(1)}, u32[]{:S(2)}, u32[]{:S(2)}) %collective-permute-start.7) | collective-permute-done | bytes 262176 | tf_op jit(solution)/shard_map/ppermute | solution.py:345
  54.6 0.0 collective-permute-done.8.refs_4_
  54.6 0.7 shard_map.42
  55.3 19.1 %all_to_all.11 = f32[32,2,16,128]{3,2,1,0:T(8,128)S(1)} all-to-all(f32[32,2,16,128]{3,2,1,0:T(8,128)S(1)} %shard_map.42), channel_id=1, replica_groups={{0,2,4,6,8,10,12,14,128,130,132,134,136,138,140,142,1,3,5,7,9,11,13,15,..., dimensions={0} | all-to-all | bytes 1048576 | tf_op jit(solution)/shard_map/all_to_all | solution.py:354
  74.5 2.7 %collective-permute-start.9 = (f32[2,16,128]{2,1,0:T(8,128)S(1)}, f32[2,16,128]{2,1,0:T(8,128)S(1)}, u32[]{:S(2)}, u32[]{:S(2)}) collective-permute-start(f32[2,16,128]{2,1,0:T(8,128)S(1)} %reduce_sum.9.own_ref), channel_id=1, source_target_pairs={{0,0},{1,16},{2,32},{3,48},{4,64},{5,80},{6,96},{7,112},{8,128},{9... | collective-permute-start | bytes 49160 | tf_op jit(solution)/shard_map/ppermute | solution.py:413
  77.2 8.5 %collective-permute-done.9.mirror_ref = f32[2,16,128]{2,1,0:T(8,128)S(1)} collective-permute-done((f32[2,16,128]{2,1,0:T(8,128)S(1)}, f32[2,16,128]{2,1,0:T(8,128)S(1)}, u32[]{:S(2)}, u32[]{:S(2)}) %collective-permute-start.9) | collective-permute-done | bytes 16416 | tf_op jit(solution)/shard_map/ppermute | solution.py:413
  85.7 0.9 %shard_map.43 = f32[2,4,2,2,16,16]{5,4,3,2,1,0:T(8,128)} custom-call(f32[2,16,128]{2,1,0:T(8,128)S(1)} %reduce_sum.9.own_ref, f32[2,16,128]{2,1,0:T(8,128)S(1)} %collective-permute-done.9.mirror_ref), custom_call_target="tpu_custom_call" | custom-call | bytes 32768 | tf_op jit(solution)/shard_map/pallas_call | solution.py:308
  (5 shorter events, 0.1 us)
Async XLA Ops:
  23.5 0.7 copy-start
  23.5 7.7 %collective-permute-start.1 = (f32[2,8,104,128]{3,2,1,0:T(8,128)S(1)}, f32[2,8,104,128]{3,2,1,0:T(8,128)S(1)}, u32[]{:S(2)}, u32[]{:S(2)}) collective-permute-start(f32[2,8,104,128]{3,2,1,0:T(8,128)S(1)} %bitcast.15), channel_id=1, source_target_pairs={{0,16},{16,0},{1,17},{17,1},{2,18},{18,2},{3,19},{19,3},{4,20},{20... | collective-permute-start | bytes 2555912 | tf_op jit(solution)/shard_map/ppermute | solution.py:381
  24.2 11.9 %collective-permute-start = (f32[8,56,128]{2,1,0:T(8,128)S(1)}, f32[8,56,128]{2,1,0:T(8,128)S(1)}, u32[]{:S(2)}, u32[]{:S(2)}) collective-permute-start(f32[8,56,128]{2,1,0:T(8,128)S(1)} %slice_bitcast_fusion), channel_id=1, source_target_pairs={{0,14},{2,0},{4,2},{6,4},{8,6},{10,8},{12,10},{14,12},{1,15},{3,1}... | collective-permute-start | bytes 688136 | tf_op jit(solution)/shard_map/ppermute | solution.py:378
  30.1 12.2 %collective-permute-start.5 = (f32[8,48,128]{2,1,0:T(8,128)S(1)}, f32[8,48,128]{2,1,0:T(8,128)S(1)}, u32[]{:S(2)}, u32[]{:S(2)}) collective-permute-start(f32[8,48,128]{2,1,0:T(8,128)S(1)} %slice_bitcast_fusion.1), channel_id=1, source_target_pairs={{0,14},{2,0},{4,2},{6,4},{8,6},{10,8},{12,10},{14,12},{1,15},{3,1}... | collective-permute-start | bytes 589832 | tf_op jit(solution)/shard_map/ppermute | solution.py:378
  37.9 8.1 %collective-permute-start.2 = (f32[32,16,128]{2,1,0:T(8,128)S(1)}, f32[32,16,128]{2,1,0:T(8,128)S(1)}, u32[]{:S(2)}, u32[]{:S(2)}) collective-permute-start(f32[32,16,128]{2,1,0:T(8,128)S(1)} %bitcast.26), channel_id=1, source_target_pairs={{0,64},{16,17},{32,96},{144,145},{64,0},{17,16},{96,32},{145,144},... | collective-permute-start | bytes 786440 | tf_op jit(solution)/shard_map/ppermute | solution.py:345
  39.1 9.6 %collective-permute-start.3 = (f32[32,16,128]{2,1,0:T(8,128)S(1)}, f32[32,16,128]{2,1,0:T(8,128)S(1)}, u32[]{:S(2)}, u32[]{:S(2)}) collective-permute-start(f32[32,16,128]{2,1,0:T(8,128)S(1)} %bitcast.25), channel_id=1, source_target_pairs={{0,32},{16,144},{32,64},{144,17},{64,96},{17,145},{96,0},{145,16},... | collective-permute-start | bytes 786440 | tf_op jit(solution)/shard_map/ppermute | solution.py:345
  39.7 8.9 %collective-permute-start.4 = (f32[32,16,128]{2,1,0:T(8,128)S(1)}, f32[32,16,128]{2,1,0:T(8,128)S(1)}, u32[]{:S(2)}, u32[]{:S(2)}) collective-permute-start(f32[32,16,128]{2,1,0:T(8,128)S(1)} %bitcast.24), channel_id=1, source_target_pairs={{0,96},{16,145},{32,0},{144,16},{64,32},{17,144},{96,64},{145,17},... | collective-permute-start | bytes 786440 | tf_op jit(solution)/shard_map/ppermute | solution.py:345
  43.8 8.1 %collective-permute-start.6 = (f32[32,16,128]{2,1,0:T(8,128)S(1)}, f32[32,16,128]{2,1,0:T(8,128)S(1)}, u32[]{:S(2)}, u32[]{:S(2)}) collective-permute-start(f32[32,16,128]{2,1,0:T(8,128)S(1)} %bitcast.29), channel_id=1, source_target_pairs={{0,64},{16,17},{32,96},{144,145},{64,0},{17,16},{96,32},{145,144},... | collective-permute-start | bytes 786440 | tf_op jit(solution)/shard_map/ppermute | solution.py:345
  45.1 9.5 %collective-permute-start.7 = (f32[32,16,128]{2,1,0:T(8,128)S(1)}, f32[32,16,128]{2,1,0:T(8,128)S(1)}, u32[]{:S(2)}, u32[]{:S(2)}) collective-permute-start(f32[32,16,128]{2,1,0:T(8,128)S(1)} %bitcast.28), channel_id=1, source_target_pairs={{0,32},{16,144},{32,64},{144,17},{64,96},{17,145},{96,0},{145,16},... | collective-permute-start | bytes 786440 | tf_op jit(solution)/shard_map/ppermute | solution.py:345
  45.9 8.7 %collective-permute-start.8 = (f32[32,16,128]{2,1,0:T(8,128)S(1)}, f32[32,16,128]{2,1,0:T(8,128)S(1)}, u32[]{:S(2)}, u32[]{:S(2)}) collective-permute-start(f32[32,16,128]{2,1,0:T(8,128)S(1)} %bitcast.27), channel_id=1, source_target_pairs={{0,96},{16,145},{32,0},{144,16},{64,32},{17,144},{96,64},{145,17},... | collective-permute-start | bytes 786440 | tf_op jit(solution)/shard_map/ppermute | solution.py:345
  74.5 11.2 %collective-permute-start.9 = (f32[2,16,128]{2,1,0:T(8,128)S(1)}, f32[2,16,128]{2,1,0:T(8,128)S(1)}, u32[]{:S(2)}, u32[]{:S(2)}) collective-permute-start(f32[2,16,128]{2,1,0:T(8,128)S(1)} %reduce_sum.9.own_ref), channel_id=1, source_target_pairs={{0,0},{1,16},{2,32},{3,48},{4,64},{5,80},{6,96},{7,112},{8,128},{9... | collective-permute-start | bytes 49160 | tf_op jit(solution)/shard_map/ppermute | solution.py:413

commit v7 on v6

--- a/solution.py
+++ b/solution.py
@@ -42,7 +42,7 @@
     return rows
 
 
-def cut_kernel(vectors_hbm, links_hbm, out_ref, vectors_ref, links_ref, arrived):
+def cut_kernel(vectors_hbm, links_hbm, out_hbm, vectors_ref, links_ref, out_ref, arrived, left):
     copies = [
         pltpu.make_async_copy(vectors_hbm.at[rows], vectors_ref.at[rows], arrived.at[index])
         for index, rows in enumerate(pl.ds(i * 384, 384) for i in (0, 2, 1, 3))
@@ -50,11 +50,20 @@
     copies.append(pltpu.make_async_copy(links_hbm, links_ref, arrived.at[4]))
     for copy in copies:
         copy.start()
+    leaving = []
+
+    def send(first):
+        rows = (slice(None), pl.ds(first, 8))
+        leaving.append(
+            pltpu.make_async_copy(out_ref.at[rows], out_hbm.at[rows], left.at[len(leaving)])
+        )
+        leaving[-1].start()
+
     for half in range(2):
         copies[2 * half].wait()
         copies[2 * half + 1].wait()
-        for j in range(2):
-            for colour in range(3):
+        for colour in range(3):
+            for j in range(2):
 
                 def load(part, spin, plane):
                     first = (((part * 16 + half * 8) * 4 + spin) * 3 + colour) * 4 + plane
@@ -74,18 +83,24 @@
                     for sign in range(2):
                         first = FIRST[sign] + colour * 16 + half * 8
                         out_ref[j * 8 + block, first : first + 8, :] = value[sign]
-    copies[4].wait()
-    own = lax.axis_index(("ylo", "x"))
-    row = lax.broadcasted_iota(jnp.int32, (8, LANES), 0)
-    rows = []
-    for part in range(2):
-        for plane in range(4):
-            mine = links_ref[pl.ds((part * 9 + own) * 4 + plane, 1), :]
-            last = links_ref[(part * 9 + 8) * 4 + plane : (part * 9 + 8) * 4 + plane + 1, :]
-            rows.append(jnp.where(row == 0, mine, last))
-    for block, value in enumerate(exchange_pieces(rows)):
-        out_ref[block, LINK_ROW : LINK_ROW + 8, :] = value
-        out_ref[8 + block, LINK_ROW : LINK_ROW + 8, :] = value
+            for sign in range(2):
+                send(FIRST[sign] + colour * 16 + half * 8)
+        if half == 0:
+            copies[4].wait()
+            own = lax.axis_index(("ylo", "x"))
+            row = lax.broadcasted_iota(jnp.int32, (8, LANES), 0)
+            rows = []
+            for part in range(2):
+                for plane in range(4):
+                    mine = links_ref[pl.ds((part * 9 + own) * 4 + plane, 1), :]
+                    at = (part * 9 + 8) * 4 + plane
+                    rows.append(jnp.where(row == 0, mine, links_ref[at : at + 1, :]))
+            for block, value in enumerate(exchange_pieces(rows)):
+                out_ref[block, LINK_ROW : LINK_ROW + 8, :] = value
+                out_ref[8 + block, LINK_ROW : LINK_ROW + 8, :] = value
+            send(LINK_ROW)
+    for copy in leaving:
+        copy.wait()
 
 
 def shifted(here, here_swapped, above, above_swapped, by):
@@ -243,31 +258,37 @@
                     ]
 
 
-def add_kernel(*refs):
-    *share_refs, out_ref = refs
+def add_kernel(separations_ref, *refs):
+    *share_refs, out_ref, order_ref = refs
     for index in range(32):
         total = share_refs[0][index]
         for share_ref in share_refs[1:]:
             total = total + share_ref[index]
         out_ref[index] = total
+    row = lax.broadcasted_iota(jnp.int32, (8, LANES), 0)
+    order = jnp.zeros((8, LANES), jnp.int32)
+    for q in range(NZD):
+        order = jnp.where(row == q, separations_ref[q], order)
+    order_ref[...] = order
 
 
 def gather_kernel(order_ref, *refs):
     share_refs, out_ref = (refs[:1], refs[1:5]), refs[5]
+    chosen = [[order_ref[q : q + 1, :] == k for k in range(NZD - 1)] for q in range(NZD)]
 
     def one(line, carry):
-        fields = []
-        for q in range(NZD):
-            at = line * 8 + order_ref[q]
+        by_length = []
+        for k in range(NZD):
             sums = []
             for sign in range(2):
                 for part in range(2):
-                    total = share_refs[sign][0][at + part]
+                    at = line * 8 + k * 2 + part
+                    total = share_refs[sign][0][at]
                     for share_ref in share_refs[sign][1:]:
-                        total = total + share_ref[at + part]
+                        total = total + share_ref[at]
                     sums.append(total * 0.5)
             plus_real, plus_imag, minus_real, minus_imag = sums
-            fields.append(
+            by_length.append(
                 [
                     plus_imag - minus_imag,
                     minus_real - plus_real,
@@ -275,6 +296,15 @@
                     plus_imag + minus_imag,
                 ]
             )
+        fields = []
+        for q in range(NZD):
+            field = by_length[NZD - 1]
+            for k in range(NZD - 1):
+                field = [
+                    jnp.where(chosen[q][k], one_length, other)
+                    for one_length, other in zip(by_length[k], field)
+                ]
+            fields.append(field)
         for pair in range(2):
             turned = jnp.concatenate(fields[2 * pair] + fields[2 * pair + 1]).T
             for z in range(8):
@@ -303,13 +333,13 @@
 
 def call(kernel, outs, inputs, scratch=(), limit=32, flops=0, space=VMEM):
     shapes = [jax.ShapeDtypeStruct(shape, held) for shape, held in outs]
-    specs = [SMEM if value.dtype == jnp.int32 else space for value in inputs]
+    specs = [SMEM if value.shape == (NZD,) else space for value in inputs]
     count = sum(value.size for value in inputs)
     return pl.pallas_call(
         kernel,
         out_shape=shapes,
         in_specs=specs,
-        out_specs=[VMEM] * len(outs),
+        out_specs=[space] * len(outs),
         scratch_shapes=list(scratch),
         compiler_params=pltpu.CompilerParams(vmem_limit_bytes=limit * 1024 * 1024),
         cost_estimate=pl.CostEstimate(flops=flops, bytes_accessed=count * 4, transcendentals=0),
@@ -364,9 +394,11 @@
         [((16, ROWS, LANES), F32)],
         (vectors, links),
         (
-            pltpu.VMEM((1536, LANES), F32),
+            pltpu.VMEM((1584, LANES), F32),
             pltpu.VMEM((72, LANES), F32),
+            pltpu.VMEM((16, ROWS, LANES), F32),
             pltpu.SemaphoreType.DMA((5,)),
+            pltpu.SemaphoreType.DMA((13,)),
         ),
         limit=56,
         space=pl.BlockSpec(memory_space=pltpu.HBM),
@@ -396,8 +428,11 @@
         half_scratch,
         flops=FIELD_FLOPS // 2,
     )
-    (summed,) = call(
-        add_kernel, [((32, 16, LANES), F32)], along_first_ring(shares), flops=4 * FIELD_FLOPS
+    summed, order = call(
+        add_kernel,
+        [((32, 16, LANES), F32), ((8, LANES), jnp.int32)],
+        (separations, *along_first_ring(shares)),
+        flops=4 * FIELD_FLOPS,
     )
     (shares,) = call(
         functools.partial(high_kernel, 1),
@@ -407,7 +442,7 @@
         flops=FIELD_FLOPS // 2,
     )
     summands = [summed] + along_first_ring(shares)
-    (parts,) = call(gather_kernel, [((32, 2, 16, LANES), F32)], (separations * 2, *summands))
+    (parts,) = call(gather_kernel, [((32, 2, 16, LANES), F32)], (order, *summands))
     parts = exchange(parts, second_groups())
     block = jnp.sum(parts, axis=0)
     mirror = lax.ppermute(

time: 88.2 us -> 87.6 us (level)
  waiting for transfers between devices: 17.1 us -> 13.7 us
  starting transfers between devices: 18.5 us -> 20.7 us
  blocking collectives: 39 us -> 40.3 us
    ppermute x1, waiting for transfers between devices: 8.47 us -> 6.13 us  [local(): lax.ppermute(block, EIG + SPACE, [(e * 16 + s, s * 16 + e) for e in range...]
    ppermute x1, starting transfers between devices: 2.74 us -> 5.05 us  [local(): lax.ppermute(block, EIG + SPACE, [(e * 16 + s, s * 16 + e) for e in range...]
    all_to_all x1, blocking collectives: 19.1 us -> 20.4 us  [exchange(): lax.all_to_all(value, EIG + SPACE, split_axis=0, concat_axis=0, tiled=Tru...]
    ppermute x6, waiting for transfers between devices: 6.46 us -> 5.33 us  [first_shift(): return lax.ppermute(value, EIG + SPACE, pairs)]
where the time goes in v7:
time: 87.6 us; the launch traced here: 86.3 us
  blocking collectives  40.3 us (46%)
  starting transfers between devices  20.7 us (24%)
  waiting for transfers between devices  13.7 us (16%)
  Pallas kernels  10.7 us (12%)
    all_to_all x1, blocking collectives, exchange(): lax.all_to_all(value, EIG + SPACE, split_axis=0, concat_axis=0, tiled=Tru...  20.4 us
    all_to_all x1, blocking collectives, local(): own = lax.all_to_all(chunks, PLANE, split_axis=0, concat_axis=0, tiled=True)  19.9 us
    pallas_call x7, Pallas kernels, call(): pl.pallas_call(kernel, out_shape=shapes, in_specs=specs, out_specs=[space...  10.7 us
    ppermute x6, starting transfers between devices, first_shift(): return lax.ppermute(value, EIG + SPACE, pairs)  8.63 us
    ppermute x2, starting transfers between devices, from_above(): return lax.ppermute(value, 'z', [(i, (i - 1) % 8) for i in range(8)])  7.02 us
    ppermute x1, waiting for transfers between devices, local(): lax.ppermute(block, EIG + SPACE, [(e * 16 + s, s * 16 + e) for e in range...  6.13 us
    ppermute x6, waiting for transfers between devices, first_shift(): return lax.ppermute(value, EIG + SPACE, pairs)  5.33 us
    ppermute x1, starting transfers between devices, local(): lax.ppermute(block, EIG + SPACE, [(e * 16 + s, s * 16 + e) for e in range...  5.05 us
  transfers between devices with their start and end apart: 10, of which 6 were waited for; matrix products, arithmetic and copies ran while one was open for 0% of the time, Pallas kernels for 7%

profile of v7, /device:TPU:24, one launch (start us, length us, event | category | flops | bytes accessed | tf_op | source)
XLA Modules:
  0.0 86.3 jit_solution(1228962339107510150)
XLA Ops:
  0.0 3.4 %shard_map.37 = f32[16,104,128]{2,1,0:T(8,128)} custom-call(f32[1536,128]{1,0:T(8,128)} %bitcast.23, f32[72,128]{1,0:T(8,128)} %bitcast.30), custom_call_target="tpu_custom_call" | custom-call | bytes 823296 | tf_op jit(solution)/shard_map/pallas_call | solution.py:338
  3.4 19.9 %all_to_all.10 = f32[16,104,128]{2,1,0:T(8,128)S(1)} all-to-all(f32[16,104,128]{2,1,0:T(8,128)} %shard_map.37), channel_id=1, replica_groups=mesh['ylo'=2,'x'=4,'core'=2,'z'=8,'yhi'=2] {'yhi','ylo','x'}, dimensions={0} | all-to-all | bytes 1703936 | tf_op jit(solution)/shard_map/all_to_all | solution.py:406
  23.4 0.0 collective-permute-start.1
  23.4 5.9 %collective-permute-start = (f32[8,56,128]{2,1,0:T(8,128)S(1)}, f32[8,56,128]{2,1,0:T(8,128)S(1)}, u32[]{:S(2)}, u32[]{:S(2)}) collective-permute-start(f32[8,56,128]{2,1,0:T(8,128)S(1)} %slice_bitcast_fusion), channel_id=1, source_target_pairs={{0,14},{2,0},{4,2},{6,4},{8,6},{10,8},{12,10},{14,12},{1,15},{3,1}... | collective-permute-start | bytes 688136 | tf_op jit(solution)/shard_map/ppermute | solution.py:410
  29.3 1.1 %collective-permute-start.5 = (f32[8,48,128]{2,1,0:T(8,128)S(1)}, f32[8,48,128]{2,1,0:T(8,128)S(1)}, u32[]{:S(2)}, u32[]{:S(2)}) collective-permute-start(f32[8,48,128]{2,1,0:T(8,128)S(1)} %slice_bitcast_fusion.1), channel_id=1, source_target_pairs={{0,14},{2,0},{4,2},{6,4},{8,6},{10,8},{12,10},{14,12},{1,15},{3,1}... | collective-permute-start | bytes 589832 | tf_op jit(solution)/shard_map/ppermute | solution.py:410
  30.4 0.0 collective-permute-done.1.other_ref
  30.4 2.6 %shard_map.38 = (f32[2,512,256]{2,1,0:T(8,128)S(1)}, f32[2,512,256]{2,1,0:T(8,128)S(1)}, bf16[2,256,384]{2,1,0:T(8,128)(2,1)S(1)}, bf16[2,256,384]{2,1,0:T(8,128...) custom-call(f32[2,8,104,128]{3,2,1,0:T(8,128)S(1)} %bitcast.18, ...), custom_call_target="tpu_custom_call" | custom-call | flops 1207959552 | bytes 1703936 | tf_op jit(solution)/shard_map/pallas_call | solution.py:338
  33.0 2.2 %collective-permute-done.above_ref = f32[8,56,128]{2,1,0:T(8,128)S(1)} collective-permute-done((f32[8,56,128]{2,1,0:T(8,128)S(1)}, f32[8,56,128]{2,1,0:T(8,128)S(1)}, u32[]{:S(2)}, u32[]{:S(2)}) %collective-permute-start) | collective-permute-done | bytes 229408 | tf_op jit(solution)/shard_map/ppermute | solution.py:410
  35.2 1.6 %shard_map.39 = (f32[16,8,16,128]{3,2,1,0:T(8,128)S(1)}, f32[72,128]{1,0:T(8,128)S(1)}) custom-call(f32[2,8,104,128]{3,2,1,0:T(8,128)S(1)} %bitcast.19, f32[8,56,128]{2,1,0:T(8,128)S(1)} %collective-permute-done.above_ref, f32[2,512,256]{2,1,0:T(8,128)S(1)} %get-tuple-element.15.refs_0_, bf16[2,256,384]{2,1,0:T(8,128)(2,1)S(1)} %get-tuple-element.16.refs_1_.refs_2_, ...), custom_call_target="tpu_custom_call" | custom-call | flops 603979776 | bytes 5275648 | tf_op jit(solution)/shard_map/pallas_call | solution.py:338
  36.8 0.1 fusion.1
  36.9 1.2 %collective-permute-start.2 = (f32[32,16,128]{2,1,0:T(8,128)S(1)}, f32[32,16,128]{2,1,0:T(8,128)S(1)}, u32[]{:S(2)}, u32[]{:S(2)}) collective-permute-start(f32[32,16,128]{2,1,0:T(8,128)S(1)} %bitcast.26), channel_id=1, source_target_pairs={{0,64},{16,17},{32,96},{144,145},{64,0},{17,16},{96,32},{145,144},... | collective-permute-start | bytes 786440 | tf_op jit(solution)/shard_map/ppermute | solution.py:375
  38.1 0.6 collective-permute-start.3
  38.8 2.6 %collective-permute-start.4 = (f32[32,16,128]{2,1,0:T(8,128)S(1)}, f32[32,16,128]{2,1,0:T(8,128)S(1)}, u32[]{:S(2)}, u32[]{:S(2)}) collective-permute-start(f32[32,16,128]{2,1,0:T(8,128)S(1)} %bitcast.24), channel_id=1, source_target_pairs={{0,96},{16,145},{32,0},{144,16},{64,32},{17,144},{96,64},{145,17},... | collective-permute-start | bytes 786440 | tf_op jit(solution)/shard_map/ppermute | solution.py:375
  41.4 0.0 collective-permute-done.5.above_ref
  41.4 1.3 %shard_map.41 = f32[16,8,16,128]{3,2,1,0:T(8,128)S(1)} custom-call(f32[2,8,104,128]{3,2,1,0:T(8,128)S(1)} %bitcast.20, f32[8,48,128]{2,1,0:T(8,128)S(1)} %collective-permute-done.5.above_ref, f32[72,128]{1,0:T(8,128)S(1)} %get-tuple-element.23.refs_0_, f32[2,512,256]{2,1,0:T(8,128)S(1)} %get-tuple-element.24.refs_1_, ...), custom_call_target="tpu_custom_call" | custom-call | flops 603979776 | bytes 5279744 | tf_op jit(solution)/shard_map/pallas_call | solution.py:338
  42.7 0.1 fusion
  42.8 1.3 %collective-permute-start.6 = (f32[32,16,128]{2,1,0:T(8,128)S(1)}, f32[32,16,128]{2,1,0:T(8,128)S(1)}, u32[]{:S(2)}, u32[]{:S(2)}) collective-permute-start(f32[32,16,128]{2,1,0:T(8,128)S(1)} %bitcast.29), channel_id=1, source_target_pairs={{0,64},{16,17},{32,96},{144,145},{64,0},{17,16},{96,32},{145,144},... | collective-permute-start | bytes 786440 | tf_op jit(solution)/shard_map/ppermute | solution.py:375
  44.1 0.6 collective-permute-start.7
  44.6 0.3 collective-permute-done.2.refs_1_
  45.0 2.3 %collective-permute-start.8 = (f32[32,16,128]{2,1,0:T(8,128)S(1)}, f32[32,16,128]{2,1,0:T(8,128)S(1)}, u32[]{:S(2)}, u32[]{:S(2)}) collective-permute-start(f32[32,16,128]{2,1,0:T(8,128)S(1)} %bitcast.27), channel_id=1, source_target_pairs={{0,96},{16,145},{32,0},{144,16},{64,32},{17,144},{96,64},{145,17},... | collective-permute-start | bytes 786440 | tf_op jit(solution)/shard_map/ppermute | solution.py:375
  47.3 0.4 collective-permute-done.3.refs_2_
  47.7 0.0 collective-permute-done.4.refs_3_
  47.7 0.0 copy-start
  47.7 0.7 copy-done
  48.3 0.6 shard_map.40
  48.9 1.9 %collective-permute-done.6.refs_2_ = f32[32,16,128]{2,1,0:T(8,128)S(1)} collective-permute-done((f32[32,16,128]{2,1,0:T(8,128)S(1)}, f32[32,16,128]{2,1,0:T(8,128)S(1)}, u32[]{:S(2)}, u32[]{:S(2)}) %collective-permute-start.6) | collective-permute-done | bytes 262176 | tf_op jit(solution)/shard_map/ppermute | solution.py:375
  50.9 2.7 %collective-permute-done.7.refs_3_ = f32[32,16,128]{2,1,0:T(8,128)S(1)} collective-permute-done((f32[32,16,128]{2,1,0:T(8,128)S(1)}, f32[32,16,128]{2,1,0:T(8,128)S(1)}, u32[]{:S(2)}, u32[]{:S(2)}) %collective-permute-start.7) | collective-permute-done | bytes 262176 | tf_op jit(solution)/shard_map/ppermute | solution.py:375
  53.6 0.0 collective-permute-done.8.refs_4_
  53.6 0.2 shard_map.42
  53.8 20.4 %all_to_all.11 = f32[32,2,16,128]{3,2,1,0:T(8,128)S(1)} all-to-all(f32[32,2,16,128]{3,2,1,0:T(8,128)S(1)} %shard_map.42), channel_id=1, replica_groups={{0,2,4,6,8,10,12,14,128,130,132,134,136,138,140,142,1,3,5,7,9,11,13,15,..., dimensions={0} | all-to-all | bytes 1048576 | tf_op jit(solution)/shard_map/all_to_all | solution.py:384
  74.2 5.0 %collective-permute-start.9 = (f32[2,16,128]{2,1,0:T(8,128)S(1)}, f32[2,16,128]{2,1,0:T(8,128)S(1)}, u32[]{:S(2)}, u32[]{:S(2)}) collective-permute-start(f32[2,16,128]{2,1,0:T(8,128)S(1)} %reduce_sum.9.own_ref), channel_id=1, source_target_pairs={{0,0},{1,16},{2,32},{3,48},{4,64},{5,80},{6,96},{7,112},{8,128},{9... | collective-permute-start | bytes 49160 | tf_op jit(solution)/shard_map/ppermute | solution.py:448
  79.3 6.1 %collective-permute-done.9.mirror_ref = f32[2,16,128]{2,1,0:T(8,128)S(1)} collective-permute-done((f32[2,16,128]{2,1,0:T(8,128)S(1)}, f32[2,16,128]{2,1,0:T(8,128)S(1)}, u32[]{:S(2)}, u32[]{:S(2)}) %collective-permute-start.9) | collective-permute-done | bytes 16416 | tf_op jit(solution)/shard_map/ppermute | solution.py:448
  85.4 0.9 %shard_map.43 = f32[2,4,2,2,16,16]{5,4,3,2,1,0:T(8,128)} custom-call(f32[2,16,128]{2,1,0:T(8,128)S(1)} %reduce_sum.9.own_ref, f32[2,16,128]{2,1,0:T(8,128)S(1)} %collective-permute-done.9.mirror_ref), custom_call_target="tpu_custom_call" | custom-call | bytes 32768 | tf_op jit(solution)/shard_map/pallas_call | solution.py:338
  (3 shorter events, 0.1 us)
Async XLA Ops:
  23.4 7.1 %collective-permute-start.1 = (f32[2,8,104,128]{3,2,1,0:T(8,128)S(1)}, f32[2,8,104,128]{3,2,1,0:T(8,128)S(1)}, u32[]{:S(2)}, u32[]{:S(2)}) collective-permute-start(f32[2,8,104,128]{3,2,1,0:T(8,128)S(1)} %bitcast.15), channel_id=1, source_target_pairs={{0,16},{16,0},{1,17},{17,1},{2,18},{18,2},{3,19},{19,3},{4,20},{20... | collective-permute-start | bytes 2555912 | tf_op jit(solution)/shard_map/ppermute | solution.py:413
  23.4 11.9 %collective-permute-start = (f32[8,56,128]{2,1,0:T(8,128)S(1)}, f32[8,56,128]{2,1,0:T(8,128)S(1)}, u32[]{:S(2)}, u32[]{:S(2)}) collective-permute-start(f32[8,56,128]{2,1,0:T(8,128)S(1)} %slice_bitcast_fusion), channel_id=1, source_target_pairs={{0,14},{2,0},{4,2},{6,4},{8,6},{10,8},{12,10},{14,12},{1,15},{3,1}... | collective-permute-start | bytes 688136 | tf_op jit(solution)/shard_map/ppermute | solution.py:410
  29.3 12.0 %collective-permute-start.5 = (f32[8,48,128]{2,1,0:T(8,128)S(1)}, f32[8,48,128]{2,1,0:T(8,128)S(1)}, u32[]{:S(2)}, u32[]{:S(2)}) collective-permute-start(f32[8,48,128]{2,1,0:T(8,128)S(1)} %slice_bitcast_fusion.1), channel_id=1, source_target_pairs={{0,14},{2,0},{4,2},{6,4},{8,6},{10,8},{12,10},{14,12},{1,15},{3,1}... | collective-permute-start | bytes 589832 | tf_op jit(solution)/shard_map/ppermute | solution.py:410
  36.9 8.1 %collective-permute-start.2 = (f32[32,16,128]{2,1,0:T(8,128)S(1)}, f32[32,16,128]{2,1,0:T(8,128)S(1)}, u32[]{:S(2)}, u32[]{:S(2)}) collective-permute-start(f32[32,16,128]{2,1,0:T(8,128)S(1)} %bitcast.26), channel_id=1, source_target_pairs={{0,64},{16,17},{32,96},{144,145},{64,0},{17,16},{96,32},{145,144},... | collective-permute-start | bytes 786440 | tf_op jit(solution)/shard_map/ppermute | solution.py:375
  38.1 9.6 %collective-permute-start.3 = (f32[32,16,128]{2,1,0:T(8,128)S(1)}, f32[32,16,128]{2,1,0:T(8,128)S(1)}, u32[]{:S(2)}, u32[]{:S(2)}) collective-permute-start(f32[32,16,128]{2,1,0:T(8,128)S(1)} %bitcast.25), channel_id=1, source_target_pairs={{0,32},{16,144},{32,64},{144,17},{64,96},{17,145},{96,0},{145,16},... | collective-permute-start | bytes 786440 | tf_op jit(solution)/shard_map/ppermute | solution.py:375
  38.8 8.9 %collective-permute-start.4 = (f32[32,16,128]{2,1,0:T(8,128)S(1)}, f32[32,16,128]{2,1,0:T(8,128)S(1)}, u32[]{:S(2)}, u32[]{:S(2)}) collective-permute-start(f32[32,16,128]{2,1,0:T(8,128)S(1)} %bitcast.24), channel_id=1, source_target_pairs={{0,96},{16,145},{32,0},{144,16},{64,32},{17,144},{96,64},{145,17},... | collective-permute-start | bytes 786440 | tf_op jit(solution)/shard_map/ppermute | solution.py:375
  42.8 8.1 %collective-permute-start.6 = (f32[32,16,128]{2,1,0:T(8,128)S(1)}, f32[32,16,128]{2,1,0:T(8,128)S(1)}, u32[]{:S(2)}, u32[]{:S(2)}) collective-permute-start(f32[32,16,128]{2,1,0:T(8,128)S(1)} %bitcast.29), channel_id=1, source_target_pairs={{0,64},{16,17},{32,96},{144,145},{64,0},{17,16},{96,32},{145,144},... | collective-permute-start | bytes 786440 | tf_op jit(solution)/shard_map/ppermute | solution.py:375
  44.1 9.5 %collective-permute-start.7 = (f32[32,16,128]{2,1,0:T(8,128)S(1)}, f32[32,16,128]{2,1,0:T(8,128)S(1)}, u32[]{:S(2)}, u32[]{:S(2)}) collective-permute-start(f32[32,16,128]{2,1,0:T(8,128)S(1)} %bitcast.28), channel_id=1, source_target_pairs={{0,32},{16,144},{32,64},{144,17},{64,96},{17,145},{96,0},{145,16},... | collective-permute-start | bytes 786440 | tf_op jit(solution)/shard_map/ppermute | solution.py:375
  45.0 8.6 %collective-permute-start.8 = (f32[32,16,128]{2,1,0:T(8,128)S(1)}, f32[32,16,128]{2,1,0:T(8,128)S(1)}, u32[]{:S(2)}, u32[]{:S(2)}) collective-permute-start(f32[32,16,128]{2,1,0:T(8,128)S(1)} %bitcast.27), channel_id=1, source_target_pairs={{0,96},{16,145},{32,0},{144,16},{64,32},{17,144},{96,64},{145,17},... | collective-permute-start | bytes 786440 | tf_op jit(solution)/shard_map/ppermute | solution.py:375
  47.7 0.7 copy-start
  74.2 11.2 %collective-permute-start.9 = (f32[2,16,128]{2,1,0:T(8,128)S(1)}, f32[2,16,128]{2,1,0:T(8,128)S(1)}, u32[]{:S(2)}, u32[]{:S(2)}) collective-permute-start(f32[2,16,128]{2,1,0:T(8,128)S(1)} %reduce_sum.9.own_ref), channel_id=1, source_target_pairs={{0,0},{1,16},{2,32},{3,48},{4,64},{5,80},{6,96},{7,112},{8,128},{9... | collective-permute-start | bytes 49160 | tf_op jit(solution)/shard_map/ppermute | solution.py:448

commit v8 on v7

--- a/solution.py
+++ b/solution.py
@@ -314,17 +314,42 @@
     lax.fori_loop(0, 4, one, 0, unroll=4)
 
 
-def place_kernel(own_ref, mirror_ref, out_ref):
+def forward_kernel(own_ref, out_hbm, held_ref, sent):
+    for pair in range(2):
+        for index in range(8):
+            held_ref[pair * 2 + index // 4, (index // 2) % 2, index % 2] = own_ref[
+                pair, :, index * 16 : index * 16 + 16
+            ]
+    copy = pltpu.make_async_copy(held_ref, out_hbm.at[0], sent.at[0])
+    copy.start()
+    copy.wait()
+
+
+def mirror_kernel(mirror_ref, _, out_hbm, held_ref, sent):
     padding = jnp.zeros((LANES - 32, LANES), jnp.float32)
     turned = jnp.concatenate([mirror_ref[0], mirror_ref[1], padding]).T
     for pair in range(2):
         for index in range(8):
-            q = pair * 2 + index // 4
-            g = (index // 2) % 2
-            part = index % 2
-            out_ref[0, q, g, part] = own_ref[pair, :, index * 16 : index * 16 + 16]
             value = turned[index * 16 : index * 16 + 16, pair * 16 : pair * 16 + 16]
-            out_ref[1, q, g, part] = -value if part else value
+            held_ref[pair * 2 + index // 4, (index // 2) % 2, index % 2] = (
+                -value if index % 2 else value
+            )
+    copy = pltpu.make_async_copy(held_ref, out_hbm.at[1], sent.at[0])
+    copy.start()
+    copy.wait()
+
+
+def place(kernel, inputs, aliases):
+    hbm = pl.BlockSpec(memory_space=pltpu.HBM)
+    return pl.pallas_call(
+        kernel,
+        out_shape=jax.ShapeDtypeStruct((2, NZD, 2, 2, 16, 16), F32),
+        in_specs=[VMEM, hbm][: len(inputs)],
+        out_specs=hbm,
+        scratch_shapes=[pltpu.VMEM((NZD, 2, 2, 16, 16), F32), pltpu.SemaphoreType.DMA((1,))],
+        input_output_aliases=aliases,
+        compiler_params=pltpu.CompilerParams(vmem_limit_bytes=32 * 1024 * 1024),
+    )(*inputs)
 
 
 SMEM = pl.BlockSpec(memory_space=pltpu.SMEM)
@@ -448,8 +473,8 @@
     mirror = lax.ppermute(
         block, EIG + SPACE, [(e * 16 + s, s * 16 + e) for e in range(16) for s in range(16)]
     )
-    (fields,) = call(place_kernel, [((2, NZD, 2, 2, 16, 16), F32)], (block, mirror))
-    return fields
+    forward = place(forward_kernel, (block,), {})
+    return place(mirror_kernel, (mirror, forward), {1: 0})
 
 
 def solution(mesh):

time: 87.6 us -> 87.5 us (level)
    pallas_call x0 -> x2, Pallas kernels: none -> 1.59 us  [place(): pl.pallas_call(kernel, out_shape=jax.ShapeDtypeStruct((2, NZD, 2, 2, 16,...]
    pallas_call x7 -> x6, Pallas kernels: 10.7 us -> 9.78 us  [call(): pl.pallas_call(kernel, out_shape=shapes, in_specs=specs, out_specs=[space...]
  transfers between devices with their start and end apart: 10 -> 10, of which waited for: 6 -> 6; matrix products, arithmetic and copies ran while one was open for 0% -> 0% of each run, Pallas kernels for 7% -> 8%
where the time goes in v8:
time: 87.5 us; the launch traced here: 86.2 us
  blocking collectives  40.3 us (46%)
  starting transfers between devices  20.7 us (24%)
  waiting for transfers between devices  12.9 us (15%)
  Pallas kernels  11.4 us (13%)
    all_to_all x1, blocking collectives, exchange(): lax.all_to_all(value, EIG + SPACE, split_axis=0, concat_axis=0, tiled=Tru...  20.4 us
    all_to_all x1, blocking collectives, local(): own = lax.all_to_all(chunks, PLANE, split_axis=0, concat_axis=0, tiled=True)  19.9 us
    pallas_call x6, Pallas kernels, call(): pl.pallas_call(kernel, out_shape=shapes, in_specs=specs, out_specs=[space...  9.78 us
    ppermute x6, starting transfers between devices, first_shift(): return lax.ppermute(value, EIG + SPACE, pairs)  8.63 us
    ppermute x2, starting transfers between devices, from_above(): return lax.ppermute(value, 'z', [(i, (i - 1) % 8) for i in range(8)])  7.02 us
    ppermute x1, waiting for transfers between devices, local(): lax.ppermute(block, EIG + SPACE, [(e * 16 + s, s * 16 + e) for e in range...  5.37 us
    ppermute x6, waiting for transfers between devices, first_shift(): return lax.ppermute(value, EIG + SPACE, pairs)  5.33 us
    ppermute x1, starting transfers between devices, local(): lax.ppermute(block, EIG + SPACE, [(e * 16 + s, s * 16 + e) for e in range...  5.05 us
  transfers between devices with their start and end apart: 10, of which 6 were waited for; matrix products, arithmetic and copies ran while one was open for 0% of the time, Pallas kernels for 8%

profile of v8, /device:TPU:24, one launch (start us, length us, event | category | flops | bytes accessed | tf_op | source)
XLA Modules:
  0.0 86.2 jit_solution(16020611972879967068)
XLA Ops:
  0.0 3.4 %shard_map.37 = f32[16,104,128]{2,1,0:T(8,128)} custom-call(f32[1536,128]{1,0:T(8,128)} %bitcast.23, f32[72,128]{1,0:T(8,128)} %bitcast.30), custom_call_target="tpu_custom_call" | custom-call | bytes 823296 | tf_op jit(solution)/shard_map/pallas_call | solution.py:363
  3.4 19.9 %all_to_all.10 = f32[16,104,128]{2,1,0:T(8,128)S(1)} all-to-all(f32[16,104,128]{2,1,0:T(8,128)} %shard_map.37), channel_id=1, replica_groups=mesh['ylo'=2,'x'=4,'core'=2,'z'=8,'yhi'=2] {'yhi','ylo','x'}, dimensions={0} | all-to-all | bytes 1703936 | tf_op jit(solution)/shard_map/all_to_all | solution.py:431
  23.4 0.0 collective-permute-start.1
  23.4 5.9 %collective-permute-start = (f32[8,56,128]{2,1,0:T(8,128)S(1)}, f32[8,56,128]{2,1,0:T(8,128)S(1)}, u32[]{:S(2)}, u32[]{:S(2)}) collective-permute-start(f32[8,56,128]{2,1,0:T(8,128)S(1)} %slice_bitcast_fusion), channel_id=1, source_target_pairs={{0,14},{2,0},{4,2},{6,4},{8,6},{10,8},{12,10},{14,12},{1,15},{3,1}... | collective-permute-start | bytes 688136 | tf_op jit(solution)/shard_map/ppermute | solution.py:435
  29.3 1.1 %collective-permute-start.5 = (f32[8,48,128]{2,1,0:T(8,128)S(1)}, f32[8,48,128]{2,1,0:T(8,128)S(1)}, u32[]{:S(2)}, u32[]{:S(2)}) collective-permute-start(f32[8,48,128]{2,1,0:T(8,128)S(1)} %slice_bitcast_fusion.1), channel_id=1, source_target_pairs={{0,14},{2,0},{4,2},{6,4},{8,6},{10,8},{12,10},{14,12},{1,15},{3,1}... | collective-permute-start | bytes 589832 | tf_op jit(solution)/shard_map/ppermute | solution.py:435
  30.4 0.0 collective-permute-done.1.other_ref
  30.4 2.6 %shard_map.38 = (f32[2,512,256]{2,1,0:T(8,128)S(1)}, f32[2,512,256]{2,1,0:T(8,128)S(1)}, bf16[2,256,384]{2,1,0:T(8,128)(2,1)S(1)}, bf16[2,256,384]{2,1,0:T(8,128...) custom-call(f32[2,8,104,128]{3,2,1,0:T(8,128)S(1)} %bitcast.18, ...), custom_call_target="tpu_custom_call" | custom-call | flops 1207959552 | bytes 1703936 | tf_op jit(solution)/shard_map/pallas_call | solution.py:363
  33.0 2.2 %collective-permute-done.above_ref = f32[8,56,128]{2,1,0:T(8,128)S(1)} collective-permute-done((f32[8,56,128]{2,1,0:T(8,128)S(1)}, f32[8,56,128]{2,1,0:T(8,128)S(1)}, u32[]{:S(2)}, u32[]{:S(2)}) %collective-permute-start) | collective-permute-done | bytes 229408 | tf_op jit(solution)/shard_map/ppermute | solution.py:435
  35.2 1.6 %shard_map.39 = (f32[16,8,16,128]{3,2,1,0:T(8,128)S(1)}, f32[72,128]{1,0:T(8,128)S(1)}) custom-call(f32[2,8,104,128]{3,2,1,0:T(8,128)S(1)} %bitcast.19, f32[8,56,128]{2,1,0:T(8,128)S(1)} %collective-permute-done.above_ref, f32[2,512,256]{2,1,0:T(8,128)S(1)} %get-tuple-element.15.refs_0_, bf16[2,256,384]{2,1,0:T(8,128)(2,1)S(1)} %get-tuple-element.16.refs_1_.refs_2_, ...), custom_call_target="tpu_custom_call" | custom-call | flops 603979776 | bytes 5275648 | tf_op jit(solution)/shard_map/pallas_call | solution.py:363
  36.8 0.1 fusion.1
  36.9 1.2 %collective-permute-start.2 = (f32[32,16,128]{2,1,0:T(8,128)S(1)}, f32[32,16,128]{2,1,0:T(8,128)S(1)}, u32[]{:S(2)}, u32[]{:S(2)}) collective-permute-start(f32[32,16,128]{2,1,0:T(8,128)S(1)} %bitcast.26), channel_id=1, source_target_pairs={{0,64},{16,17},{32,96},{144,145},{64,0},{17,16},{96,32},{145,144},... | collective-permute-start | bytes 786440 | tf_op jit(solution)/shard_map/ppermute | solution.py:400
  38.1 0.6 collective-permute-start.3
  38.8 2.6 %collective-permute-start.4 = (f32[32,16,128]{2,1,0:T(8,128)S(1)}, f32[32,16,128]{2,1,0:T(8,128)S(1)}, u32[]{:S(2)}, u32[]{:S(2)}) collective-permute-start(f32[32,16,128]{2,1,0:T(8,128)S(1)} %bitcast.24), channel_id=1, source_target_pairs={{0,96},{16,145},{32,0},{144,16},{64,32},{17,144},{96,64},{145,17},... | collective-permute-start | bytes 786440 | tf_op jit(solution)/shard_map/ppermute | solution.py:400
  41.4 0.0 collective-permute-done.5.above_ref
  41.4 1.3 %shard_map.41 = f32[16,8,16,128]{3,2,1,0:T(8,128)S(1)} custom-call(f32[2,8,104,128]{3,2,1,0:T(8,128)S(1)} %bitcast.20, f32[8,48,128]{2,1,0:T(8,128)S(1)} %collective-permute-done.5.above_ref, f32[72,128]{1,0:T(8,128)S(1)} %get-tuple-element.23.refs_0_, f32[2,512,256]{2,1,0:T(8,128)S(1)} %get-tuple-element.24.refs_1_, ...), custom_call_target="tpu_custom_call" | custom-call | flops 603979776 | bytes 5279744 | tf_op jit(solution)/shard_map/pallas_call | solution.py:363
  42.7 0.1 fusion
  42.8 1.3 %collective-permute-start.6 = (f32[32,16,128]{2,1,0:T(8,128)S(1)}, f32[32,16,128]{2,1,0:T(8,128)S(1)}, u32[]{:S(2)}, u32[]{:S(2)}) collective-permute-start(f32[32,16,128]{2,1,0:T(8,128)S(1)} %bitcast.29), channel_id=1, source_target_pairs={{0,64},{16,17},{32,96},{144,145},{64,0},{17,16},{96,32},{145,144},... | collective-permute-start | bytes 786440 | tf_op jit(solution)/shard_map/ppermute | solution.py:400
  44.1 0.6 collective-permute-start.7
  44.6 0.3 collective-permute-done.2.refs_1_
  45.0 2.3 %collective-permute-start.8 = (f32[32,16,128]{2,1,0:T(8,128)S(1)}, f32[32,16,128]{2,1,0:T(8,128)S(1)}, u32[]{:S(2)}, u32[]{:S(2)}) collective-permute-start(f32[32,16,128]{2,1,0:T(8,128)S(1)} %bitcast.27), channel_id=1, source_target_pairs={{0,96},{16,145},{32,0},{144,16},{64,32},{17,144},{96,64},{145,17},... | collective-permute-start | bytes 786440 | tf_op jit(solution)/shard_map/ppermute | solution.py:400
  47.3 0.4 collective-permute-done.3.refs_2_
  47.7 0.0 collective-permute-done.4.refs_3_
  47.7 0.0 copy-start
  47.7 0.7 copy-done
  48.3 0.6 shard_map.40
  48.9 1.9 %collective-permute-done.6.refs_2_ = f32[32,16,128]{2,1,0:T(8,128)S(1)} collective-permute-done((f32[32,16,128]{2,1,0:T(8,128)S(1)}, f32[32,16,128]{2,1,0:T(8,128)S(1)}, u32[]{:S(2)}, u32[]{:S(2)}) %collective-permute-start.6) | collective-permute-done | bytes 262176 | tf_op jit(solution)/shard_map/ppermute | solution.py:400
  50.9 2.7 %collective-permute-done.7.refs_3_ = f32[32,16,128]{2,1,0:T(8,128)S(1)} collective-permute-done((f32[32,16,128]{2,1,0:T(8,128)S(1)}, f32[32,16,128]{2,1,0:T(8,128)S(1)}, u32[]{:S(2)}, u32[]{:S(2)}) %collective-permute-start.7) | collective-permute-done | bytes 262176 | tf_op jit(solution)/shard_map/ppermute | solution.py:400
  53.6 0.0 collective-permute-done.8.refs_4_
  53.6 0.2 shard_map.42
  53.8 20.4 %all_to_all.11 = f32[32,2,16,128]{3,2,1,0:T(8,128)S(1)} all-to-all(f32[32,2,16,128]{3,2,1,0:T(8,128)S(1)} %shard_map.42), channel_id=1, replica_groups={{0,2,4,6,8,10,12,14,128,130,132,134,136,138,140,142,1,3,5,7,9,11,13,15,..., dimensions={0} | all-to-all | bytes 1048576 | tf_op jit(solution)/shard_map/all_to_all | solution.py:409
  74.2 5.0 %collective-permute-start.9 = (f32[2,16,128]{2,1,0:T(8,128)S(1)}, f32[2,16,128]{2,1,0:T(8,128)S(1)}, u32[]{:S(2)}, u32[]{:S(2)}) collective-permute-start(f32[2,16,128]{2,1,0:T(8,128)S(1)} %reduce_sum.9.own_ref), channel_id=1, source_target_pairs={{0,0},{1,16},{2,32},{3,48},{4,64},{5,80},{6,96},{7,112},{8,128},{9... | collective-permute-start | bytes 49160 | tf_op jit(solution)/shard_map/ppermute | solution.py:473
  79.3 0.8 shard_map.43._
  80.0 5.4 %collective-permute-done.9.mirror_ref = f32[2,16,128]{2,1,0:T(8,128)S(1)} collective-permute-done((f32[2,16,128]{2,1,0:T(8,128)S(1)}, f32[2,16,128]{2,1,0:T(8,128)S(1)}, u32[]{:S(2)}, u32[]{:S(2)}) %collective-permute-start.9) | collective-permute-done | bytes 16416 | tf_op jit(solution)/shard_map/ppermute | solution.py:473
  85.4 0.8 shard_map.44
  (3 shorter events, 0.1 us)
Async XLA Ops:
  23.4 7.1 %collective-permute-start.1 = (f32[2,8,104,128]{3,2,1,0:T(8,128)S(1)}, f32[2,8,104,128]{3,2,1,0:T(8,128)S(1)}, u32[]{:S(2)}, u32[]{:S(2)}) collective-permute-start(f32[2,8,104,128]{3,2,1,0:T(8,128)S(1)} %bitcast.15), channel_id=1, source_target_pairs={{0,16},{16,0},{1,17},{17,1},{2,18},{18,2},{3,19},{19,3},{4,20},{20... | collective-permute-start | bytes 2555912 | tf_op jit(solution)/shard_map/ppermute | solution.py:438
  23.4 11.9 %collective-permute-start = (f32[8,56,128]{2,1,0:T(8,128)S(1)}, f32[8,56,128]{2,1,0:T(8,128)S(1)}, u32[]{:S(2)}, u32[]{:S(2)}) collective-permute-start(f32[8,56,128]{2,1,0:T(8,128)S(1)} %slice_bitcast_fusion), channel_id=1, source_target_pairs={{0,14},{2,0},{4,2},{6,4},{8,6},{10,8},{12,10},{14,12},{1,15},{3,1}... | collective-permute-start | bytes 688136 | tf_op jit(solution)/shard_map/ppermute | solution.py:435
  29.3 12.0 %collective-permute-start.5 = (f32[8,48,128]{2,1,0:T(8,128)S(1)}, f32[8,48,128]{2,1,0:T(8,128)S(1)}, u32[]{:S(2)}, u32[]{:S(2)}) collective-permute-start(f32[8,48,128]{2,1,0:T(8,128)S(1)} %slice_bitcast_fusion.1), channel_id=1, source_target_pairs={{0,14},{2,0},{4,2},{6,4},{8,6},{10,8},{12,10},{14,12},{1,15},{3,1}... | collective-permute-start | bytes 589832 | tf_op jit(solution)/shard_map/ppermute | solution.py:435
  36.9 8.1 %collective-permute-start.2 = (f32[32,16,128]{2,1,0:T(8,128)S(1)}, f32[32,16,128]{2,1,0:T(8,128)S(1)}, u32[]{:S(2)}, u32[]{:S(2)}) collective-permute-start(f32[32,16,128]{2,1,0:T(8,128)S(1)} %bitcast.26), channel_id=1, source_target_pairs={{0,64},{16,17},{32,96},{144,145},{64,0},{17,16},{96,32},{145,144},... | collective-permute-start | bytes 786440 | tf_op jit(solution)/shard_map/ppermute | solution.py:400
  38.1 9.6 %collective-permute-start.3 = (f32[32,16,128]{2,1,0:T(8,128)S(1)}, f32[32,16,128]{2,1,0:T(8,128)S(1)}, u32[]{:S(2)}, u32[]{:S(2)}) collective-permute-start(f32[32,16,128]{2,1,0:T(8,128)S(1)} %bitcast.25), channel_id=1, source_target_pairs={{0,32},{16,144},{32,64},{144,17},{64,96},{17,145},{96,0},{145,16},... | collective-permute-start | bytes 786440 | tf_op jit(solution)/shard_map/ppermute | solution.py:400
  38.8 8.9 %collective-permute-start.4 = (f32[32,16,128]{2,1,0:T(8,128)S(1)}, f32[32,16,128]{2,1,0:T(8,128)S(1)}, u32[]{:S(2)}, u32[]{:S(2)}) collective-permute-start(f32[32,16,128]{2,1,0:T(8,128)S(1)} %bitcast.24), channel_id=1, source_target_pairs={{0,96},{16,145},{32,0},{144,16},{64,32},{17,144},{96,64},{145,17},... | collective-permute-start | bytes 786440 | tf_op jit(solution)/shard_map/ppermute | solution.py:400
  42.8 8.1 %collective-permute-start.6 = (f32[32,16,128]{2,1,0:T(8,128)S(1)}, f32[32,16,128]{2,1,0:T(8,128)S(1)}, u32[]{:S(2)}, u32[]{:S(2)}) collective-permute-start(f32[32,16,128]{2,1,0:T(8,128)S(1)} %bitcast.29), channel_id=1, source_target_pairs={{0,64},{16,17},{32,96},{144,145},{64,0},{17,16},{96,32},{145,144},... | collective-permute-start | bytes 786440 | tf_op jit(solution)/shard_map/ppermute | solution.py:400
  44.1 9.5 %collective-permute-start.7 = (f32[32,16,128]{2,1,0:T(8,128)S(1)}, f32[32,16,128]{2,1,0:T(8,128)S(1)}, u32[]{:S(2)}, u32[]{:S(2)}) collective-permute-start(f32[32,16,128]{2,1,0:T(8,128)S(1)} %bitcast.28), channel_id=1, source_target_pairs={{0,32},{16,144},{32,64},{144,17},{64,96},{17,145},{96,0},{145,16},... | collective-permute-start | bytes 786440 | tf_op jit(solution)/shard_map/ppermute | solution.py:400
  45.0 8.6 %collective-permute-start.8 = (f32[32,16,128]{2,1,0:T(8,128)S(1)}, f32[32,16,128]{2,1,0:T(8,128)S(1)}, u32[]{:S(2)}, u32[]{:S(2)}) collective-permute-start(f32[32,16,128]{2,1,0:T(8,128)S(1)} %bitcast.27), channel_id=1, source_target_pairs={{0,96},{16,145},{32,0},{144,16},{64,32},{17,144},{96,64},{145,17},... | collective-permute-start | bytes 786440 | tf_op jit(solution)/shard_map/ppermute | solution.py:400
  47.7 0.7 copy-start
  74.2 11.2 %collective-permute-start.9 = (f32[2,16,128]{2,1,0:T(8,128)S(1)}, f32[2,16,128]{2,1,0:T(8,128)S(1)}, u32[]{:S(2)}, u32[]{:S(2)}) collective-permute-start(f32[2,16,128]{2,1,0:T(8,128)S(1)} %reduce_sum.9.own_ref), channel_id=1, source_target_pairs={{0,0},{1,16},{2,32},{3,48},{4,64},{5,80},{6,96},{7,112},{8,128},{9... | collective-permute-start | bytes 49160 | tf_op jit(solution)/shard_map/ppermute | solution.py:473
